TPU v7x, 32 devices: a whole 2x2x4 slice. The times are simulated.
32 devices in a mesh: head: 4 (over y, core), seq: 8 (over z, x).
Axes of the slice: x: 2, y: 2, z: 4, core: 2. Of those that a mesh axis runs over, the one named last changes fastest.
Arguments:
- query_rows: bfloat16 [1024, 768], P(('seq', 'head')), may hold values from -6 to 6
- key_rows: bfloat16 [1024, 768], P(('seq', 'head')), may hold values from -6 to 6
- value_rows: bfloat16 [1024, 768], P(('seq', 'head')), may hold values from -6 to 6
- gate_rows: bfloat16 [1024, 768], P(('seq', 'head')), may hold values from -1 to 1
- step_rates: float32 [1024, 12], P('seq', 'head'), may hold values from 5e-05 to 0.0005
- first_weight: float32 [12, 64, 256], P('head'), may hold values from -0.75 to 0.75
- first_bias: float32 [12, 256], P('head'), may hold values from -3 to 3
- second_weight: float32 [12, 256, 64], P('head'), may hold values from -0.375 to 0.375
- second_bias: float32 [12, 64], P('head'), may hold values from -3 to 3
- norm_gain: float32 [12, 64], P('head'), may hold values from 0.5 to 1.5
- norm_shift: float32 [12, 64], P('head'), may hold values from -3 to 3
Outputs:
- layer_output: bfloat16 [1024, 768], P(('seq', 'head'))
All inputs are finite; a program needn't handle non-finite values.
Results may differ from a plain program's by a relative error of at most 0.0049.
Values may be sent and summed in bfloat16 or wider, within the bound.
No kernel may reach another device: no remote copies, remote signals or barrier semaphores. Data moves between devices by JAX's collectives and lax.ppermute only.
A program may use at most 64 MiB of HBM per device.

v0:
```python
import jax
import jax.numpy as jnp
from jax import lax
from jax.sharding import PartitionSpec as P

D_HEAD = 64
INNER = 256
MINI = 64


highest = lax.Precision.HIGHEST
eps_norm = 1e-06
root_factor = 0.7978845608028654
cube_factor = 0.044715


def shifted(block, axis, distance):
    devices = range(lax.axis_size(axis))
    route = [(i - distance, i) for i in devices if i - distance in devices]
    return lax.ppermute(block, axis, route)


def gelu_tanh(values):
    tanh_term = jnp.tanh(root_factor * (values + cube_factor * values * values * values))
    return 0.5 * values * (1.0 + tanh_term)


def gelu_slope(values):
    tanh_term = jnp.tanh(root_factor * (values + cube_factor * values * values * values))
    return 0.5 * (1.0 + tanh_term) + 0.5 * values * (1.0 - tanh_term * tanh_term) * root_factor * (
        1.0 + 3.0 * cube_factor * values * values
    )


def layer_norm(values, gain_row, shift_row):
    centred = values - jnp.mean(values, axis=-1, keepdims=True)
    spread = jnp.sqrt(jnp.mean(centred * centred, axis=-1, keepdims=True) + eps_norm)
    normed = centred / spread
    return (normed, spread, gain_row * normed + shift_row)


def unpack(fast_state):
    weight_one = fast_state[:D_HEAD]
    second_turned = fast_state[D_HEAD : 2 * D_HEAD]
    bias_one = fast_state[2 * D_HEAD]
    bias_two = fast_state[2 * D_HEAD + 1, :D_HEAD]
    return (weight_one, bias_one, second_turned, bias_two)


def gradients(fast_state, key_block, value_block, gain_row, shift_row):
    weight_one, bias_one, second_turned, bias_two = unpack(fast_state)
    pre_one = jnp.dot(key_block, weight_one, precision=highest) + bias_one
    act_one = gelu_tanh(pre_one)
    pre_two = jnp.einsum("ti,di->td", act_one, second_turned, precision=highest) + bias_two
    normed, spread, fitted = layer_norm(pre_two, gain_row, shift_row)
    scaled = gain_row * (fitted - (value_block - key_block))
    grad_two = (
        scaled
        - jnp.mean(scaled, axis=-1, keepdims=True)
        - normed * jnp.mean(scaled * normed, axis=-1, keepdims=True)
    ) / spread
    grad_one = jnp.dot(grad_two, second_turned, precision=highest) * gelu_slope(pre_one)
    return (act_one, grad_one, grad_two)


def renew(fast_state, key_block, act_one, grad_one, grad_two, rate_row):
    weight_one, bias_one, second_turned, bias_two = unpack(fast_state)
    weighted_one = rate_row[:, None] * grad_one
    weighted_two = rate_row[:, None] * grad_two
    new_first = weight_one - jnp.einsum("td,ti->di", key_block, weighted_one, precision=highest)
    new_second = second_turned - jnp.einsum("td,ti->di", weighted_two, act_one, precision=highest)
    new_bias_one = bias_one - jnp.sum(weighted_one, axis=0)
    new_bias_two = bias_two - jnp.sum(weighted_two, axis=0)
    filler = jnp.zeros((fast_state.shape[1] - D_HEAD,), jnp.float32)
    return jnp.concatenate(
        [
            new_first,
            new_second,
            new_bias_one[None, :],
            jnp.concatenate([new_bias_two, filler])[None, :],
        ],
        axis=0,
    )


def dual_output(
    fast_state, query_block, key_block, act_one, grad_one, grad_two, rate_row, gain_row, shift_row
):
    weight_one, bias_one, second_turned, bias_two = unpack(fast_state)
    lower_mask = jnp.arange(MINI)[:, None] >= jnp.arange(MINI)[None, :]
    step_matrix = jnp.where(lower_mask, rate_row[None, :], 0.0)
    attend_one = (
        jnp.einsum("sd,td->st", query_block, key_block, precision=highest) + 1.0
    ) * step_matrix
    dual_one = (
        jnp.dot(query_block, weight_one, precision=highest)
        + bias_one
        - jnp.dot(attend_one, grad_one, precision=highest)
    )
    dual_act = gelu_tanh(dual_one)
    attend_two = (jnp.einsum("si,ti->st", dual_act, act_one, precision=highest) + 1.0) * step_matrix
    dual_two = (
        jnp.einsum("si,di->sd", dual_act, second_turned, precision=highest)
        + bias_two
        - jnp.dot(attend_two, grad_two, precision=highest)
    )
    return layer_norm(dual_two, gain_row, shift_row)[2]


def orient(array_in, reverse):
    if reverse:
        return jnp.flip(array_in, 0)
    return array_in


def to_blocks(array_in):
    block_count = array_in.shape[0] // MINI
    return array_in.reshape((block_count, MINI) + array_in.shape[1:])


def segment(fast_state, query_head, key_head, value_head, rate_head, gain_row, shift_row):

    def advance(carried, block_data):
        query_block = block_data[0].astype(jnp.float32)
        key_block = block_data[1].astype(jnp.float32)
        value_block = block_data[2].astype(jnp.float32)
        rate_row = block_data[3]
        act_one, grad_one, grad_two = gradients(
            carried, key_block, value_block, gain_row, shift_row
        )
        updated = renew(carried, key_block, act_one, grad_one, grad_two, rate_row)
        emitted = dual_output(
            carried,
            query_block,
            key_block,
            act_one,
            grad_one,
            grad_two,
            rate_row,
            gain_row,
            shift_row,
        )
        return (updated, emitted)

    return lax.scan(
        advance,
        fast_state,
        (to_blocks(query_head), to_blocks(key_head), to_blocks(value_head), to_blocks(rate_head)),
    )


def local(
    query_rows,
    key_rows,
    value_rows,
    gate_rows,
    step_rates,
    first_weight,
    first_bias,
    second_weight,
    second_bias,
    norm_gain,
    norm_shift,
):
    query_local, key_local, value_local, gate_local = (
        lax.all_to_all(query_rows, "head", split_axis=1, concat_axis=0, tiled=True),
        lax.all_to_all(key_rows, "head", split_axis=1, concat_axis=0, tiled=True),
        lax.all_to_all(value_rows, "head", split_axis=1, concat_axis=0, tiled=True),
        lax.all_to_all(gate_rows, "head", split_axis=1, concat_axis=0, tiled=True),
    )
    token_count = query_local.shape[0]
    heads_local = step_rates.shape[1]
    query_heads = query_local.reshape(token_count, heads_local, D_HEAD)
    key_heads = key_local.reshape(token_count, heads_local, D_HEAD)
    value_heads = value_local.reshape(token_count, heads_local, D_HEAD)
    filler = jnp.zeros((heads_local, 1, INNER - D_HEAD), jnp.float32)
    initial = jnp.concatenate(
        [
            first_weight,
            jnp.swapaxes(second_weight, 1, 2),
            first_bias[:, None, :],
            jnp.concatenate([second_bias[:, None, :], filler], axis=2),
        ],
        axis=1,
    )
    state_rows = 2 * D_HEAD + 2
    position = lax.axis_index("seq")
    chain_size = lax.axis_size("seq")
    store_shape = (token_count, heads_local, D_HEAD)
    blank_store = jnp.zeros(store_shape, jnp.float32)

    def direction_turn(section_turn, received, stored, first_device, chain_place, reverse):
        head_now = section_turn - chain_place
        active = jnp.logical_and(head_now >= 0, head_now < heads_local)
        chosen = jnp.clip(head_now, 0, heads_local - 1)
        starting = jnp.where(
            first_device, lax.dynamic_index_in_dim(initial, chosen, 0, keepdims=False), received
        )

        def work(operands):
            start_state, kept = operands
            query_head = orient(
                lax.dynamic_index_in_dim(query_heads, chosen, 1, keepdims=False), reverse
            )
            key_head = orient(
                lax.dynamic_index_in_dim(key_heads, chosen, 1, keepdims=False), reverse
            )
            value_head = orient(
                lax.dynamic_index_in_dim(value_heads, chosen, 1, keepdims=False), reverse
            )
            rate_head = orient(
                lax.dynamic_index_in_dim(step_rates, chosen, 1, keepdims=False), reverse
            )
            gain_row = lax.dynamic_index_in_dim(norm_gain, chosen, 0, keepdims=False)
            shift_row = lax.dynamic_index_in_dim(norm_shift, chosen, 0, keepdims=False)
            finished, emitted = segment(
                start_state, query_head, key_head, value_head, rate_head, gain_row, shift_row
            )
            rows_out = orient(emitted.reshape(token_count, D_HEAD), reverse)
            kept = lax.dynamic_update_slice(kept, rows_out[:, None, :], (0, chosen, 0))
            return (finished, kept)

        def skip(operands):
            return (jnp.zeros_like(operands[0]), operands[1])

        return lax.cond(active, work, skip, (starting, stored))

    def turn_body(section_turn, loop_state):
        received_ahead, received_back, store_ahead, store_back = loop_state
        sent_ahead, store_ahead = direction_turn(
            section_turn, received_ahead, store_ahead, position == 0, position, False
        )
        sent_back, store_back = direction_turn(
            section_turn,
            received_back,
            store_back,
            position == chain_size - 1,
            chain_size - 1 - position,
            True,
        )
        received_ahead = shifted(sent_ahead, "seq", 1)
        received_back = shifted(sent_back, "seq", -1)
        return (received_ahead, received_back, store_ahead, store_back)

    empty_state = jnp.zeros((state_rows, INNER), jnp.float32)
    loop_state = lax.fori_loop(
        0,
        chain_size + heads_local - 1,
        turn_body,
        (empty_state, empty_state, blank_store, blank_store),
    )
    store_ahead = loop_state[2]
    store_back = loop_state[3]
    combined = store_ahead + store_back
    summed = combined.reshape(token_count, heads_local * D_HEAD).astype(jnp.bfloat16)
    summed = lax.optimization_barrier(summed)
    gated = (gate_local.astype(jnp.float32) * summed.astype(jnp.float32)).astype(jnp.bfloat16)
    return lax.all_to_all(gated, "head", split_axis=0, concat_axis=1, tiled=True)


def solution(mesh):
    in_specs = (
        P(("seq", "head"), None),
        P(("seq", "head"), None),
        P(("seq", "head"), None),
        P(("seq", "head"), None),
        P("seq", "head"),
        P("head", None, None),
        P("head", None),
        P("head", None, None),
        P("head", None),
        P("head", None),
        P("head", None),
    )
    out_specs = P(("seq", "head"), None)
    return jax.shard_map(local, mesh=mesh, in_specs=in_specs, out_specs=out_specs, check_vma=False)
```

profile of v0, /device:TPU:26, one launch (start us, length us, event | category | flops | bytes accessed | tf_op | source)
XLA Modules:
  0.0 495.8 jit_solution(14926572574153682317)
XLA Ops:
  1.6 3.4 all-to-all-start.1
  5.7 3.3 all-to-all-done.1
  9.1 3.4 all-to-all-start.2
  13.3 3.3 all-to-all-done.2
  16.6 3.3 all-to-all-start.3
  21.8 2.2 all-to-all-done.3
  23.9 3.3 all-to-all-start
  28.3 457.0 %while.66 = (s32[]{:T(128)}, f32[130,256]{1,0:T(8,128)S(1)}, f32[130,256]{1,0:T(8,128)S(1)}, f32[128,3,64]{2,1,0:T(4,128)S(1)}, f32[128,3,64]{2,1,0:T(4,128)S(1)...) while((s32[]{:T(128)}, f32[130,256]{1,0:T(8,128)S(1)}, ...), condition=%wide.region_25.26_spmd, body=%wide.region_0.25_spmd.sunk | while | flops 236359936 | bytes 7138877 | solution.py:246
  28.3 27.4 %conditional.5 = (f32[130,256]{1,0:T(8,128)}, f32[128,3,64]{2,1,0:T(4,128)S(1)}) conditional(s32[]{:T(128)} %convert_element_type.79, f32[128,3,64]{2,1,0:T(4,128)S(1)} %get-tuple-element.1107, (pred[]{:T(512)}, s32[]{:T(128)}, f32[3,130,256]{2,1,0:T(8,128)S(1)}, f32[130,256]{1,0:T(8,128)S(1)}, bf16[128,3,64]{2,0,1:T(8,128)(2,1)S(1)}, ...), branch_computations={%region_13.13_spmd, %region_14.24_spmd} | conditional | flops 118179968 | bytes 3119138 | solution.py:226
  29.6 24.6 %while.65 = (s32[]{:T(128)}, f32[130,256]{1,0:T(8,128)}, f32[2,64,64]{2,1,0:T(8,128)S(1)}, bf16[2,64,64]{1,2,0:T(8,128)(2,1)S(1)}, f32[2,64]{1,0:T(2,128)S(1)}, ...) while((s32[]{:T(128)}, f32[130,256]{1,0:T(8,128)}, ...), condition=%wide.region_24.23_spmd, body=%wide.region_15.22_spmd.sunk | while | flops 118146688 | bytes 2256769 | solution.py:145
  54.2 1.5 dynamic_update_slice.16
  55.7 1.3 collective-permute-start.1
  59.0 2.2 collective-permute-done.1
  61.2 4.7 collective-permute-done
  65.8 27.4 %conditional.5 = (f32[130,256]{1,0:T(8,128)}, f32[128,3,64]{2,1,0:T(4,128)S(1)}) conditional(s32[]{:T(128)} %convert_element_type.79, f32[128,3,64]{2,1,0:T(4,128)S(1)} %get-tuple-element.1107, (pred[]{:T(512)}, s32[]{:T(128)}, f32[3,130,256]{2,1,0:T(8,128)S(1)}, f32[130,256]{1,0:T(8,128)S(1)}, bf16[128,3,64]{2,0,1:T(8,128)(2,1)S(1)}, ...), branch_computations={%region_13.13_spmd, %region_14.24_spmd} | conditional | flops 118179968 | bytes 3119138 | solution.py:226
  67.1 24.6 %while.65 = (s32[]{:T(128)}, f32[130,256]{1,0:T(8,128)}, f32[2,64,64]{2,1,0:T(8,128)S(1)}, bf16[2,64,64]{1,2,0:T(8,128)(2,1)S(1)}, f32[2,64]{1,0:T(2,128)S(1)}, ...) while((s32[]{:T(128)}, f32[130,256]{1,0:T(8,128)}, ...), condition=%wide.region_24.23_spmd, body=%wide.region_15.22_spmd.sunk | while | flops 118146688 | bytes 2256769 | solution.py:145
  91.7 1.5 dynamic_update_slice.16
  93.3 1.6 collective-permute-start.1
  97.9 4.7 collective-permute-done
  102.7 27.4 %conditional.5 = (f32[130,256]{1,0:T(8,128)}, f32[128,3,64]{2,1,0:T(4,128)S(1)}) conditional(s32[]{:T(128)} %convert_element_type.79, f32[128,3,64]{2,1,0:T(4,128)S(1)} %get-tuple-element.1107, (pred[]{:T(512)}, s32[]{:T(128)}, f32[3,130,256]{2,1,0:T(8,128)S(1)}, f32[130,256]{1,0:T(8,128)S(1)}, bf16[128,3,64]{2,0,1:T(8,128)(2,1)S(1)}, ...), branch_computations={%region_13.13_spmd, %region_14.24_spmd} | conditional | flops 118179968 | bytes 3119138 | solution.py:226
  104.0 24.6 %while.65 = (s32[]{:T(128)}, f32[130,256]{1,0:T(8,128)}, f32[2,64,64]{2,1,0:T(8,128)S(1)}, bf16[2,64,64]{1,2,0:T(8,128)(2,1)S(1)}, f32[2,64]{1,0:T(2,128)S(1)}, ...) while((s32[]{:T(128)}, f32[130,256]{1,0:T(8,128)}, ...), condition=%wide.region_24.23_spmd, body=%wide.region_15.22_spmd.sunk | while | flops 118146688 | bytes 2256769 | solution.py:145
  128.6 1.5 dynamic_update_slice.16
  130.1 3.0 collective-permute-start.1
  136.1 4.9 collective-permute-done
  141.6 29.6 %collective-permute-start.1 = (f32[130,256]{1,0:T(8,128)}, f32[130,256]{1,0:T(8,128)S(1)}, u32[]{:S(2)}, u32[]{:S(2)}) collective-permute-start(f32[130,256]{1,0:T(8,128)} %get-tuple-element.963), channel_id=1, source_target_pairs={{1,0},{2,1},{3,2},{4,3},{5,4},{6,5},{7,6},{9,8},{10,9},{11,10},{12... | collective-permute-start | bytes 399368 | tf_op jit(solution)/shard_map/while/body/eval_jaxpr/ppermute | solution.py:20
  174.1 4.9 collective-permute-done
  179.7 2.8 collective-permute-start.1
  185.4 30.7 %collective-permute-done = f32[130,256]{1,0:T(8,128)S(1)} collective-permute-done((f32[130,256]{1,0:T(8,128)}, f32[130,256]{1,0:T(8,128)S(1)}, u32[]{:S(2)}, u32[]{:S(2)}) %collective-permute-start) | collective-permute-done | bytes 133152 | tf_op jit(solution)/shard_map/while/body/eval_jaxpr/ppermute | solution.py:20
  216.8 4.5 collective-permute-start.1
  224.3 26.7 %collective-permute-done = f32[130,256]{1,0:T(8,128)S(1)} collective-permute-done((f32[130,256]{1,0:T(8,128)}, f32[130,256]{1,0:T(8,128)S(1)}, u32[]{:S(2)}, u32[]{:S(2)}) %collective-permute-start) | collective-permute-done | bytes 133152 | tf_op jit(solution)/shard_map/while/body/eval_jaxpr/ppermute | solution.py:20
  251.6 57.7 %collective-permute-start.1 = (f32[130,256]{1,0:T(8,128)}, f32[130,256]{1,0:T(8,128)S(1)}, u32[]{:S(2)}, u32[]{:S(2)}) collective-permute-start(f32[130,256]{1,0:T(8,128)} %get-tuple-element.963), channel_id=1, source_target_pairs={{1,0},{2,1},{3,2},{4,3},{5,4},{6,5},{7,6},{9,8},{10,9},{11,10},{12... | collective-permute-start | bytes 399368 | tf_op jit(solution)/shard_map/while/body/eval_jaxpr/ppermute | solution.py:20
  312.2 31.3 %collective-permute-done = f32[130,256]{1,0:T(8,128)S(1)} collective-permute-done((f32[130,256]{1,0:T(8,128)}, f32[130,256]{1,0:T(8,128)S(1)}, u32[]{:S(2)}, u32[]{:S(2)}) %collective-permute-start) | collective-permute-done | bytes 133152 | tf_op jit(solution)/shard_map/while/body/eval_jaxpr/ppermute | solution.py:20
  344.2 4.8 collective-permute-start.1
  349.1 27.1 %conditional.4 = (f32[130,256]{1,0:T(8,128)}, f32[128,3,64]{2,1,0:T(4,128)S(1)}) conditional(s32[]{:T(128)} %convert_element_type.78, f32[128,3,64]{2,1,0:T(4,128)S(1)} %get-tuple-element.1106, (pred[]{:T(512)}, s32[]{:T(128)}, f32[3,130,256]{2,1,0:T(8,128)S(1)}, f32[130,256]{1,0:T(8,128)S(1)}, bf16[128,3,64]{2,0,1:T(8,128)(2,1)S(1)}, ...), branch_computations={%region_1.1_spmd, %region_2.12_spmd} | conditional | flops 118179968 | bytes 2954274 | solution.py:226
  350.1 24.5 %while.64 = (s32[]{:T(128)}, f32[130,256]{1,0:T(8,128)}, f32[2,64,64]{2,1,0:T(8,128)S(1)}, bf16[2,64,64]{1,2,0:T(8,128)(2,1)S(1)}, f32[2,64]{1,0:T(2,128)S(1)}, ...) while((s32[]{:T(128)}, f32[130,256]{1,0:T(8,128)}, ...), condition=%wide.region_12.11_spmd, body=%wide.region_3.10_spmd.sunk | while | flops 118146688 | bytes 2256769 | solution.py:145
  374.6 1.5 dynamic_update_slice.14
  377.4 28.3 %collective-permute-done = f32[130,256]{1,0:T(8,128)S(1)} collective-permute-done((f32[130,256]{1,0:T(8,128)}, f32[130,256]{1,0:T(8,128)S(1)}, u32[]{:S(2)}, u32[]{:S(2)}) %collective-permute-start) | collective-permute-done | bytes 133152 | tf_op jit(solution)/shard_map/while/body/eval_jaxpr/ppermute | solution.py:20
  406.4 4.8 collective-permute-start.1
  411.2 27.1 %conditional.4 = (f32[130,256]{1,0:T(8,128)}, f32[128,3,64]{2,1,0:T(4,128)S(1)}) conditional(s32[]{:T(128)} %convert_element_type.78, f32[128,3,64]{2,1,0:T(4,128)S(1)} %get-tuple-element.1106, (pred[]{:T(512)}, s32[]{:T(128)}, f32[3,130,256]{2,1,0:T(8,128)S(1)}, f32[130,256]{1,0:T(8,128)S(1)}, bf16[128,3,64]{2,0,1:T(8,128)(2,1)S(1)}, ...), branch_computations={%region_1.1_spmd, %region_2.12_spmd} | conditional | flops 118179968 | bytes 2954274 | solution.py:226
  412.3 24.5 %while.64 = (s32[]{:T(128)}, f32[130,256]{1,0:T(8,128)}, f32[2,64,64]{2,1,0:T(8,128)S(1)}, bf16[2,64,64]{1,2,0:T(8,128)(2,1)S(1)}, f32[2,64]{1,0:T(2,128)S(1)}, ...) while((s32[]{:T(128)}, f32[130,256]{1,0:T(8,128)}, ...), condition=%wide.region_12.11_spmd, body=%wide.region_3.10_spmd.sunk | while | flops 118146688 | bytes 2256769 | solution.py:145
  436.8 1.5 dynamic_update_slice.14
  439.6 5.9 %collective-permute-done = f32[130,256]{1,0:T(8,128)S(1)} collective-permute-done((f32[130,256]{1,0:T(8,128)}, f32[130,256]{1,0:T(8,128)S(1)}, u32[]{:S(2)}, u32[]{:S(2)}) %collective-permute-start) | collective-permute-done | bytes 133152 | tf_op jit(solution)/shard_map/while/body/eval_jaxpr/ppermute | solution.py:20
  446.1 4.9 collective-permute-start.1
  451.1 27.1 %conditional.4 = (f32[130,256]{1,0:T(8,128)}, f32[128,3,64]{2,1,0:T(4,128)S(1)}) conditional(s32[]{:T(128)} %convert_element_type.78, f32[128,3,64]{2,1,0:T(4,128)S(1)} %get-tuple-element.1106, (pred[]{:T(512)}, s32[]{:T(128)}, f32[3,130,256]{2,1,0:T(8,128)S(1)}, f32[130,256]{1,0:T(8,128)S(1)}, bf16[128,3,64]{2,0,1:T(8,128)(2,1)S(1)}, ...), branch_computations={%region_1.1_spmd, %region_2.12_spmd} | conditional | flops 118179968 | bytes 2954274 | solution.py:226
  452.1 24.5 %while.64 = (s32[]{:T(128)}, f32[130,256]{1,0:T(8,128)}, f32[2,64,64]{2,1,0:T(8,128)S(1)}, bf16[2,64,64]{1,2,0:T(8,128)(2,1)S(1)}, f32[2,64]{1,0:T(2,128)S(1)}, ...) while((s32[]{:T(128)}, f32[130,256]{1,0:T(8,128)}, ...), condition=%wide.region_12.11_spmd, body=%wide.region_3.10_spmd.sunk | while | flops 118146688 | bytes 2256769 | solution.py:145
  476.6 1.5 dynamic_update_slice.14
  479.4 5.8 %collective-permute-done = f32[130,256]{1,0:T(8,128)S(1)} collective-permute-done((f32[130,256]{1,0:T(8,128)}, f32[130,256]{1,0:T(8,128)S(1)}, u32[]{:S(2)}, u32[]{:S(2)}) %collective-permute-start) | collective-permute-done | bytes 133152 | tf_op jit(solution)/shard_map/while/body/eval_jaxpr/ppermute | solution.py:20
  485.7 9.3 %all_to_all.80 = bf16[4,32,192]{2,1,0:T(8,128)(2,1)S(1)} all-to-all(bf16[4,32,192]{2,1,0:T(8,128)(2,1)S(1)} %bitcast.206), channel_id=1, replica_groups=mesh['head'=4,'seq'=8] {'head'}, dimensions={0} | all-to-all | bytes 98304 | tf_op jit(solution)/shard_map/all_to_all | solution.py:258
  (537 shorter events, 196.9 us)
Async XLA Ops:
  1.5 3.4 copy-start.2
  1.6 7.5 %all-to-all-start.1 = ((bf16[32,4,192]{2,0,1:T(8,128)(2,1)}), bf16[32,4,192]{2,0,1:T(8,128)(2,1)S(1)}, u32[]{:S(2)}, u32[]{:S(2)}) async-start(bf16[32,4,192]{2,0,1:T(8,128)(2,1)} %copy.40), calls=%async_computation.1 | async-start | bytes 131072 | tf_op jit(solution)/shard_map/all_to_all | solution.py:166
  5.1 7.4 %copy-start.8 = (f32[3,64]{1,0:T(4,128)S(1)}, f32[3,64]{1,0:T(4,128)}, u32[]{:S(2)}) copy-start(f32[3,64]{1,0:T(4,128)} %param.29) | copy-start | bytes 2308
  5.7 6.7 %copy-start.7 = (f32[3,256]{1,0:T(4,128)S(1)}, f32[3,256]{1,0:T(4,128)}, u32[]{:S(2)}) copy-start(f32[3,256]{1,0:T(4,128)} %param.27) | copy-start | bytes 9220
  5.7 6.8 %copy-start.3 = (bf16[32,768]{1,0:T(8,128)(2,1)S(1)}, bf16[32,768]{1,0:T(8,128)(2,1)}, u32[]{:S(2)}) copy-start(bf16[32,768]{1,0:T(8,128)(2,1)} %param.23) | copy-start | bytes 147460
  9.1 10.8 %copy-start.1 = (f32[3,64,256]{2,1,0:T(8,128)S(1)}, f32[3,64,256]{2,1,0:T(8,128)}, u32[]{:S(2)}) copy-start(f32[3,64,256]{2,1,0:T(8,128)} %param.26) | copy-start | bytes 589828
  9.1 7.5 %all-to-all-start.2 = ((bf16[32,4,192]{2,0,1:T(8,128)(2,1)}), bf16[32,4,192]{2,0,1:T(8,128)(2,1)S(1)}, u32[]{:S(2)}, u32[]{:S(2)}) async-start(bf16[32,4,192]{2,0,1:T(8,128)(2,1)} %copy.41), calls=%async_computation.2 | async-start | bytes 131072 | tf_op jit(solution)/shard_map/all_to_all | solution.py:167
  12.5 7.4 %copy-start = (f32[3,256,64]{1,2,0:T(8,128)S(1)}, f32[3,256,64]{1,2,0:T(8,128)}, u32[]{:S(2)}) copy-start(f32[3,256,64]{1,2,0:T(8,128)} %param.28) | copy-start | bytes 589828
  16.6 7.4 %all-to-all-start.3 = ((bf16[32,4,192]{2,0,1:T(8,128)(2,1)}), bf16[32,4,192]{2,0,1:T(8,128)(2,1)S(1)}, u32[]{:S(2)}, u32[]{:S(2)}) async-start(bf16[32,4,192]{2,0,1:T(8,128)(2,1)} %copy.42), calls=%async_computation.3 | async-start | bytes 131072 | tf_op jit(solution)/shard_map/all_to_all | solution.py:168
  19.9 0.8 copy-start.4
  23.9 461.7 %all-to-all-start = ((bf16[32,4,192]{2,0,1:T(8,128)(2,1)}), bf16[32,4,192]{2,0,1:T(8,128)(2,1)S(1)}, u32[]{:S(2)}, u32[]{:S(2)}) async-start(bf16[32,4,192]{2,0,1:T(8,128)(2,1)} %copy.39), calls=%async_computation | async-start | bytes 131072 | tf_op jit(solution)/shard_map/all_to_all | solution.py:169
  27.6 0.7 copy-start.5
  27.6 0.7 copy-start.6
  27.6 0.7 copy-start.9
  55.7 5.4 %collective-permute-start.1 = (f32[130,256]{1,0:T(8,128)}, f32[130,256]{1,0:T(8,128)S(1)}, u32[]{:S(2)}, u32[]{:S(2)}) collective-permute-start(f32[130,256]{1,0:T(8,128)} %get-tuple-element.963), channel_id=1, source_target_pairs={{1,0},{2,1},{3,2},{4,3},{5,4},{6,5},{7,6},{9,8},{10,9},{11,10},{12... | collective-permute-start | bytes 399368 | tf_op jit(solution)/shard_map/while/body/eval_jaxpr/ppermute | solution.py:20
  57.7 8.1 %collective-permute-start = (f32[130,256]{1,0:T(8,128)}, f32[130,256]{1,0:T(8,128)S(1)}, u32[]{:S(2)}, u32[]{:S(2)}) collective-permute-start(f32[130,256]{1,0:T(8,128)} %get-tuple-element.962), channel_id=1, source_target_pairs={{0,1},{1,2},{2,3},{3,4},{4,5},{5,6},{6,7},{8,9},{9,10},{10,11},{11... | collective-permute-start | bytes 399368 | tf_op jit(solution)/shard_map/while/body/eval_jaxpr/ppermute | solution.py:20
  93.3 4.7 collective-permute-start.1
  95.5 7.1 %collective-permute-start = (f32[130,256]{1,0:T(8,128)}, f32[130,256]{1,0:T(8,128)S(1)}, u32[]{:S(2)}, u32[]{:S(2)}) collective-permute-start(f32[130,256]{1,0:T(8,128)} %get-tuple-element.962), channel_id=1, source_target_pairs={{0,1},{1,2},{2,3},{3,4},{4,5},{5,6},{6,7},{8,9},{9,10},{10,11},{11... | collective-permute-start | bytes 399368 | tf_op jit(solution)/shard_map/while/body/eval_jaxpr/ppermute | solution.py:20
  130.1 5.9 %collective-permute-start.1 = (f32[130,256]{1,0:T(8,128)}, f32[130,256]{1,0:T(8,128)S(1)}, u32[]{:S(2)}, u32[]{:S(2)}) collective-permute-start(f32[130,256]{1,0:T(8,128)} %get-tuple-element.963), channel_id=1, source_target_pairs={{1,0},{2,1},{3,2},{4,3},{5,4},{6,5},{7,6},{9,8},{10,9},{11,10},{12... | collective-permute-start | bytes 399368 | tf_op jit(solution)/shard_map/while/body/eval_jaxpr/ppermute | solution.py:20
  133.8 7.1 %collective-permute-start = (f32[130,256]{1,0:T(8,128)}, f32[130,256]{1,0:T(8,128)S(1)}, u32[]{:S(2)}, u32[]{:S(2)}) collective-permute-start(f32[130,256]{1,0:T(8,128)} %get-tuple-element.962), channel_id=1, source_target_pairs={{0,1},{1,2},{2,3},{3,4},{4,5},{5,6},{6,7},{8,9},{9,10},{10,11},{11... | collective-permute-start | bytes 399368 | tf_op jit(solution)/shard_map/while/body/eval_jaxpr/ppermute | solution.py:20
  141.6 32.5 %collective-permute-start.1 = (f32[130,256]{1,0:T(8,128)}, f32[130,256]{1,0:T(8,128)S(1)}, u32[]{:S(2)}, u32[]{:S(2)}) collective-permute-start(f32[130,256]{1,0:T(8,128)} %get-tuple-element.963), channel_id=1, source_target_pairs={{1,0},{2,1},{3,2},{4,3},{5,4},{6,5},{7,6},{9,8},{10,9},{11,10},{12... | collective-permute-start | bytes 399368 | tf_op jit(solution)/shard_map/while/body/eval_jaxpr/ppermute | solution.py:20
  171.9 7.1 %collective-permute-start = (f32[130,256]{1,0:T(8,128)}, f32[130,256]{1,0:T(8,128)S(1)}, u32[]{:S(2)}, u32[]{:S(2)}) collective-permute-start(f32[130,256]{1,0:T(8,128)} %get-tuple-element.962), channel_id=1, source_target_pairs={{0,1},{1,2},{2,3},{3,4},{4,5},{5,6},{6,7},{8,9},{9,10},{10,11},{11... | collective-permute-start | bytes 399368 | tf_op jit(solution)/shard_map/while/body/eval_jaxpr/ppermute | solution.py:20
  179.7 5.7 %collective-permute-start.1 = (f32[130,256]{1,0:T(8,128)}, f32[130,256]{1,0:T(8,128)S(1)}, u32[]{:S(2)}, u32[]{:S(2)}) collective-permute-start(f32[130,256]{1,0:T(8,128)} %get-tuple-element.963), channel_id=1, source_target_pairs={{1,0},{2,1},{3,2},{4,3},{5,4},{6,5},{7,6},{9,8},{10,9},{11,10},{12... | collective-permute-start | bytes 399368 | tf_op jit(solution)/shard_map/while/body/eval_jaxpr/ppermute | solution.py:20
  183.2 32.9 %collective-permute-start = (f32[130,256]{1,0:T(8,128)}, f32[130,256]{1,0:T(8,128)S(1)}, u32[]{:S(2)}, u32[]{:S(2)}) collective-permute-start(f32[130,256]{1,0:T(8,128)} %get-tuple-element.962), channel_id=1, source_target_pairs={{0,1},{1,2},{2,3},{3,4},{4,5},{5,6},{6,7},{8,9},{9,10},{10,11},{11... | collective-permute-start | bytes 399368 | tf_op jit(solution)/shard_map/while/body/eval_jaxpr/ppermute | solution.py:20
  216.8 7.4 %collective-permute-start.1 = (f32[130,256]{1,0:T(8,128)}, f32[130,256]{1,0:T(8,128)S(1)}, u32[]{:S(2)}, u32[]{:S(2)}) collective-permute-start(f32[130,256]{1,0:T(8,128)} %get-tuple-element.963), channel_id=1, source_target_pairs={{1,0},{2,1},{3,2},{4,3},{5,4},{6,5},{7,6},{9,8},{10,9},{11,10},{12... | collective-permute-start | bytes 399368 | tf_op jit(solution)/shard_map/while/body/eval_jaxpr/ppermute | solution.py:20
  222.1 28.9 %collective-permute-start = (f32[130,256]{1,0:T(8,128)}, f32[130,256]{1,0:T(8,128)S(1)}, u32[]{:S(2)}, u32[]{:S(2)}) collective-permute-start(f32[130,256]{1,0:T(8,128)} %get-tuple-element.962), channel_id=1, source_target_pairs={{0,1},{1,2},{2,3},{3,4},{4,5},{5,6},{6,7},{8,9},{9,10},{10,11},{11... | collective-permute-start | bytes 399368 | tf_op jit(solution)/shard_map/while/body/eval_jaxpr/ppermute | solution.py:20
  251.6 60.6 %collective-permute-start.1 = (f32[130,256]{1,0:T(8,128)}, f32[130,256]{1,0:T(8,128)S(1)}, u32[]{:S(2)}, u32[]{:S(2)}) collective-permute-start(f32[130,256]{1,0:T(8,128)} %get-tuple-element.963), channel_id=1, source_target_pairs={{1,0},{2,1},{3,2},{4,3},{5,4},{6,5},{7,6},{9,8},{10,9},{11,10},{12... | collective-permute-start | bytes 399368 | tf_op jit(solution)/shard_map/while/body/eval_jaxpr/ppermute | solution.py:20
  310.0 33.6 %collective-permute-start = (f32[130,256]{1,0:T(8,128)}, f32[130,256]{1,0:T(8,128)S(1)}, u32[]{:S(2)}, u32[]{:S(2)}) collective-permute-start(f32[130,256]{1,0:T(8,128)} %get-tuple-element.962), channel_id=1, source_target_pairs={{0,1},{1,2},{2,3},{3,4},{4,5},{5,6},{6,7},{8,9},{9,10},{10,11},{11... | collective-permute-start | bytes 399368 | tf_op jit(solution)/shard_map/while/body/eval_jaxpr/ppermute | solution.py:20
  344.2 33.2 %collective-permute-start.1 = (f32[130,256]{1,0:T(8,128)}, f32[130,256]{1,0:T(8,128)S(1)}, u32[]{:S(2)}, u32[]{:S(2)}) collective-permute-start(f32[130,256]{1,0:T(8,128)} %get-tuple-element.963), channel_id=1, source_target_pairs={{1,0},{2,1},{3,2},{4,3},{5,4},{6,5},{7,6},{9,8},{10,9},{11,10},{12... | collective-permute-start | bytes 399368 | tf_op jit(solution)/shard_map/while/body/eval_jaxpr/ppermute | solution.py:20
  376.1 29.6 %collective-permute-start = (f32[130,256]{1,0:T(8,128)}, f32[130,256]{1,0:T(8,128)S(1)}, u32[]{:S(2)}, u32[]{:S(2)}) collective-permute-start(f32[130,256]{1,0:T(8,128)} %get-tuple-element.962), channel_id=1, source_target_pairs={{0,1},{1,2},{2,3},{3,4},{4,5},{5,6},{6,7},{8,9},{9,10},{10,11},{11... | collective-permute-start | bytes 399368 | tf_op jit(solution)/shard_map/while/body/eval_jaxpr/ppermute | solution.py:20
  406.4 33.2 %collective-permute-start.1 = (f32[130,256]{1,0:T(8,128)}, f32[130,256]{1,0:T(8,128)S(1)}, u32[]{:S(2)}, u32[]{:S(2)}) collective-permute-start(f32[130,256]{1,0:T(8,128)} %get-tuple-element.963), channel_id=1, source_target_pairs={{1,0},{2,1},{3,2},{4,3},{5,4},{6,5},{7,6},{9,8},{10,9},{11,10},{12... | collective-permute-start | bytes 399368 | tf_op jit(solution)/shard_map/while/body/eval_jaxpr/ppermute | solution.py:20
  438.3 7.2 %collective-permute-start = (f32[130,256]{1,0:T(8,128)}, f32[130,256]{1,0:T(8,128)S(1)}, u32[]{:S(2)}, u32[]{:S(2)}) collective-permute-start(f32[130,256]{1,0:T(8,128)} %get-tuple-element.962), channel_id=1, source_target_pairs={{0,1},{1,2},{2,3},{3,4},{4,5},{5,6},{6,7},{8,9},{9,10},{10,11},{11... | collective-permute-start | bytes 399368 | tf_op jit(solution)/shard_map/while/body/eval_jaxpr/ppermute | solution.py:20
  446.1 33.3 %collective-permute-start.1 = (f32[130,256]{1,0:T(8,128)}, f32[130,256]{1,0:T(8,128)S(1)}, u32[]{:S(2)}, u32[]{:S(2)}) collective-permute-start(f32[130,256]{1,0:T(8,128)} %get-tuple-element.963), channel_id=1, source_target_pairs={{1,0},{2,1},{3,2},{4,3},{5,4},{6,5},{7,6},{9,8},{10,9},{11,10},{12... | collective-permute-start | bytes 399368 | tf_op jit(solution)/shard_map/while/body/eval_jaxpr/ppermute | solution.py:20
  478.1 7.2 %collective-permute-start = (f32[130,256]{1,0:T(8,128)}, f32[130,256]{1,0:T(8,128)S(1)}, u32[]{:S(2)}, u32[]{:S(2)}) collective-permute-start(f32[130,256]{1,0:T(8,128)} %get-tuple-element.962), channel_id=1, source_target_pairs={{0,1},{1,2},{2,3},{3,4},{4,5},{5,6},{6,7},{8,9},{9,10},{10,11},{11... | collective-permute-start | bytes 399368 | tf_op jit(solution)/shard_map/while/body/eval_jaxpr/ppermute | solution.py:20
where the time goes:
time: 503 us; the launch traced here: 496 us
  waiting for transfers between devices  165 us (33%)
  starting transfers between devices  141 us (28%)
  matrix products  98.8 us (20%)
  local copies, waits for them, and re-layouts  46 us (9%)
  other arithmetic  33.5 us (7%)
  blocking collectives  9.27 us (2%)
    ppermute x20, waiting for transfers between devices, shifted(): return lax.ppermute(block, axis, route)  156 us
    ppermute x20, starting transfers between devices, shifted(): return lax.ppermute(block, axis, route)  128 us
    dot_general x12, matrix products, gradients(): jnp.dot(grad_two, second_turned, precision=highest) * gelu_slope(pre_one)  13.4 us
    dot_general x12, matrix products, gradients(): jnp.einsum('ti,di->td', act_one, second_turned, precision=highest)  13 us
    dot_general x12, matrix products, renew(): jnp.einsum('td,ti->di', key_block, weighted_one, precision=highest)  13 us
    dot_general x12, matrix products, gradients(): pre_one = jnp.dot(key_block, weight_one, precision=highest) + bias_one  12.8 us
    dot_general x12, matrix products, renew(): jnp.einsum('td,ti->di', weighted_two, act_one, precision=highest)  12.7 us
    dot_general x12, matrix products, dual_output(): jnp.einsum('si,di->sd', dual_act, second_turned, precision=highest)  12.5 us
  transfers between devices with their start and end apart: 24, of which 20 were waited for; matrix products, arithmetic and copies ran while one was open for 35% of the time, Pallas kernels for 0%

commit v1 on v0

v1 whole, which is shorter than its diff:
```python
import functools

import jax
import jax.numpy as jnp
from jax import lax
from jax.experimental import pallas as pl
from jax.experimental.pallas import tpu as pltpu
from jax.sharding import PartitionSpec as P

D_HEAD = 64
INNER = 256
MINI = 64
CHUNK = 8

eps_norm = 1e-06
root_factor = 0.7978845608028654
cube_factor = 0.044715
f32 = jnp.float32
bf16 = jnp.bfloat16


def mm(left, right):
    return lax.dot_general(left, right, (((1,), (0,)), ((), ())), preferred_element_type=f32)


def mm_turned(left, right):
    return lax.dot_general(left, right, (((1,), (1,)), ((), ())), preferred_element_type=f32)


def gelu_and_slope(values):
    square = values * values
    tanh_term = jnp.tanh(values * (root_factor + root_factor * cube_factor * square))
    half = 0.5 + 0.5 * tanh_term
    act = values * half
    inner = root_factor + 3.0 * root_factor * cube_factor * square
    return act, half + act * (1.0 - tanh_term) * inner


def gelu(values):
    tanh_term = jnp.tanh(values * (root_factor + root_factor * cube_factor * (values * values)))
    return values * (0.5 + 0.5 * tanh_term)


def row_mean(values):
    return jnp.mean(values, axis=1, keepdims=True)


def run_chunk(first_step, steps, total, backward, qk_ref, v_ref, r_ref, state, gain, shift, emit):
    weight_one, bias_one, second_turned, bias_two = state
    rows = lax.broadcasted_iota(jnp.int32, (MINI, MINI), 0)
    columns = lax.broadcasted_iota(jnp.int32, (MINI, MINI), 1)
    ahead = rows - columns
    seen = jnp.where(backward == 0, ahead, -ahead) >= 0
    gain_square = gain * gain

    def place(step):
        return jnp.where(backward == 0, step, total - 1 - step)

    def load_qk(step):
        return qk_ref[pl.ds(pl.multiple_of(place(step) * MINI, MINI), MINI), :]

    pre_one = None
    qk = load_qk(first_step)
    for local_step in range(steps):
        step = first_step + local_step
        spot = place(step)
        value = v_ref[pl.ds(pl.multiple_of(spot * MINI, MINI), MINI), :].astype(f32)
        rate = r_ref[spot]
        query, key = qk[:, :D_HEAD], qk[:, D_HEAD:]
        if local_step + 1 < steps:
            qk = load_qk(step + 1)
            next_key = qk[:, D_HEAD:]
        else:
            next_key = key
        first_high = weight_one.astype(bf16)
        first_low = (weight_one - first_high.astype(f32)).astype(bf16)
        second_high = second_turned.astype(bf16)
        probes = jnp.concatenate([next_key, query], axis=0)
        plain = mm(
            jnp.concatenate([probes, probes], axis=1),
            jnp.concatenate([first_high, first_low], axis=0),
        ) + bias_one
        if pre_one is None:
            pre_one = mm(key, first_high) + mm(key, first_low) + bias_one
        attend = (mm_turned(probes, key) + 1.0) * rate
        mixer = jnp.concatenate(
            [
                attend[:MINI],
                jnp.where(seen, attend[MINI:], 0.0),
                key.astype(f32).T * rate,
                jnp.broadcast_to(rate, (16, MINI)),
            ],
            axis=0,
        ).astype(bf16)
        act, slope = gelu_and_slope(pre_one)
        act_high = act.astype(bf16)
        centred = mm_turned(act_high, second_high) + bias_two
        pull = gain * (shift - value + key.astype(f32))
        scaled = gain_square * centred
        inverse = lax.rsqrt(row_mean(centred * centred) + eps_norm)
        mean_a = inverse * row_mean(scaled) + row_mean(pull)
        mean_an = inverse * (inverse * row_mean(scaled * centred) + row_mean(pull * centred))
        grad_two = inverse * ((gain_square - mean_an) * (inverse * centred) + (pull - mean_a))
        grad_two_high = grad_two.astype(bf16)
        grad_one = (mm(grad_two_high, second_high) * slope).astype(bf16)
        mixed = mm(mixer, grad_one)
        pre_one = plain[:MINI] - mixed[:MINI]
        dual_act = gelu(plain[MINI:] - mixed[MINI : 2 * MINI])
        dual_high = dual_act.astype(bf16)
        dual_low = (dual_act - dual_high.astype(f32)).astype(bf16)
        attend_two = jnp.where(seen, (mm_turned(dual_high, act_high) + 1.0) * rate, 0.0)
        pulled = mm(
            jnp.concatenate([attend_two, jnp.broadcast_to(rate, (16, MINI))], axis=0).astype(bf16),
            grad_two_high,
        )
        dual_two = (
            mm_turned(dual_high, second_high) + mm_turned(dual_low, second_high) + bias_two - pulled[:MINI]
        )
        spread = lax.rsqrt(row_mean(dual_two * dual_two) + eps_norm)
        emit(spot, gain * (dual_two * spread) + shift)
        weight_one = weight_one - mixed[2 * MINI : 3 * MINI]
        bias_one = bias_one - mixed[3 * MINI : 3 * MINI + 1]
        second_turned = second_turned - mm((grad_two.T * rate).astype(bf16), act_high)
        bias_two = bias_two - pulled[MINI : MINI + 1]
    return weight_one, bias_one, second_turned, bias_two


def run_phase(total, backward, qk_ref, v_ref, r_ref, state_refs, gain, shift, emit):
    def chunk(first_step, steps):
        state = tuple(ref[...] for ref in state_refs)
        state = run_chunk(
            first_step, steps, total, backward, qk_ref, v_ref, r_ref, state, gain, shift, emit
        )
        for ref, part in zip(state_refs, state):
            ref[...] = part

    if total <= CHUNK:
        chunk(0, total)
    else:
        assert total % CHUNK == 0

        def body(index, carry):
            chunk(index * CHUNK, CHUNK)
            return carry

        lax.fori_loop(0, total // CHUNK, body, 0)


def centre_start(w1_ref, c1_ref, w2t_ref, c2_ref):
    second_turned = w2t_ref[...]
    second_turned = second_turned - jnp.mean(second_turned, axis=0, keepdims=True)
    bias_two = c2_ref[...] - row_mean(c2_ref[...])
    return w1_ref[...], c1_ref[...], second_turned, bias_two


def first_phase(total, dir_ref, qk_ref, v_ref, r_ref, w1_ref, c1_ref, w2t_ref, c2_ref, gain_ref, shift_ref,
                y_ref, delta_ref, *state_refs):
    start = centre_start(w1_ref, c1_ref, w2t_ref, c2_ref)
    for ref, part in zip(state_refs, start):
        ref[...] = part

    def emit(spot, rows):
        y_ref[pl.ds(pl.multiple_of(spot * MINI, MINI), MINI), :] = rows

    run_phase(total, dir_ref[0], qk_ref, v_ref, r_ref, state_refs, gain_ref[...], shift_ref[...], emit)
    start = centre_start(w1_ref, c1_ref, w2t_ref, c2_ref)
    ends = [ref[...] - part for ref, part in zip(state_refs, start)]
    delta_ref[0:D_HEAD, :] = ends[0].astype(bf16)
    delta_ref[D_HEAD : 2 * D_HEAD, :] = ends[2].astype(bf16)
    wide = jnp.concatenate([ends[3], jnp.zeros((1, INNER - D_HEAD), f32)], axis=1)
    delta_ref[2 * D_HEAD : 2 * D_HEAD + 16, :] = jnp.concatenate(
        [jnp.broadcast_to(ends[1], (8, INNER)), jnp.broadcast_to(wide, (8, INNER))], axis=0
    ).astype(bf16)


def second_phase(total, dir_ref, qk_ref, v_ref, r_ref, w1_ref, c1_ref, w2t_ref, c2_ref, gain_ref, shift_ref,
                 y_ref, delta_ref, out_ref, *state_refs):
    start = centre_start(w1_ref, c1_ref, w2t_ref, c2_ref)
    biases = delta_ref[2 * D_HEAD : 2 * D_HEAD + 16, :].astype(f32)
    deltas = (
        delta_ref[0:D_HEAD, :].astype(f32),
        biases[0:1],
        delta_ref[D_HEAD : 2 * D_HEAD, :].astype(f32),
        biases[8:9, :D_HEAD],
    )
    for ref, part, delta in zip(state_refs, start, deltas):
        ref[...] = part + delta

    def emit(spot, rows):
        spots = pl.ds(pl.multiple_of(spot * MINI, MINI), MINI)
        out_ref[spots, :] = (y_ref[spots, :] + rows).astype(bf16)

    run_phase(total, dir_ref[0], qk_ref, v_ref, r_ref, state_refs, gain_ref[...], shift_ref[...], emit)


def call_phase(kernel, total, outs, *operands):
    in_vmem = pl.BlockSpec(memory_space=pltpu.VMEM)
    return pl.pallas_call(
        functools.partial(kernel, total),
        out_shape=outs,
        in_specs=[pl.BlockSpec(memory_space=pltpu.SMEM)] + [in_vmem] * (len(operands) - 1),
        out_specs=[in_vmem] * len(outs),
        scratch_shapes=[
            pltpu.VMEM((D_HEAD, INNER), f32),
            pltpu.VMEM((1, INNER), f32),
            pltpu.VMEM((D_HEAD, INNER), f32),
            pltpu.VMEM((1, D_HEAD), f32),
        ],
        compiler_params=pltpu.CompilerParams(vmem_limit_bytes=24 * 2**20),
    )(*operands)


def local(head_size, seq_size, query_rows, key_rows, value_rows, gate_rows, step_rates, first_weight,
          first_bias, second_weight, second_bias, norm_gain, norm_shift):
    rows_here = query_rows.shape[0]
    heads_local = step_rates.shape[1]
    token_block = step_rates.shape[0]
    half_seq = seq_size // 2
    group = half_seq * head_size
    half_tokens = group * rows_here
    total = half_tokens // MINI
    spare = half_seq - heads_local
    seq_at = lax.axis_index("seq")
    half = seq_at // half_seq
    slot = jnp.minimum(seq_at % half_seq, heads_local - 1)
    group_at = lax.axis_index("head")
    halves = [
        [s * head_size + h for s in range(k * half_seq, (k + 1) * half_seq) for h in range(head_size)]
        for k in range(2)
    ]

    def exchange(blocks):
        return lax.all_to_all(blocks, ("seq", "head"), 0, 0, axis_index_groups=halves)

    def by_slot(rows):
        return rows.reshape(rows_here, head_size, heads_local, D_HEAD).transpose(2, 1, 0, 3)

    query, key, value = by_slot(query_rows), by_slot(key_rows), by_slot(value_rows)
    pairs = jnp.concatenate([query, key], axis=3)
    folded = jnp.concatenate([value[:, :, : rows_here // 2], value[:, :, rows_here // 2 :]], axis=3)
    rates = step_rates.T
    high = rates.astype(bf16)
    rest = rates - high.astype(f32)
    middle = rest.astype(bf16)
    low = (rest - middle.astype(f32)).astype(bf16)
    rate_rows = jnp.stack([high, middle, low], axis=1)
    rate_rows = jnp.concatenate([rate_rows, jnp.zeros((heads_local, 5, token_block), bf16)], axis=1)
    rate_rows = jnp.broadcast_to(rate_rows[:, None], (heads_local, head_size, 8, token_block))
    blocks = jnp.concatenate([pairs, folded, rate_rows], axis=2)
    blocks = jnp.concatenate([blocks, jnp.zeros((spare,) + blocks.shape[1:], bf16)], axis=0)
    got = exchange(blocks.reshape((group,) + blocks.shape[2:]))

    qk_all = got[:, :rows_here].reshape(half_tokens, 2 * D_HEAD)
    got_value = got[:, rows_here : rows_here + rows_here // 2]
    v_all = jnp.stack([got_value[..., :D_HEAD], got_value[..., D_HEAD:]], axis=1).reshape(half_tokens, D_HEAD)
    got_rate = got[:, rows_here + rows_here // 2 :].reshape(half_seq, head_size, 8, token_block)
    got_rate = lax.dynamic_index_in_dim(got_rate, group_at, 1, keepdims=False).astype(f32)
    r_all = (got_rate[:, 0] + got_rate[:, 1] + got_rate[:, 2]).reshape(total, 1, MINI)

    def pick(array_in):
        return lax.dynamic_index_in_dim(array_in, slot, 0, keepdims=False)

    params = (
        pick(first_weight),
        pick(first_bias)[None],
        pick(second_weight).T,
        pick(second_bias)[None],
        pick(norm_gain)[None],
        pick(norm_shift)[None],
    )
    ahead = half.astype(jnp.int32).reshape(1)
    y_first, delta = call_phase(
        first_phase,
        total,
        [
            jax.ShapeDtypeStruct((half_tokens, D_HEAD), f32),
            jax.ShapeDtypeStruct((2 * D_HEAD + 16, INNER), bf16),
        ],
        ahead, qk_all, v_all, r_all, *params,
    )
    route = [(s, (s + half_seq) % seq_size) for s in range(seq_size)]
    delta = lax.ppermute(delta, "seq", route)
    (summed,) = call_phase(
        second_phase,
        total,
        [jax.ShapeDtypeStruct((half_tokens, D_HEAD), bf16)],
        1 - ahead, qk_all, v_all, r_all, *params, y_first, delta,
    )
    summed = summed.reshape(group, 2, rows_here // 2, D_HEAD)
    back = exchange(jnp.concatenate([summed[:, 0], summed[:, 1]], axis=2))
    back = back.reshape(half_seq, head_size, rows_here // 2, 2, D_HEAD)[:heads_local]
    back = back.transpose(3, 2, 1, 0, 4).reshape(rows_here, head_size * heads_local * D_HEAD)
    return (gate_rows.astype(f32) * back.astype(f32)).astype(bf16)


def solution(mesh):
    tokens = P(("seq", "head"), None)
    in_specs = (
        tokens,
        tokens,
        tokens,
        tokens,
        P("seq", "head"),
        P("head", None, None),
        P("head", None),
        P("head", None, None),
        P("head", None),
        P("head", None),
        P("head", None),
    )
    body = functools.partial(local, mesh.shape["head"], mesh.shape["seq"])
    return jax.shard_map(body, mesh=mesh, in_specs=in_specs, out_specs=tokens, check_vma=False)
```

time: 503 us -> 48.5 us (0.10)
  the two profiles are of different devices: /device:TPU:26 before, /device:TPU:0 now
where the time goes in v1:
time: 48.5 us; the launch traced here: 48 us
  Pallas kernels  13.6 us (28%)
  starting transfers between devices  8.94 us (18%)
  blocking collectives  8.4 us (17%)
  waiting for transfers between devices  7.86 us (16%)
  local copies, waits for them, and re-layouts  7.05 us (15%)
  other arithmetic  1.92 us (4%)
    pallas_call x2, Pallas kernels, call_phase(): pl.pallas_call(functools.partial(kernel, total), out_shape=outs, in_specs...  13.6 us
    all_to_all x1, blocking collectives, exchange(): lax.all_to_all(blocks, ('seq', 'head'), 0, 0, axis_index_groups=halves)  8.4 us
    all_to_all x1, starting transfers between devices, exchange(): lax.all_to_all(blocks, ('seq', 'head'), 0, 0, axis_index_groups=halves)  6.29 us
    all_to_all x1, waiting for transfers between devices, exchange(): lax.all_to_all(blocks, ('seq', 'head'), 0, 0, axis_index_groups=halves)  4.41 us
    ppermute x1, waiting for transfers between devices, local(): delta = lax.ppermute(delta, 'seq', route)  3.45 us
    ppermute x1, starting transfers between devices, local(): delta = lax.ppermute(delta, 'seq', route)  2.65 us
    dynamic_slice x3, local copies, waits for them, and re-layouts, pick(): return lax.dynamic_index_in_dim(array_in, slot, 0, keepdims=False)  2.08 us
    unnamed x11, local copies, waits for them, and re-layouts  1.3 us
  transfers between devices with their start and end apart: 2, of which 2 were waited for; matrix products, arithmetic and copies ran while one was open for 6% of the time, Pallas kernels for 0%

profile of v1, /device:TPU:0, one launch (start us, length us, event | category | flops | bytes accessed | tf_op | source)
XLA Modules:
  0.0 48.0 jit_solution(10506725690967986050)
XLA Ops:
  0.0 0.0 copy-start
  0.0 0.0 copy-start.4
  0.0 0.8 %fusion.2 = bf16[3,1,128]{2,0,1:T(4,128)(2,1)S(1)} fusion(f32[128,3]{0,1:T(4,128)} %param.15), kind=kLoop, calls=%fused_computation.24 | loop fusion | flops 384 | bytes 2304 | tf_op jit(solution)/shard_map/stack | solution.py:246
  0.8 0.0 copy-done.4
  0.8 0.0 copy-start.1
  0.8 1.0 %reshape.68 = bf16[32,4,3,64]{3,2,1,0:T(4,128)(2,1)S(1)} reshape(bf16[32,768]{1,0:T(8,128)(2,1)} %param.11) | data formatting | bytes 98304 | tf_op jit(solution)/shard_map/reshape | solution.py:236
  1.7 0.0 copy-done.1
  1.7 0.0 copy-start.2
  1.8 0.1 reshape.69
  1.9 0.6 %copy-done.2 = bf16[32,768]{1,0:T(8,128)(2,1)S(1)} copy-done((bf16[32,768]{1,0:T(8,128)(2,1)S(1)}, bf16[32,768]{1,0:T(8,128)(2,1)}, u32[]{:S(2)}) %copy-start.2) | copy-done | bytes 49176
  2.5 0.1 reshape.70
  2.8 0.1 pad.13.clone
  2.8 0.1 maximum_maximum_fusion
  2.9 0.3 pad_maximum_fusion
  3.2 0.1 copy.25
  3.3 0.7 %concatenate.22.clone = bf16[4,4,56,128]{3,2,1,0:T(8,128)(2,1)} pad(bf16[3,4,56,128]{3,2,1,0:T(8,128)(2,1)S(1)} %copy.25, bf16[]{:T(256)} %constant.61.clone.1), padding=0_1x0_0x0_0x0_0 | pad | bytes 401410 | tf_op jit(solution)/shard_map/concatenate | solution.py:250
  4.0 6.3 %all-to-all-start = ((bf16[16,56,128]{2,1,0:T(8,128)(2,1)}), bf16[16,56,128]{2,1,0:T(8,128)(2,1)S(1)}, u32[]{:S(2)}, u32[]{:S(2)}) async-start(bf16[16,56,128]{2,1,0:T(8,128)(2,1)} %bitcast.8), calls=%async_computation | async-start | bytes 458752 | tf_op jit(solution)/shard_map/all_to_all | solution.py:233
  10.3 0.7 %constant_dynamic-slice_fusion.3.c1_ref = f32[1,256]{1,0:T(1,128)S(1)} fusion(f32[3,256]{1,0:T(4,128)} %param.17, s32[]{:T(128)S(6)} %select_n.30), kind=kLoop, calls=%fused_computation.22 | loop fusion | bytes 2052 | tf_op jit(solution)/shard_map/jit(dynamic_index_in_dim)/dynamic_slice | solution.py:261
  11.0 0.7 %constant_dynamic-slice_fusion.2.c2_ref = f32[1,64]{1,0:T(1,128)S(1)} fusion(f32[3,64]{1,0:T(4,128)} %param.19, s32[]{:T(128)S(6)} %select_n.30), kind=kLoop, calls=%fused_computation.21 | loop fusion | bytes 516 | tf_op jit(solution)/shard_map/jit(dynamic_index_in_dim)/dynamic_slice | solution.py:261
  11.7 0.7 %constant_dynamic-slice_fusion = (f32[1,64]{1,0:T(1,128)S(1)}, f32[1,64]{1,0:T(1,128)S(1)}) fusion(f32[3,64]{1,0:T(4,128)} %param.21, s32[]{:T(128)S(6)} %select_n.30, f32[3,64]{1,0:T(4,128)} %param.20), kind=kLoop, calls=%fused_computation.19 | loop fusion | bytes 1028 | tf_op jit(solution)/shard_map/jit(dynamic_index_in_dim)/dynamic_slice | solution.py:261
  12.4 0.0 copy-done
  12.4 0.9 %dynamic-slice_bitcast_fusion.w2t_ref = f32[64,256]{1,0:T(8,128)S(1)} fusion(f32[3,256,64]{1,2,0:T(8,128)} %param.18, s32[]{:T(128)S(6)} %select_n.30), kind=kLoop, calls=%fused_computation.8 | loop fusion | bytes 131076 | tf_op jit(solution)/shard_map/transpose | solution.py:266
  13.3 4.4 %all-to-all-done = bf16[16,56,128]{2,1,0:T(8,128)(2,1)S(1)} async-done(((bf16[16,56,128]{2,1,0:T(8,128)(2,1)}), bf16[16,56,128]{2,1,0:T(8,128)(2,1)S(1)}, u32[]{:S(2)}, u32[]{:S(2)}) %all-to-all-start) | async-done | bytes 229408 | tf_op jit(solution)/shard_map/all_to_all | solution.py:233
  17.7 0.1 add.50.r_ref
  17.8 0.1 slice_bitcast_fusion.3
  18.0 6.8 %shard_map.109 = (f32[512,64]{1,0:T(8,128)S(1)}, bf16[144,256]{1,0:T(8,128)(2,1)S(1)}) custom-call(s32[1]{0:T(128)} %bitcast.dir_ref, bf16[512,128]{1,0:T(8,128)(2,1)S(1)} %bitcast.58, bf16[512,64]{1,0:T(8,128)(2,1)S(1)} %bitcast.56, f32[8,1,64]{2,1,0:T(1,128)S(1)} %add.50.r_ref, f32[64,256]{1,0:T(8,128)S(1)} %dynamic-slice_bitcast_fusion.1.w1_ref, ...), custom_call_target="tpu_custom_call" | custom-call | tf_op jit(solution)/shard_map/pallas_call | solution.py:198
  24.8 2.7 %collective-permute-start = (bf16[144,256]{1,0:T(8,128)(2,1)S(1)}, bf16[144,256]{1,0:T(8,128)(2,1)S(1)}, u32[]{:S(2)}, u32[]{:S(2)}) collective-permute-start(bf16[144,256]{1,0:T(8,128)(2,1)S(1)} %get-tuple-element.8), channel_id=1, source_target_pairs={{0,4},{1,5},{2,6},{3,7},{4,0},{5,1},{6,2},{7,3},{8,12},{9,13},{10,... | collective-permute-start | bytes 221192 | tf_op jit(solution)/shard_map/ppermute | solution.py:282
  27.5 3.5 %collective-permute-done.delta_ref = bf16[144,256]{1,0:T(8,128)(2,1)S(1)} collective-permute-done((bf16[144,256]{1,0:T(8,128)(2,1)S(1)}, bf16[144,256]{1,0:T(8,128)(2,1)S(1)}, u32[]{:S(2)}, u32[]{:S(2)}) %collective-permute-start) | collective-permute-done | bytes 73760 | tf_op jit(solution)/shard_map/ppermute | solution.py:282
  30.9 6.8 %shard_map.110 = bf16[512,64]{1,0:T(8,128)(2,1)S(1)} custom-call(s32[1]{0:T(128)S(6)} %sub.14.dir_ref, bf16[512,128]{1,0:T(8,128)(2,1)S(1)} %bitcast.59, bf16[512,64]{1,0:T(8,128)(2,1)S(1)} %bitcast.57, f32[8,1,64]{2,1,0:T(1,128)S(1)} %add.50.r_ref, f32[64,256]{1,0:T(8,128)S(1)} %dynamic-slice_bitcast_fusion.1.w1_ref, ...), custom_call_target="tpu_custom_call" | custom-call | tf_op jit(solution)/shard_map/pallas_call | solution.py:198
  37.8 0.1 pad_maximum_fusion.2
  37.9 8.4 %all_to_all.10 = bf16[16,16,128]{2,1,0:T(8,128)(2,1)S(1)} all-to-all(bf16[16,16,128]{2,1,0:T(8,128)(2,1)S(1)} %pad_maximum_fusion.2), channel_id=1, replica_groups={{0,8,16,24,1,9,17,25,2,10,18,26,3,11,19,27},{4,12,20,28,5,13,21,29,6,14..., dimensions={0} | all-to-all | bytes 131072 | tf_op jit(solution)/shard_map/all_to_all | solution.py:233
  46.3 0.2 reshape.78
  46.4 0.1 copy.22
  46.6 0.0 copy-start.3
  46.6 0.2 reshape.77
  46.8 0.6 %copy-done.3 = bf16[32,768]{1,0:T(8,128)(2,1)S(1)} copy-done((bf16[32,768]{1,0:T(8,128)(2,1)S(1)}, bf16[32,768]{1,0:T(8,128)(2,1)}, u32[]{:S(2)}) %copy-start.3) | copy-done | bytes 49176
  47.4 0.6 %multiply_convert_fusion = bf16[32,768]{1,0:T(8,128)(2,1)} fusion(f32[32,768]{1,0:T(8,128)S(1)} %reshape.77, bf16[32,768]{1,0:T(8,128)(2,1)S(1)} %copy-done.3), kind=kLoop, calls=%fused_computation.2 | loop fusion | flops 73728 | bytes 196608 | tf_op jit(solution)/shard_map/convert_element_type | solution.py:293
  (13 shorter events, 0.2 us)
Async XLA Ops:
  0.0 12.4 %copy-start = (f32[3,64,256]{2,1,0:T(8,128)S(1)}, f32[3,64,256]{2,1,0:T(8,128)}, u32[]{:S(2)}) copy-start(f32[3,64,256]{2,1,0:T(8,128)} %param.16) | copy-start | bytes 589828
  0.0 0.8 %copy-start.4 = (f32[128,3]{0,1:T(4,128)S(1)}, f32[128,3]{0,1:T(4,128)}, u32[]{:S(2)}) copy-start(f32[128,3]{0,1:T(4,128)} %param.15) | copy-start | bytes 4612
  0.8 1.0 %copy-start.1 = (bf16[32,768]{1,0:T(8,128)(2,1)S(1)}, bf16[32,768]{1,0:T(8,128)(2,1)}, u32[]{:S(2)}) copy-start(bf16[32,768]{1,0:T(8,128)(2,1)} %param.12) | copy-start | bytes 147460
  1.7 0.8 %copy-start.2 = (bf16[32,768]{1,0:T(8,128)(2,1)S(1)}, bf16[32,768]{1,0:T(8,128)(2,1)}, u32[]{:S(2)}) copy-start(bf16[32,768]{1,0:T(8,128)(2,1)} %param.13) | copy-start | bytes 147460
  4.0 13.7 %all-to-all-start = ((bf16[16,56,128]{2,1,0:T(8,128)(2,1)}), bf16[16,56,128]{2,1,0:T(8,128)(2,1)S(1)}, u32[]{:S(2)}, u32[]{:S(2)}) async-start(bf16[16,56,128]{2,1,0:T(8,128)(2,1)} %bitcast.8), calls=%async_computation | async-start | bytes 458752 | tf_op jit(solution)/shard_map/all_to_all | solution.py:233
  24.8 6.1 %collective-permute-start = (bf16[144,256]{1,0:T(8,128)(2,1)S(1)}, bf16[144,256]{1,0:T(8,128)(2,1)S(1)}, u32[]{:S(2)}, u32[]{:S(2)}) collective-permute-start(bf16[144,256]{1,0:T(8,128)(2,1)S(1)} %get-tuple-element.8), channel_id=1, source_target_pairs={{0,4},{1,5},{2,6},{3,7},{4,0},{5,1},{6,2},{7,3},{8,12},{9,13},{10,... | collective-permute-start | bytes 221192 | tf_op jit(solution)/shard_map/ppermute | solution.py:282
  46.6 0.8 %copy-start.3 = (bf16[32,768]{1,0:T(8,128)(2,1)S(1)}, bf16[32,768]{1,0:T(8,128)(2,1)}, u32[]{:S(2)}) copy-start(bf16[32,768]{1,0:T(8,128)(2,1)} %param.14) | copy-start | bytes 147460

commit v2 on v1

--- a/solution.py
+++ b/solution.py
@@ -56,32 +56,16 @@
     def place(step):
         return jnp.where(backward == 0, step, total - 1 - step)
 
-    def load_qk(step):
-        return qk_ref[pl.ds(pl.multiple_of(place(step) * MINI, MINI), MINI), :]
-
-    pre_one = None
-    qk = load_qk(first_step)
-    for local_step in range(steps):
-        step = first_step + local_step
-        spot = place(step)
-        value = v_ref[pl.ds(pl.multiple_of(spot * MINI, MINI), MINI), :].astype(f32)
-        rate = r_ref[spot]
-        query, key = qk[:, :D_HEAD], qk[:, D_HEAD:]
-        if local_step + 1 < steps:
-            qk = load_qk(step + 1)
-            next_key = qk[:, D_HEAD:]
-        else:
-            next_key = key
-        first_high = weight_one.astype(bf16)
-        first_low = (weight_one - first_high.astype(f32)).astype(bf16)
-        second_high = second_turned.astype(bf16)
-        probes = jnp.concatenate([next_key, query], axis=0)
-        plain = mm(
-            jnp.concatenate([probes, probes], axis=1),
-            jnp.concatenate([first_high, first_low], axis=0),
-        ) + bias_one
-        if pre_one is None:
-            pre_one = mm(key, first_high) + mm(key, first_low) + bias_one
+    places = [place(first_step + step) for step in range(steps)]
+    pairs = [qk_ref[pl.ds(pl.multiple_of(spot * MINI, MINI), MINI), :] for spot in places]
+    queries = [pair[:, :D_HEAD] for pair in pairs]
+    keys = [pair[:, D_HEAD:] for pair in pairs]
+    rates = [r_ref[spot] for spot in places]
+
+    def prepare(step):
+        key, rate = keys[step], rates[step]
+        value = v_ref[pl.ds(pl.multiple_of(places[step] * MINI, MINI), MINI), :].astype(f32)
+        probes = jnp.concatenate([keys[min(step + 1, steps - 1)], queries[step]], axis=0)
         attend = (mm_turned(probes, key) + 1.0) * rate
         mixer = jnp.concatenate(
             [
@@ -92,36 +76,60 @@
             ],
             axis=0,
         ).astype(bf16)
-        act, slope = gelu_and_slope(pre_one)
-        act_high = act.astype(bf16)
-        centred = mm_turned(act_high, second_high) + bias_two
         pull = gain * (shift - value + key.astype(f32))
+        return probes, mixer, pull, row_mean(pull), jnp.broadcast_to(rate, (MINI, MINI)).T
+
+    def later_weights(waiting):
+        _, dual_high, act_high, _, rate = waiting
+        return jnp.where(seen, 0.0, (mm_turned(dual_high, act_high) + 1.0) * rate).astype(bf16)
+
+    def finish(waiting, plain_two, bias_now, unseen):
+        spot, _, _, grad_two_high, _ = waiting
+        dual_two = plain_two + bias_now + mm(unseen, grad_two_high)
+        emit(spot, gain * (dual_two * lax.rsqrt(row_mean(dual_two * dual_two) + eps_norm)) + shift)
+
+    ready = prepare(0)
+    first_high = weight_one.astype(bf16)
+    first_low = (weight_one - first_high.astype(f32)).astype(bf16)
+    act, slope = gelu_and_slope(mm(keys[0], first_high) + mm(keys[0], first_low) + bias_one)
+    act_high = act.astype(bf16)
+    waiting = None
+    for step in range(steps):
+        probes, mixer, pull, pull_mean, rate_column = ready
+        second_high = second_turned.astype(bf16)
+        stacked = act_high if waiting is None else jnp.concatenate([act_high, waiting[1]], axis=0)
+        passed = mm_turned(stacked, second_high)
+        centred = passed[:MINI] + bias_two
+        first_high = weight_one.astype(bf16)
+        first_low = (weight_one - first_high.astype(f32)).astype(bf16)
+        plain = mm(
+            jnp.concatenate([probes, probes], axis=1),
+            jnp.concatenate([first_high, first_low], axis=0),
+        ) + bias_one
+        if waiting is not None:
+            unseen = later_weights(waiting)
+        if step + 1 < steps:
+            ready = prepare(step + 1)
         scaled = gain_square * centred
         inverse = lax.rsqrt(row_mean(centred * centred) + eps_norm)
-        mean_a = inverse * row_mean(scaled) + row_mean(pull)
+        mean_a = inverse * row_mean(scaled) + pull_mean
         mean_an = inverse * (inverse * row_mean(scaled * centred) + row_mean(pull * centred))
         grad_two = inverse * ((gain_square - mean_an) * (inverse * centred) + (pull - mean_a))
         grad_two_high = grad_two.astype(bf16)
         grad_one = (mm(grad_two_high, second_high) * slope).astype(bf16)
+        if waiting is not None:
+            finish(waiting, passed[MINI:], bias_two, unseen)
+        weighted = grad_two * rate_column
+        second_turned = second_turned - mm(weighted.T.astype(bf16), act_high)
+        bias_two = bias_two - jnp.sum(weighted, axis=0, keepdims=True)
         mixed = mm(mixer, grad_one)
-        pre_one = plain[:MINI] - mixed[:MINI]
-        dual_act = gelu(plain[MINI:] - mixed[MINI : 2 * MINI])
-        dual_high = dual_act.astype(bf16)
-        dual_low = (dual_act - dual_high.astype(f32)).astype(bf16)
-        attend_two = jnp.where(seen, (mm_turned(dual_high, act_high) + 1.0) * rate, 0.0)
-        pulled = mm(
-            jnp.concatenate([attend_two, jnp.broadcast_to(rate, (16, MINI))], axis=0).astype(bf16),
-            grad_two_high,
-        )
-        dual_two = (
-            mm_turned(dual_high, second_high) + mm_turned(dual_low, second_high) + bias_two - pulled[:MINI]
-        )
-        spread = lax.rsqrt(row_mean(dual_two * dual_two) + eps_norm)
-        emit(spot, gain * (dual_two * spread) + shift)
+        dual_high = gelu(plain[MINI:] - mixed[MINI : 2 * MINI]).astype(bf16)
+        waiting = (places[step], dual_high, act_high, grad_two_high, rates[step])
+        act, slope = gelu_and_slope(plain[:MINI] - mixed[:MINI])
+        act_high = act.astype(bf16)
         weight_one = weight_one - mixed[2 * MINI : 3 * MINI]
         bias_one = bias_one - mixed[3 * MINI : 3 * MINI + 1]
-        second_turned = second_turned - mm((grad_two.T * rate).astype(bf16), act_high)
-        bias_two = bias_two - pulled[MINI : MINI + 1]
+    finish(waiting, mm_turned(waiting[1], second_turned.astype(bf16)), bias_two, later_weights(waiting))
     return weight_one, bias_one, second_turned, bias_two
 
 
@@ -191,6 +199,53 @@
         out_ref[spots, :] = (y_ref[spots, :] + rows).astype(bf16)
 
     run_phase(total, dir_ref[0], qk_ref, v_ref, r_ref, state_refs, gain_ref[...], shift_ref[...], emit)
+
+
+def pack_kernel(head_size, heads_local, query_hbm, key_hbm, value_hbm, rate_hbm, out_ref, query_ref, key_ref,
+                value_ref, rate_ref, arrived):
+    copies = [
+        pltpu.make_async_copy(source, target, arrived.at[at])
+        for at, (source, target) in enumerate(
+            [(rate_hbm, rate_ref), (query_hbm, query_ref), (key_hbm, key_ref), (value_hbm, value_ref)]
+        )
+    ]
+    for copy in copies:
+        copy.start()
+    for copy in copies:
+        copy.wait()
+    fold = query_ref.shape[0] // 2
+    row_at = lax.broadcasted_iota(jnp.int32, (8, rate_ref.shape[1]), 0)
+    for s in range(out_ref.shape[0] // head_size):
+        if s >= heads_local:
+            for h in range(head_size):
+                out_ref[s * head_size + h] = jnp.zeros(out_ref.shape[1:], bf16)
+            continue
+        rate = rate_ref[s : s + 1, :]
+        high = rate.astype(bf16).astype(f32)
+        middle = (rate - high).astype(bf16).astype(f32)
+        low = rate - high - middle
+        rate_rows = jnp.where(row_at == 0, high, jnp.where(row_at == 1, middle, jnp.where(row_at == 2, low, 0.0)))
+        for h in range(head_size):
+            at = (h * heads_local + s) * D_HEAD
+            value = value_ref[:, at : at + D_HEAD]
+            pair = jnp.concatenate([query_ref[:, at : at + D_HEAD], key_ref[:, at : at + D_HEAD]], axis=1)
+            folded = jnp.concatenate([value[:fold], value[fold:]], axis=1)
+            out_ref[s * head_size + h] = jnp.concatenate([pair, folded, rate_rows.astype(bf16)], axis=0)
+
+
+def join_kernel(head_size, heads_local, back_ref, gate_ref, out_ref):
+    fold = back_ref.shape[1]
+    for pair_at in range(head_size * heads_local // 2):
+        blocks = []
+        for head in (2 * pair_at, 2 * pair_at + 1):
+            blocks.append(back_ref[(head % heads_local) * head_size + head // heads_local])
+        columns = slice(pair_at * 2 * D_HEAD, (pair_at + 1) * 2 * D_HEAD)
+        for part in range(2):
+            lanes = slice(part * D_HEAD, (part + 1) * D_HEAD)
+            ttt = jnp.concatenate([blocks[0][:, lanes], blocks[1][:, lanes]], axis=1)
+            spots = slice(part * fold, (part + 1) * fold)
+            gated = gate_ref[spots, columns].astype(f32) * ttt.astype(f32)
+            out_ref[spots, columns] = gated.astype(bf16)
 
 
 def call_phase(kernel, total, outs, *operands):
@@ -210,27 +265,9 @@
     )(*operands)
 
 
-def local(head_size, seq_size, query_rows, key_rows, value_rows, gate_rows, step_rates, first_weight,
-          first_bias, second_weight, second_bias, norm_gain, norm_shift):
+def pack_plain(head_size, half_seq, query_rows, key_rows, value_rows, step_rates):
     rows_here = query_rows.shape[0]
-    heads_local = step_rates.shape[1]
-    token_block = step_rates.shape[0]
-    half_seq = seq_size // 2
-    group = half_seq * head_size
-    half_tokens = group * rows_here
-    total = half_tokens // MINI
-    spare = half_seq - heads_local
-    seq_at = lax.axis_index("seq")
-    half = seq_at // half_seq
-    slot = jnp.minimum(seq_at % half_seq, heads_local - 1)
-    group_at = lax.axis_index("head")
-    halves = [
-        [s * head_size + h for s in range(k * half_seq, (k + 1) * half_seq) for h in range(head_size)]
-        for k in range(2)
-    ]
-
-    def exchange(blocks):
-        return lax.all_to_all(blocks, ("seq", "head"), 0, 0, axis_index_groups=halves)
+    token_block, heads_local = step_rates.shape
 
     def by_slot(rows):
         return rows.reshape(rows_here, head_size, heads_local, D_HEAD).transpose(2, 1, 0, 3)
@@ -247,8 +284,51 @@
     rate_rows = jnp.concatenate([rate_rows, jnp.zeros((heads_local, 5, token_block), bf16)], axis=1)
     rate_rows = jnp.broadcast_to(rate_rows[:, None], (heads_local, head_size, 8, token_block))
     blocks = jnp.concatenate([pairs, folded, rate_rows], axis=2)
-    blocks = jnp.concatenate([blocks, jnp.zeros((spare,) + blocks.shape[1:], bf16)], axis=0)
-    got = exchange(blocks.reshape((group,) + blocks.shape[2:]))
+    spare = jnp.zeros((half_seq - heads_local,) + blocks.shape[1:], bf16)
+    blocks = jnp.concatenate([blocks, spare], axis=0)
+    return blocks.reshape((half_seq * head_size,) + blocks.shape[2:])
+
+
+def local(head_size, seq_size, query_rows, key_rows, value_rows, gate_rows, step_rates, first_weight,
+          first_bias, second_weight, second_bias, norm_gain, norm_shift):
+    rows_here = query_rows.shape[0]
+    heads_local = step_rates.shape[1]
+    token_block = step_rates.shape[0]
+    half_seq = seq_size // 2
+    group = half_seq * head_size
+    half_tokens = group * rows_here
+    total = half_tokens // MINI
+    seq_at = lax.axis_index("seq")
+    half = seq_at // half_seq
+    slot = jnp.minimum(seq_at % half_seq, heads_local - 1)
+    group_at = lax.axis_index("head")
+    halves = [
+        [s * head_size + h for s in range(k * half_seq, (k + 1) * half_seq) for h in range(head_size)]
+        for k in range(2)
+    ]
+
+    def exchange(blocks):
+        return lax.all_to_all(blocks, ("seq", "head"), 0, 0, axis_index_groups=halves)
+
+    block_rows = rows_here + rows_here // 2 + 8
+    kernels_fit = rows_here % 32 == 0 and token_block == 2 * D_HEAD and head_size * heads_local % 2 == 0
+    if kernels_fit:
+        blocks = pl.pallas_call(
+            functools.partial(pack_kernel, head_size, heads_local),
+            out_shape=jax.ShapeDtypeStruct((group, block_rows, 2 * D_HEAD), bf16),
+            in_specs=[pl.BlockSpec(memory_space=pltpu.HBM)] * 4,
+            scratch_shapes=[
+                pltpu.VMEM(query_rows.shape, bf16),
+                pltpu.VMEM(key_rows.shape, bf16),
+                pltpu.VMEM(value_rows.shape, bf16),
+                pltpu.VMEM((heads_local, token_block), f32),
+                pltpu.SemaphoreType.DMA((4,)),
+            ],
+            compiler_params=pltpu.CompilerParams(vmem_limit_bytes=60 * 2**20),
+        )(query_rows, key_rows, value_rows, step_rates.T)
+    else:
+        blocks = pack_plain(head_size, half_seq, query_rows, key_rows, value_rows, step_rates)
+    got = exchange(blocks)
 
     qk_all = got[:, :rows_here].reshape(half_tokens, 2 * D_HEAD)
     got_value = got[:, rows_here : rows_here + rows_here // 2]
@@ -288,6 +368,12 @@
     )
     summed = summed.reshape(group, 2, rows_here // 2, D_HEAD)
     back = exchange(jnp.concatenate([summed[:, 0], summed[:, 1]], axis=2))
+    if kernels_fit:
+        return pl.pallas_call(
+            functools.partial(join_kernel, head_size, heads_local),
+            out_shape=jax.ShapeDtypeStruct(gate_rows.shape, bf16),
+            compiler_params=pltpu.CompilerParams(vmem_limit_bytes=8 * 2**20),
+        )(back, gate_rows)
     back = back.reshape(half_seq, head_size, rows_here // 2, 2, D_HEAD)[:heads_local]
     back = back.transpose(3, 2, 1, 0, 4).reshape(rows_here, head_size * heads_local * D_HEAD)
     return (gate_rows.astype(f32) * back.astype(f32)).astype(bf16)

time: 48.5 us -> 40.8 us (0.84)
  local copies, waits for them, and re-layouts: 7.05 us -> 3.16 us
  Pallas kernels: 13.6 us -> 11.6 us
  other arithmetic: 1.92 us -> 0.14 us
    pallas_call x2, Pallas kernels: 13.6 us -> 9.21 us  [call_phase(): pl.pallas_call(functools.partial(kernel, total), out_shape=outs, in_specs...]
    pallas_call x0 -> x2, Pallas kernels: none -> 2.43 us  [the longest x1 1.73 us: local(): pl.pallas_call(functools.partial(pack_kernel, head_size, heads_local), ou...]
    unnamed x11 -> x4, local copies, waits for them, and re-layouts: 1.3 us -> 0.01 us
    reshape x3 -> x0, local copies, waits for them, and re-layouts: 1.25 us -> none  [by_slot(): rows.reshape(rows_here, head_size, heads_local, D_HEAD)]
    concatenate x2 -> x0, local copies, waits for them, and re-layouts: 0.79 us -> none  [the longest x1 0.71 us: local(): jnp.concatenate([blocks, jnp.zeros((spare,) + blocks.shape[1:], bf16)], a...]
    another operation x2 -> x0, other arithmetic: 0.76 us -> none  [local(): rate_rows = jnp.stack([high, middle, low], axis=1)]
    convert_element_type x2 -> x0, other arithmetic: 0.64 us -> none  [local(): return (gate_rows.astype(f32) * back.astype(f32)).astype(bf16)]
    convert_element_type x3 -> x0, local copies, waits for them, and re-layouts: 0.5 us -> none  [local(): return (gate_rows.astype(f32) * back.astype(f32)).astype(bf16)]
  transfers between devices with their start and end apart: 2 -> 2, of which waited for: 2 -> 2; matrix products, arithmetic and copies ran while one was open for 6% -> 7% of each run, Pallas kernels for 0% -> 0%
where the time goes in v2:
time: 40.8 us; the launch traced here: 40.4 us
  Pallas kernels  11.6 us (28%)
  starting transfers between devices  8.95 us (22%)
  blocking collectives  8.54 us (21%)
  waiting for transfers between devices  7.86 us (19%)
  local copies, waits for them, and re-layouts  3.16 us (8%)
    pallas_call x2, Pallas kernels, call_phase(): pl.pallas_call(functools.partial(kernel, total), out_shape=outs, in_specs...  9.21 us
    all_to_all x1, blocking collectives, exchange(): lax.all_to_all(blocks, ('seq', 'head'), 0, 0, axis_index_groups=halves)  8.54 us
    all_to_all x1, starting transfers between devices, exchange(): lax.all_to_all(blocks, ('seq', 'head'), 0, 0, axis_index_groups=halves)  6.3 us
    all_to_all x1, waiting for transfers between devices, exchange(): lax.all_to_all(blocks, ('seq', 'head'), 0, 0, axis_index_groups=halves)  4.41 us
    ppermute x1, waiting for transfers between devices, local(): delta = lax.ppermute(delta, 'seq', route)  3.45 us
    ppermute x1, starting transfers between devices, local(): delta = lax.ppermute(delta, 'seq', route)  2.65 us
    dynamic_slice x3, local copies, waits for them, and re-layouts, pick(): return lax.dynamic_index_in_dim(array_in, slot, 0, keepdims=False)  2.08 us
    pallas_call x1, Pallas kernels, local(): pl.pallas_call(functools.partial(pack_kernel, head_size, heads_local), ou...  1.73 us
  transfers between devices with their start and end apart: 2, of which 2 were waited for; matrix products, arithmetic and copies ran while one was open for 7% of the time, Pallas kernels for 0%

profile of v2, /device:TPU:0, one launch (start us, length us, event | category | flops | bytes accessed | tf_op | source)
XLA Modules:
  0.0 40.4 jit_solution(17350909566446060562)
XLA Ops:
  0.0 0.0 copy-start
  0.0 1.7 %shard_map.109 = bf16[16,56,128]{2,1,0:T(8,128)(2,1)} custom-call(bf16[32,768]{1,0:T(8,128)(2,1)} %query_hbm.1, bf16[32,768]{1,0:T(8,128)(2,1)} %key_hbm.1, bf16[32,768]{1,0:T(8,128)(2,1)} %value_hbm.1, f32[3,128]{1,0:T(4,128)} %bitcast.37), custom_call_target="tpu_custom_call" | custom-call | tf_op jit(solution)/shard_map/pallas_call | solution.py:316
  1.7 6.3 %all-to-all-start = ((bf16[16,56,128]{2,1,0:T(8,128)(2,1)}), bf16[16,56,128]{2,1,0:T(8,128)(2,1)S(1)}, u32[]{:S(2)}, u32[]{:S(2)}) async-start(bf16[16,56,128]{2,1,0:T(8,128)(2,1)} %shard_map.109), calls=%async_computation | async-start | bytes 458752 | tf_op jit(solution)/shard_map/all_to_all | solution.py:311
  8.1 0.7 %constant_dynamic-slice_fusion.3.c1_ref = f32[1,256]{1,0:T(1,128)S(1)} fusion(f32[3,256]{1,0:T(4,128)} %param.17, s32[]{:T(128)S(6)} %select_n.30), kind=kLoop, calls=%fused_computation.15 | loop fusion | bytes 2052 | tf_op jit(solution)/shard_map/jit(dynamic_index_in_dim)/dynamic_slice | solution.py:341
  8.8 0.7 %constant_dynamic-slice_fusion.2.c2_ref = f32[1,64]{1,0:T(1,128)S(1)} fusion(f32[3,64]{1,0:T(4,128)} %param.19, s32[]{:T(128)S(6)} %select_n.30), kind=kLoop, calls=%fused_computation.14 | loop fusion | bytes 516 | tf_op jit(solution)/shard_map/jit(dynamic_index_in_dim)/dynamic_slice | solution.py:341
  9.5 0.7 %constant_dynamic-slice_fusion = (f32[1,64]{1,0:T(1,128)S(1)}, f32[1,64]{1,0:T(1,128)S(1)}) fusion(f32[3,64]{1,0:T(4,128)} %param.21, s32[]{:T(128)S(6)} %select_n.30, f32[3,64]{1,0:T(4,128)} %param.20), kind=kLoop, calls=%fused_computation.12 | loop fusion | bytes 1028 | tf_op jit(solution)/shard_map/jit(dynamic_index_in_dim)/dynamic_slice | solution.py:341
  10.2 0.0 copy-done
  10.2 0.9 %dynamic-slice_bitcast_fusion.w2t_ref = f32[64,256]{1,0:T(8,128)S(1)} fusion(f32[3,256,64]{1,2,0:T(8,128)} %param.18, s32[]{:T(128)S(6)} %select_n.30), kind=kLoop, calls=%fused_computation.6 | loop fusion | bytes 131076 | tf_op jit(solution)/shard_map/transpose | solution.py:346
  11.0 4.4 %all-to-all-done = bf16[16,56,128]{2,1,0:T(8,128)(2,1)S(1)} async-done(((bf16[16,56,128]{2,1,0:T(8,128)(2,1)}), bf16[16,56,128]{2,1,0:T(8,128)(2,1)S(1)}, u32[]{:S(2)}, u32[]{:S(2)}) %all-to-all-start) | async-done | bytes 229408 | tf_op jit(solution)/shard_map/all_to_all | solution.py:311
  15.5 0.1 add.48.r_ref
  15.5 0.1 slice_bitcast_fusion.3
  15.7 4.6 %shard_map.110 = (f32[512,64]{1,0:T(8,128)S(1)}, bf16[144,256]{1,0:T(8,128)(2,1)S(1)}) custom-call(s32[1]{0:T(128)} %bitcast.dir_ref, bf16[512,128]{1,0:T(8,128)(2,1)S(1)} %bitcast.33, bf16[512,64]{1,0:T(8,128)(2,1)S(1)} %bitcast.31, f32[8,1,64]{2,1,0:T(1,128)S(1)} %add.48.r_ref, f32[64,256]{1,0:T(8,128)S(1)} %dynamic-slice_bitcast_fusion.1.w1_ref, ...), custom_call_target="tpu_custom_call" | custom-call | tf_op jit(solution)/shard_map/pallas_call | solution.py:253
  20.3 2.6 %collective-permute-start = (bf16[144,256]{1,0:T(8,128)(2,1)S(1)}, bf16[144,256]{1,0:T(8,128)(2,1)S(1)}, u32[]{:S(2)}, u32[]{:S(2)}) collective-permute-start(bf16[144,256]{1,0:T(8,128)(2,1)S(1)} %get-tuple-element.8), channel_id=1, source_target_pairs={{0,4},{1,5},{2,6},{3,7},{4,0},{5,1},{6,2},{7,3},{8,12},{9,13},{10,... | collective-permute-start | bytes 221192 | tf_op jit(solution)/shard_map/ppermute | solution.py:362
  23.0 3.5 %collective-permute-done.delta_ref = bf16[144,256]{1,0:T(8,128)(2,1)S(1)} collective-permute-done((bf16[144,256]{1,0:T(8,128)(2,1)S(1)}, bf16[144,256]{1,0:T(8,128)(2,1)S(1)}, u32[]{:S(2)}, u32[]{:S(2)}) %collective-permute-start) | collective-permute-done | bytes 73760 | tf_op jit(solution)/shard_map/ppermute | solution.py:362
  26.4 4.6 %shard_map.111 = bf16[512,64]{1,0:T(8,128)(2,1)S(1)} custom-call(s32[1]{0:T(128)S(6)} %sub.8.dir_ref, bf16[512,128]{1,0:T(8,128)(2,1)S(1)} %bitcast.34, bf16[512,64]{1,0:T(8,128)(2,1)S(1)} %bitcast.32, f32[8,1,64]{2,1,0:T(1,128)S(1)} %add.48.r_ref, f32[64,256]{1,0:T(8,128)S(1)} %dynamic-slice_bitcast_fusion.1.w1_ref, ...), custom_call_target="tpu_custom_call" | custom-call | tf_op jit(solution)/shard_map/pallas_call | solution.py:253
  31.1 0.1 pad_maximum_fusion.1
  31.2 0.0 copy-start.1
  31.2 8.5 %all_to_all.10.back_ref = bf16[16,16,128]{2,1,0:T(8,128)(2,1)S(1)} all-to-all(bf16[16,16,128]{2,1,0:T(8,128)(2,1)S(1)} %pad_maximum_fusion.1), channel_id=1, replica_groups={{0,8,16,24,1,9,17,25,2,10,18,26,3,11,19,27},{4,12,20,28,5,13,21,29,6,14..., dimensions={0} | all-to-all | bytes 131072 | tf_op jit(solution)/shard_map/all_to_all | solution.py:311
  39.7 0.0 copy-done.1
  39.7 0.7 %shard_map.112 = bf16[32,768]{1,0:T(8,128)(2,1)} custom-call(bf16[16,16,128]{2,1,0:T(8,128)(2,1)S(1)} %all_to_all.10.back_ref, bf16[32,768]{1,0:T(8,128)(2,1)S(1)} %copy-done.1), custom_call_target="tpu_custom_call" | custom-call | tf_op jit(solution)/shard_map/pallas_call | solution.py:372
  (9 shorter events, 0.1 us)
Async XLA Ops:
  0.0 10.2 %copy-start = (f32[3,64,256]{2,1,0:T(8,128)S(1)}, f32[3,64,256]{2,1,0:T(8,128)}, u32[]{:S(2)}) copy-start(f32[3,64,256]{2,1,0:T(8,128)} %param.16) | copy-start | bytes 589828
  1.7 13.7 %all-to-all-start = ((bf16[16,56,128]{2,1,0:T(8,128)(2,1)}), bf16[16,56,128]{2,1,0:T(8,128)(2,1)S(1)}, u32[]{:S(2)}, u32[]{:S(2)}) async-start(bf16[16,56,128]{2,1,0:T(8,128)(2,1)} %shard_map.109), calls=%async_computation | async-start | bytes 458752 | tf_op jit(solution)/shard_map/all_to_all | solution.py:311
  20.3 6.1 %collective-permute-start = (bf16[144,256]{1,0:T(8,128)(2,1)S(1)}, bf16[144,256]{1,0:T(8,128)(2,1)S(1)}, u32[]{:S(2)}, u32[]{:S(2)}) collective-permute-start(bf16[144,256]{1,0:T(8,128)(2,1)S(1)} %get-tuple-element.8), channel_id=1, source_target_pairs={{0,4},{1,5},{2,6},{3,7},{4,0},{5,1},{6,2},{7,3},{8,12},{9,13},{10,... | collective-permute-start | bytes 221192 | tf_op jit(solution)/shard_map/ppermute | solution.py:362
  31.2 8.6 %copy-start.1 = (bf16[32,768]{1,0:T(8,128)(2,1)S(1)}, bf16[32,768]{1,0:T(8,128)(2,1)}, u32[]{:S(2)}) copy-start(bf16[32,768]{1,0:T(8,128)(2,1)} %gate_ref.1) | copy-start | bytes 147460

commit v3 on v2

v3 whole, which is shorter than its diff:
```python
import functools

import jax
import jax.numpy as jnp
from jax import lax
from jax.experimental import pallas as pl
from jax.experimental.pallas import tpu as pltpu
from jax.sharding import PartitionSpec as P

D_HEAD = 64
INNER = 256
MINI = 64
CHUNK = 8

eps_norm = 1e-06
root_factor = 0.7978845608028654
cube_factor = 0.044715
f32 = jnp.float32
bf16 = jnp.bfloat16


def mm(left, right):
    return lax.dot_general(left, right, (((1,), (0,)), ((), ())), preferred_element_type=f32)


def mm_turned(left, right):
    return lax.dot_general(left, right, (((1,), (1,)), ((), ())), preferred_element_type=f32)


def gelu_and_slope(values):
    square = values * values
    tanh_term = jnp.tanh(values * (root_factor + root_factor * cube_factor * square))
    half = 0.5 + 0.5 * tanh_term
    act = values * half
    inner = root_factor + 3.0 * root_factor * cube_factor * square
    return act, half + act * (1.0 - tanh_term) * inner


def gelu(values):
    tanh_term = jnp.tanh(values * (root_factor + root_factor * cube_factor * (values * values)))
    return values * (0.5 + 0.5 * tanh_term)


def row_mean(values):
    return jnp.mean(values, axis=1, keepdims=True)


def tokens_of(first_step, steps, total, backward, qk_ref, v_ref, r_ref):
    lower = lax.broadcasted_iota(jnp.int32, (MINI, 2 * D_HEAD), 1) < D_HEAD
    places, pairs, queries, keys, values, rates = [], [], [], [], [], []
    for step in range(first_step, first_step + steps) if isinstance(first_step, int) else range(steps):
        at = step if isinstance(first_step, int) else first_step + step
        spot = jnp.where(backward == 0, at, total - 1 - at)
        spots = pl.ds(pl.multiple_of(spot * MINI, MINI), MINI)
        pair = qk_ref[spots, :]
        turned = jnp.concatenate([pair[:, D_HEAD:], pair[:, :D_HEAD]], axis=1)
        places.append(spot)
        pairs.append(pair)
        queries.append(jnp.where(lower, pair, turned))
        keys.append(jnp.where(lower, turned, pair))
        values.append(v_ref[spots, :])
        rates.append(r_ref[spot])
    return places, pairs, queries, keys, values, rates


def columns_of(gain, shift):
    both = jnp.concatenate([jnp.broadcast_to(gain, (MINI, D_HEAD)), jnp.broadcast_to(shift, (MINI, D_HEAD))], axis=1).T
    return both[:D_HEAD], both[D_HEAD:]


def order_of(backward, shape):
    ahead = lax.broadcasted_iota(jnp.int32, shape, 0) - lax.broadcasted_iota(jnp.int32, shape, 1)
    return jnp.where(backward == 0, ahead, -ahead)


def prepare(one, backward, tokens, gain, shift, columns):
    _, _, queries, keys, values, rates = tokens
    gain_column, shift_column = columns
    steps = len(keys)
    two = min(one + 1, steps - 1)
    lower = lax.broadcasted_iota(jnp.int32, (MINI, 2 * D_HEAD), 1) < D_HEAD
    none = jnp.zeros((MINI, 2 * D_HEAD), bf16)
    seen = order_of(backward, (MINI, MINI)) >= 0
    nexts = [keys[min(step + 1, steps - 1)] for step in (one, two)]
    probes = jnp.concatenate(
        [jnp.where(lower, nexts[0], nexts[1]), jnp.where(lower, queries[one], queries[two])], axis=0
    )
    met = jnp.concatenate([jnp.where(lower, keys[one], none), none, jnp.where(lower, none, keys[two]), none], axis=0)
    attend = mm_turned(probes, met) + 1.0
    made = []
    for at, step in enumerate((one, two)):
        rate = rates[step]
        here = attend[:, 2 * at * MINI : (2 * at + 1) * MINI] * rate
        value, key = values[step].astype(f32), keys[step].astype(f32)
        both = jnp.where(lower, jnp.concatenate([value, value], axis=1), key).T
        value_turned, key_turned = both[:D_HEAD], both[D_HEAD:]
        mixer = jnp.concatenate(
            [
                (-here[:MINI]).astype(bf16),
                jnp.where(seen, -here[MINI:], 0.0).astype(bf16),
                (key_turned * -rate).astype(bf16),
                jnp.broadcast_to(-rate, (16, MINI)).astype(bf16),
            ],
            axis=0,
        )
        plain = jnp.concatenate([nexts[at], queries[step], none, none[:16]], axis=0)
        pull = gain * (shift - value + key[:, :D_HEAD])
        pull_turned = gain_column * (shift_column - value_turned + key_turned)
        pull_row = jnp.mean(pull_turned, axis=0, keepdims=True)
        made.append((plain, mixer, pull, pull_turned, pull_row))
    return made


def finish(waiting, backward, gain, shift, emit):
    count = len(waiting)
    shape = (count * MINI, count * MINI)
    rows, columns = (lax.broadcasted_iota(jnp.int32, shape, dim) // MINI for dim in range(2))
    unseen = jnp.logical_and(rows == columns, order_of(backward, shape) < 0)
    dual, acts, weighted = (jnp.concatenate([one[at] for one in waiting], axis=0) for at in (1, 2, 3))
    hidden = mm(jnp.where(unseen, mm_turned(dual, acts) + 1.0, 0.0).astype(bf16), weighted)
    for at, one in enumerate(waiting):
        dual_two = one[4] + hidden[at * MINI : (at + 1) * MINI]
        spread = lax.rsqrt(row_mean(dual_two * dual_two) + eps_norm)
        emit(one[0], gain * (dual_two * spread) + shift)


def run_chunk(backward, tokens, state, gain, shift, emit, ready=None, keep_last=False):
    weight_one, bias_one, second_turned, bias_two = state
    places, pairs, queries, keys, values, rates = tokens
    steps = len(places)
    gain_square = gain * gain
    columns = columns_of(gain, shift)
    square_column = columns[0] * columns[0]
    blank = jnp.zeros((D_HEAD, INNER), bf16)
    first_high = weight_one.astype(bf16)
    first_low = (weight_one - first_high.astype(f32)).astype(bf16)
    act, slope = gelu_and_slope(
        mm(
            jnp.concatenate([pairs[0], pairs[0]], axis=1),
            jnp.concatenate([blank, first_high, blank, first_low], axis=0),
        )
        + bias_one
    )
    act_high = act.astype(bf16)
    bias_column = jnp.broadcast_to(bias_two, (MINI, D_HEAD)).T
    made = [] if ready is not None else prepare(0, backward, tokens, gain, shift, columns)
    waiting = []
    dual_high = None
    for step in range(steps):
        plain, mixer, pull, pull_turned, pull_row = made[step] if ready is None else ready(step)
        rate = rates[step]
        second_high = second_turned.astype(bf16)
        stacked = act_high if dual_high is None else jnp.concatenate([act_high, dual_high], axis=0)
        passed = mm_turned(stacked, second_high)
        if dual_high is not None:
            waiting[-1] = waiting[-1] + (passed[MINI:] + bias_two,)
        centred = passed[:MINI] + bias_two
        scaled = gain_square * centred
        back = mm(jnp.concatenate([part.astype(bf16) for part in (pull, centred, scaled)], axis=0), second_high)
        first_high = weight_one.astype(bf16)
        first_low = (weight_one - first_high.astype(f32)).astype(bf16)
        inverse = lax.rsqrt(row_mean(centred * centred) + eps_norm)
        mean_an = inverse * (inverse * row_mean(scaled * centred) + row_mean(pull * centred))
        grad_one = inverse * (inverse * (back[2 * MINI :] - mean_an * back[MINI : 2 * MINI]) + back[:MINI]) * slope
        grad_one = grad_one.astype(bf16)
        turned = mm_turned(second_high, act_high) + bias_column
        scaled_turned = square_column * turned
        inverse_row = lax.rsqrt(jnp.mean(turned * turned, axis=0, keepdims=True) + eps_norm)
        mean_a_row = inverse_row * jnp.mean(scaled_turned, axis=0, keepdims=True) + pull_row
        mean_an_row = inverse_row * (
            inverse_row * jnp.mean(scaled_turned * turned, axis=0, keepdims=True)
            + jnp.mean(pull_turned * turned, axis=0, keepdims=True)
        )
        weighted_turned = (rate * inverse_row) * (
            (square_column - mean_an_row) * (inverse_row * turned) + (pull_turned - mean_a_row)
        )
        second_turned = second_turned - mm(weighted_turned.astype(bf16), act_high)
        mixed = mm(
            jnp.concatenate([plain, mixer], axis=1), jnp.concatenate([first_high, first_low, grad_one], axis=0)
        )
        weighted = weighted_turned.T
        bias_column = bias_column - jnp.sum(weighted_turned, axis=1, keepdims=True)
        bias_two = bias_two - jnp.sum(weighted, axis=0, keepdims=True)
        if len(waiting) == 2:
            finish(waiting, backward, gain, shift, emit)
            waiting = []
        if ready is None and step % 2 == 0 and step + 2 < steps:
            made = made + prepare(step + 2, backward, tokens, gain, shift, columns)
        dual_high = gelu(mixed[MINI : 2 * MINI] + bias_one).astype(bf16)
        waiting.append((places[step], dual_high, act_high, weighted.astype(bf16)))
        act, slope = gelu_and_slope(mixed[:MINI] + bias_one)
        act_high = act.astype(bf16)
        weight_one = weight_one + mixed[2 * MINI : 3 * MINI]
        bias_one = bias_one + mixed[3 * MINI : 3 * MINI + 1]
    if not keep_last:
        waiting[-1] = waiting[-1] + (mm_turned(dual_high, second_turned.astype(bf16)) + bias_two,)
        finish(waiting, backward, gain, shift, emit)
    return (weight_one, bias_one, second_turned, bias_two), waiting


def run_chunks(total, backward, qk_ref, v_ref, r_ref, state_refs, gain, shift, emit):
    assert total % CHUNK == 0

    def body(index, carry):
        tokens = tokens_of(index * CHUNK, CHUNK, total, backward, qk_ref, v_ref, r_ref)
        state, _ = run_chunk(backward, tokens, tuple(ref[...] for ref in state_refs), gain, shift, emit)
        for ref, part in zip(state_refs, state):
            ref[...] = part
        return carry

    lax.fori_loop(0, total // CHUNK, body, 0)
    return tuple(ref[...] for ref in state_refs)


def centre_start(w1_ref, c1_ref, w2t_ref, c2_ref):
    second_turned = w2t_ref[...]
    second_turned = second_turned - jnp.mean(second_turned, axis=0, keepdims=True)
    bias_two = c2_ref[...] - row_mean(c2_ref[...])
    return w1_ref[...], c1_ref[...], second_turned, bias_two


def first_phase(total, dir_ref, qk_ref, v_ref, r_ref, w1_ref, c1_ref, w2t_ref, c2_ref, gain_ref, shift_ref, y_ref,
                delta_ref, *refs):
    backward = dir_ref[0]
    gain, shift = gain_ref[...], shift_ref[...]
    start = centre_start(w1_ref, c1_ref, w2t_ref, c2_ref)

    def emit(spot, rows):
        y_ref[pl.ds(pl.multiple_of(spot * MINI, MINI), MINI), :] = rows

    if total <= CHUNK:
        dual_ref, act_ref, weighted_ref, two_ref, second_ref, bias_ref = refs
        tokens = tokens_of(0, total, total, backward, qk_ref, v_ref, r_ref)
        end, waiting = run_chunk(backward, tokens, start, gain, shift, emit, keep_last=True)
        for at, one in enumerate(waiting):
            spots = slice(at * MINI, (at + 1) * MINI)
            dual_ref[spots, :], act_ref[spots, :], weighted_ref[spots, :] = one[1:4]
        two_ref[...] = waiting[0][4]
        second_ref[...] = end[2].astype(bf16)
        bias_ref[...] = end[3]
    else:
        for ref, part in zip(refs, start):
            ref[...] = part
        end = run_chunks(total, backward, qk_ref, v_ref, r_ref, refs, gain, shift, emit)
    start = centre_start(w1_ref, c1_ref, w2t_ref, c2_ref)
    ends = [part - first for part, first in zip(end, start)]
    delta_ref[0:D_HEAD, :] = ends[0].astype(bf16)
    delta_ref[D_HEAD : 2 * D_HEAD, :] = ends[2].astype(bf16)
    wide = jnp.concatenate([ends[3], jnp.zeros((1, INNER - D_HEAD), f32)], axis=1)
    delta_ref[2 * D_HEAD : 2 * D_HEAD + 16, :] = jnp.concatenate(
        [jnp.broadcast_to(ends[1], (8, INNER)), jnp.broadcast_to(wide, (8, INNER))], axis=0
    ).astype(bf16)


def between_phases(total, dir_ref, qk_ref, v_ref, r_ref, gain_ref, shift_ref, dual_ref, act_ref, weighted_ref, two_ref,
                   second_ref, bias_ref, tail_ref, plain_ref, mixer_ref, pull_ref, turned_ref, row_ref):
    gain, shift = gain_ref[...], shift_ref[...]
    backward = 1 - dir_ref[0]
    tokens = tokens_of(0, total, total, backward, qk_ref, v_ref, r_ref)
    columns = columns_of(gain, shift)
    for one in range(0, total, 2):
        for at, made in enumerate(prepare(one, backward, tokens, gain, shift, columns)):
            for ref, part in zip((plain_ref, mixer_ref, pull_ref, turned_ref, row_ref), made):
                ref[one + at] = part
    last_two = mm_turned(dual_ref[MINI:, :], second_ref[...]) + bias_ref[...]
    waiting = []
    for at, plain_two in enumerate((two_ref[...], last_two)):
        spots = slice(at * MINI, (at + 1) * MINI)
        waiting.append((at, dual_ref[spots, :], act_ref[spots, :], weighted_ref[spots, :], plain_two))

    def emit(at, rows):
        tail_ref[at * MINI : (at + 1) * MINI, :] = rows

    finish(waiting, dir_ref[0], gain, shift, emit)


def second_phase(total, dir_ref, qk_ref, v_ref, r_ref, w1_ref, c1_ref, w2t_ref, c2_ref, gain_ref, shift_ref, y_ref,
                 delta_ref, *refs):
    backward = 1 - dir_ref[0]
    gain, shift = gain_ref[...], shift_ref[...]
    biases = delta_ref[2 * D_HEAD : 2 * D_HEAD + 16, :].astype(f32)
    deltas = (
        delta_ref[0:D_HEAD, :].astype(f32),
        biases[0:1],
        delta_ref[D_HEAD : 2 * D_HEAD, :].astype(f32),
        biases[8:9, :D_HEAD],
    )
    start = centre_start(w1_ref, c1_ref, w2t_ref, c2_ref)
    state = tuple(part + delta for part, delta in zip(start, deltas))
    if total <= CHUNK:
        tail_ref, *ready_refs, out_ref = refs
        tokens = tokens_of(0, total, total, backward, qk_ref, v_ref, r_ref)
        done = []

        def emit(spot, rows):
            spots = pl.ds(pl.multiple_of(spot * MINI, MINI), MINI)
            step = len(done)
            done.append(step)
            if step < 2:
                first = tail_ref[(1 - step) * MINI : (2 - step) * MINI, :]
            else:
                first = y_ref[spots, :]
            out_ref[spots, :] = (first + rows).astype(bf16)

        def ready(step):
            return tuple(ref[step] for ref in ready_refs)

        run_chunk(backward, tokens, state, gain, shift, emit, ready)
    else:
        out_ref, *state_refs = refs
        for ref, part in zip(state_refs, state):
            ref[...] = part

        def emit(spot, rows):
            spots = pl.ds(pl.multiple_of(spot * MINI, MINI), MINI)
            out_ref[spots, :] = (y_ref[spots, :] + rows).astype(bf16)

        run_chunks(total, backward, qk_ref, v_ref, r_ref, state_refs, gain, shift, emit)


def pack_kernel(head_size, heads_local, query_hbm, key_hbm, value_hbm, rate_hbm, out_hbm, query_ref, key_ref,
                value_ref, rate_ref, block_ref, arrived, left):
    copies = [
        pltpu.make_async_copy(source, target, arrived.at[at])
        for at, (source, target) in enumerate(
            [(query_hbm, query_ref), (key_hbm, key_ref), (value_hbm, value_ref), (rate_hbm, rate_ref)]
        )
    ]
    for copy in copies:
        copy.start()
    leaving = []

    def leave(s):
        blocks = pl.ds(s * head_size, head_size)
        leaving.append(pltpu.make_async_copy(block_ref.at[blocks], out_hbm.at[blocks], left.at[s]))
        leaving[-1].start()

    for s in range(heads_local, out_hbm.shape[0] // head_size):
        for h in range(head_size):
            block_ref[s * head_size + h] = jnp.zeros(out_hbm.shape[1:], bf16)
        leave(s)
    for copy in copies:
        copy.wait()
    fold = query_ref.shape[0] // 2
    row_at = lax.broadcasted_iota(jnp.int32, (8, rate_ref.shape[1]), 0)
    for s in range(heads_local):
        rate = rate_ref[s : s + 1, :]
        high = rate.astype(bf16).astype(f32)
        middle = (rate - high).astype(bf16).astype(f32)
        low = rate - high - middle
        rate_rows = jnp.where(row_at == 0, high, jnp.where(row_at == 1, middle, jnp.where(row_at == 2, low, 0.0)))
        for h in range(head_size):
            at = (h * heads_local + s) * D_HEAD
            value = value_ref[:, at : at + D_HEAD]
            pair = jnp.concatenate([query_ref[:, at : at + D_HEAD], key_ref[:, at : at + D_HEAD]], axis=1)
            folded = jnp.concatenate([value[:fold], value[fold:]], axis=1)
            block_ref[s * head_size + h] = jnp.concatenate([pair, folded, rate_rows.astype(bf16)], axis=0)
        leave(s)
    for copy in leaving:
        copy.wait()


def join_kernel(head_size, heads_local, back_ref, gate_ref, out_ref):
    fold = back_ref.shape[1]
    for pair_at in range(head_size * heads_local // 2):
        blocks = []
        for head in (2 * pair_at, 2 * pair_at + 1):
            blocks.append(back_ref[(head % heads_local) * head_size + head // heads_local])
        columns = slice(pair_at * 2 * D_HEAD, (pair_at + 1) * 2 * D_HEAD)
        for part in range(2):
            lanes = slice(part * D_HEAD, (part + 1) * D_HEAD)
            ttt = jnp.concatenate([blocks[0][:, lanes], blocks[1][:, lanes]], axis=1)
            spots = slice(part * fold, (part + 1) * fold)
            gated = gate_ref[spots, columns].astype(f32) * ttt.astype(f32)
            out_ref[spots, columns] = gated.astype(bf16)


def call_phase(kernel, outs, keeps_state, *operands):
    in_vmem = pl.BlockSpec(memory_space=pltpu.VMEM)
    state = [(D_HEAD, INNER), (1, INNER), (D_HEAD, INNER), (1, D_HEAD)] if keeps_state else []
    return pl.pallas_call(
        kernel,
        out_shape=outs,
        in_specs=[pl.BlockSpec(memory_space=pltpu.SMEM)] + [in_vmem] * (len(operands) - 1),
        out_specs=[in_vmem] * len(outs),
        scratch_shapes=[pltpu.VMEM(shape, f32) for shape in state],
        compiler_params=pltpu.CompilerParams(vmem_limit_bytes=24 * 2**20),
        cost_estimate=pl.CostEstimate(flops=10**8, bytes_accessed=10**6, transcendentals=10**5),
    )(*operands)


def pack_plain(head_size, half_seq, query_rows, key_rows, value_rows, step_rates):
    rows_here = query_rows.shape[0]
    token_block, heads_local = step_rates.shape

    def by_slot(rows):
        return rows.reshape(rows_here, head_size, heads_local, D_HEAD).transpose(2, 1, 0, 3)

    query, key, value = by_slot(query_rows), by_slot(key_rows), by_slot(value_rows)
    pairs = jnp.concatenate([query, key], axis=3)
    folded = jnp.concatenate([value[:, :, : rows_here // 2], value[:, :, rows_here // 2 :]], axis=3)
    rates = step_rates.T
    high = rates.astype(bf16)
    rest = rates - high.astype(f32)
    middle = rest.astype(bf16)
    low = (rest - middle.astype(f32)).astype(bf16)
    rate_rows = jnp.stack([high, middle, low], axis=1)
    rate_rows = jnp.concatenate([rate_rows, jnp.zeros((heads_local, 5, token_block), bf16)], axis=1)
    rate_rows = jnp.broadcast_to(rate_rows[:, None], (heads_local, head_size, 8, token_block))
    blocks = jnp.concatenate([pairs, folded, rate_rows], axis=2)
    spare = jnp.zeros((half_seq - heads_local,) + blocks.shape[1:], bf16)
    blocks = jnp.concatenate([blocks, spare], axis=0)
    return blocks.reshape((half_seq * head_size,) + blocks.shape[2:])


def local(head_size, seq_size, query_rows, key_rows, value_rows, gate_rows, step_rates, first_weight,
          first_bias, second_weight, second_bias, norm_gain, norm_shift):
    rows_here = query_rows.shape[0]
    heads_local = step_rates.shape[1]
    token_block = step_rates.shape[0]
    half_seq = seq_size // 2
    group = half_seq * head_size
    half_tokens = group * rows_here
    total = half_tokens // MINI
    seq_at = lax.axis_index("seq")
    half = seq_at // half_seq
    slot = jnp.minimum(seq_at % half_seq, heads_local - 1)
    group_at = lax.axis_index("head")
    halves = [
        [s * head_size + h for s in range(k * half_seq, (k + 1) * half_seq) for h in range(head_size)]
        for k in range(2)
    ]

    def exchange(blocks):
        return lax.all_to_all(blocks, ("seq", "head"), 0, 0, axis_index_groups=halves)

    block_rows = rows_here + rows_here // 2 + 8
    kernels_fit = rows_here % 32 == 0 and token_block == 2 * D_HEAD and head_size * heads_local % 2 == 0
    if kernels_fit:
        blocks = pl.pallas_call(
            functools.partial(pack_kernel, head_size, heads_local),
            out_shape=jax.ShapeDtypeStruct((group, block_rows, 2 * D_HEAD), bf16),
            in_specs=[pl.BlockSpec(memory_space=pltpu.HBM)] * 4,
            out_specs=pl.BlockSpec(memory_space=pltpu.HBM),
            scratch_shapes=[
                pltpu.VMEM(query_rows.shape, bf16),
                pltpu.VMEM(key_rows.shape, bf16),
                pltpu.VMEM(value_rows.shape, bf16),
                pltpu.VMEM((heads_local, token_block), f32),
                pltpu.VMEM((group, block_rows, 2 * D_HEAD), bf16),
                pltpu.SemaphoreType.DMA((4,)),
                pltpu.SemaphoreType.DMA((half_seq,)),
            ],
            compiler_params=pltpu.CompilerParams(vmem_limit_bytes=60 * 2**20),
        )(query_rows, key_rows, value_rows, step_rates.T)
    else:
        blocks = pack_plain(head_size, half_seq, query_rows, key_rows, value_rows, step_rates)
    got = exchange(blocks)

    qk_all = got[:, :rows_here].reshape(half_tokens, 2 * D_HEAD)
    got_value = got[:, rows_here : rows_here + rows_here // 2]
    v_all = jnp.stack([got_value[..., :D_HEAD], got_value[..., D_HEAD:]], axis=1).reshape(half_tokens, D_HEAD)
    got_rate = got[:, rows_here + rows_here // 2 :].reshape(half_seq, head_size, 8, token_block)
    got_rate = lax.dynamic_index_in_dim(got_rate, group_at, 1, keepdims=False).astype(f32)
    r_all = (got_rate[:, 0] + got_rate[:, 1] + got_rate[:, 2]).reshape(total, 1, MINI)

    def pick(array_in):
        return lax.dynamic_index_in_dim(array_in, slot, 0, keepdims=False)

    params = (
        pick(first_weight),
        pick(first_bias)[None],
        pick(second_weight).T,
        pick(second_bias)[None],
        pick(norm_gain)[None],
        pick(norm_shift)[None],
    )
    ahead = half.astype(jnp.int32).reshape(1)
    short = total <= CHUNK
    shape = jax.ShapeDtypeStruct
    outs = [shape((half_tokens, D_HEAD), f32), shape((2 * D_HEAD + 16, INNER), bf16)]
    if short:
        outs += [
            shape((2 * MINI, INNER), bf16),
            shape((2 * MINI, INNER), bf16),
            shape((2 * MINI, D_HEAD), bf16),
            shape((MINI, D_HEAD), f32),
            shape((D_HEAD, INNER), bf16),
            shape((1, D_HEAD), f32),
        ]
    tokens = (ahead, qk_all, v_all, r_all)
    y_first, delta, *left = call_phase(functools.partial(first_phase, total), outs, not short, *tokens, *params)
    route = [(s, (s + half_seq) % seq_size) for s in range(seq_size)]
    delta = lax.ppermute(delta, "seq", route)
    extra = []
    if short:
        outs = [
            shape((2 * MINI, D_HEAD), f32),
            shape((total, 3 * MINI + 16, 2 * D_HEAD), bf16),
            shape((total, 3 * MINI + 16, D_HEAD), bf16),
            shape((total, MINI, D_HEAD), f32),
            shape((total, MINI, D_HEAD), f32),
            shape((total, 1, MINI), f32),
        ]
        extra = call_phase(functools.partial(between_phases, total), outs, False, *tokens, *params[4:], *left)
    (summed,) = call_phase(
        functools.partial(second_phase, total),
        [shape((half_tokens, D_HEAD), bf16)],
        not short, *tokens, *params, y_first, delta, *extra,
    )
    summed = summed.reshape(group, 2, rows_here // 2, D_HEAD)
    back = exchange(jnp.concatenate([summed[:, 0], summed[:, 1]], axis=2))
    if kernels_fit:
        return pl.pallas_call(
            functools.partial(join_kernel, head_size, heads_local),
            out_shape=jax.ShapeDtypeStruct(gate_rows.shape, bf16),
            compiler_params=pltpu.CompilerParams(vmem_limit_bytes=8 * 2**20),
        )(back, gate_rows)
    back = back.reshape(half_seq, head_size, rows_here // 2, 2, D_HEAD)[:heads_local]
    back = back.transpose(3, 2, 1, 0, 4).reshape(rows_here, head_size * heads_local * D_HEAD)
    return (gate_rows.astype(f32) * back.astype(f32)).astype(bf16)


def solution(mesh):
    tokens = P(("seq", "head"), None)
    in_specs = (
        tokens,
        tokens,
        tokens,
        tokens,
        P("seq", "head"),
        P("head", None, None),
        P("head", None),
        P("head", None, None),
        P("head", None),
        P("head", None),
        P("head", None),
    )
    body = functools.partial(local, mesh.shape["head"], mesh.shape["seq"])
    return jax.shard_map(body, mesh=mesh, in_specs=in_specs, out_specs=tokens, check_vma=False)
```

time: 40.8 us -> 39.3 us (0.963)
  Pallas kernels: 11.6 us -> 10.8 us
  waiting for transfers between devices: 7.86 us -> 7.2 us
    pallas_call x2 -> x3, Pallas kernels: 9.21 us -> 8.39 us  [call_phase(): pl.pallas_call(kernel, out_shape=outs, in_specs=[pl.BlockSpec(memory_spac...]
    ppermute x1, waiting for transfers between devices: 3.45 us -> 2.79 us  [local(): delta = lax.ppermute(delta, 'seq', route)]
  transfers between devices with their start and end apart: 2 -> 2, of which waited for: 2 -> 2; matrix products, arithmetic and copies ran while one was open for 7% -> 8% of each run, Pallas kernels for 0% -> 2%
where the time goes in v3:
time: 39.3 us; the launch traced here: 38.9 us
  Pallas kernels  10.8 us (27%)
  starting transfers between devices  8.96 us (23%)
  blocking collectives  8.54 us (22%)
  waiting for transfers between devices  7.2 us (18%)
  local copies, waits for them, and re-layouts  3.16 us (8%)
    all_to_all x1, blocking collectives, exchange(): lax.all_to_all(blocks, ('seq', 'head'), 0, 0, axis_index_groups=halves)  8.54 us
    pallas_call x3, Pallas kernels, call_phase(): pl.pallas_call(kernel, out_shape=outs, in_specs=[pl.BlockSpec(memory_spac...  8.39 us
    all_to_all x1, starting transfers between devices, exchange(): lax.all_to_all(blocks, ('seq', 'head'), 0, 0, axis_index_groups=halves)  6.3 us
    all_to_all x1, waiting for transfers between devices, exchange(): lax.all_to_all(blocks, ('seq', 'head'), 0, 0, axis_index_groups=halves)  4.41 us
    ppermute x1, waiting for transfers between devices, local(): delta = lax.ppermute(delta, 'seq', route)  2.79 us
    ppermute x1, starting transfers between devices, local(): delta = lax.ppermute(delta, 'seq', route)  2.66 us
    dynamic_slice x3, local copies, waits for them, and re-layouts, pick(): return lax.dynamic_index_in_dim(array_in, slot, 0, keepdims=False)  2.08 us
    pallas_call x1, Pallas kernels, local(): pl.pallas_call(functools.partial(pack_kernel, head_size, heads_local), ou...  1.7 us
  transfers between devices with their start and end apart: 2, of which 2 were waited for; matrix products, arithmetic and copies ran while one was open for 8% of the time, Pallas kernels for 2%

profile of v3, /device:TPU:0, one launch (start us, length us, event | category | flops | bytes accessed | tf_op | source)
XLA Modules:
  0.0 38.9 jit_solution(10571810469713996994)
XLA Ops:
  0.0 0.0 copy-start
  0.0 1.7 %shard_map.109 = bf16[16,56,128]{2,1,0:T(8,128)(2,1)} custom-call(bf16[32,768]{1,0:T(8,128)(2,1)} %query_hbm.1, bf16[32,768]{1,0:T(8,128)(2,1)} %key_hbm.1, bf16[32,768]{1,0:T(8,128)(2,1)} %value_hbm.1, f32[3,128]{1,0:T(4,128)} %bitcast.39), custom_call_target="tpu_custom_call" | custom-call | tf_op jit(solution)/shard_map/pallas_call | solution.py:440
  1.7 6.3 %all-to-all-start = ((bf16[16,56,128]{2,1,0:T(8,128)(2,1)}), bf16[16,56,128]{2,1,0:T(8,128)(2,1)S(1)}, u32[]{:S(2)}, u32[]{:S(2)}) async-start(bf16[16,56,128]{2,1,0:T(8,128)(2,1)} %shard_map.109), calls=%async_computation | async-start | bytes 458752 | tf_op jit(solution)/shard_map/all_to_all | solution.py:435
  8.0 0.7 %constant_dynamic-slice_fusion.3.c1_ref = f32[1,256]{1,0:T(1,128)S(1)} fusion(f32[3,256]{1,0:T(4,128)} %param.17, s32[]{:T(128)S(6)} %select_n.30), kind=kLoop, calls=%fused_computation.15 | loop fusion | bytes 2052 | tf_op jit(solution)/shard_map/jit(dynamic_index_in_dim)/dynamic_slice | solution.py:468
  8.7 0.7 %constant_dynamic-slice_fusion.2.c2_ref = f32[1,64]{1,0:T(1,128)S(1)} fusion(f32[3,64]{1,0:T(4,128)} %param.19, s32[]{:T(128)S(6)} %select_n.30), kind=kLoop, calls=%fused_computation.14 | loop fusion | bytes 516 | tf_op jit(solution)/shard_map/jit(dynamic_index_in_dim)/dynamic_slice | solution.py:468
  9.4 0.7 %constant_dynamic-slice_fusion = (f32[1,64]{1,0:T(1,128)S(1)}, f32[1,64]{1,0:T(1,128)S(1)}) fusion(f32[3,64]{1,0:T(4,128)} %param.21, s32[]{:T(128)S(6)} %select_n.30, f32[3,64]{1,0:T(4,128)} %param.20), kind=kLoop, calls=%fused_computation.12 | loop fusion | bytes 1028 | tf_op jit(solution)/shard_map/jit(dynamic_index_in_dim)/dynamic_slice | solution.py:468
  10.1 0.0 copy-done
  10.1 0.9 %dynamic-slice_bitcast_fusion.w2t_ref = f32[64,256]{1,0:T(8,128)S(1)} fusion(f32[3,256,64]{1,2,0:T(8,128)} %param.18, s32[]{:T(128)S(6)} %select_n.30), kind=kLoop, calls=%fused_computation.6 | loop fusion | bytes 131076 | tf_op jit(solution)/shard_map/transpose | solution.py:473
  11.0 4.4 %all-to-all-done = bf16[16,56,128]{2,1,0:T(8,128)(2,1)S(1)} async-done(((bf16[16,56,128]{2,1,0:T(8,128)(2,1)}), bf16[16,56,128]{2,1,0:T(8,128)(2,1)S(1)}, u32[]{:S(2)}, u32[]{:S(2)}) %all-to-all-start) | async-done | bytes 229408 | tf_op jit(solution)/shard_map/all_to_all | solution.py:435
  15.4 0.1 add.48.r_ref
  15.5 0.1 slice_bitcast_fusion.3
  15.7 3.8 %shard_map.110 = (f32[512,64]{1,0:T(8,128)S(1)}, bf16[144,256]{1,0:T(8,128)(2,1)S(1)}, bf16[128,256]{1,0:T(8,128)(2,1)S(1)}, bf16[128,256]{1,0:T(8,128)(2,1)S(1)...) custom-call(s32[1]{0:T(128)} %bitcast.dir_ref, ...), custom_call_target="tpu_custom_call" | custom-call | flops 100000000 | bytes 1000000 | tf_op jit(solution)/shard_map/pallas_call | solution.py:381
  19.4 2.7 %collective-permute-start = (bf16[144,256]{1,0:T(8,128)(2,1)S(1)}, bf16[144,256]{1,0:T(8,128)(2,1)S(1)}, u32[]{:S(2)}, u32[]{:S(2)}) collective-permute-start(bf16[144,256]{1,0:T(8,128)(2,1)S(1)} %get-tuple-element.20), channel_id=1, source_target_pairs={{0,4},{1,5},{2,6},{3,7},{4,0},{5,1},{6,2},{7,3},{8,12},{9,13},{10,... | collective-permute-start | bytes 221192 | tf_op jit(solution)/shard_map/ppermute | solution.py:494
  22.1 0.6 %shard_map.111 = (f32[128,64]{1,0:T(8,128)S(1)}, bf16[8,208,128]{2,1,0:T(8,128)(2,1)S(1)}, bf16[8,208,64]{2,1,0:T(8,128)(2,1)S(1)}, f32[8,64,64]{2,1,0:T(8,128)S...) custom-call(s32[1]{0:T(128)} %bitcast.dir_ref, bf16[512,128]{1,0:T(8,128)(2,1)S(1)} %bitcast.35, ...), custom_call_target="tpu_custom_call" | custom-call | flops 100000000 | bytes 1000000 | tf_op jit(solution)/shard_map/pallas_call | solution.py:381
  22.7 2.8 %collective-permute-done.delta_ref = bf16[144,256]{1,0:T(8,128)(2,1)S(1)} collective-permute-done((bf16[144,256]{1,0:T(8,128)(2,1)S(1)}, bf16[144,256]{1,0:T(8,128)(2,1)S(1)}, u32[]{:S(2)}, u32[]{:S(2)}) %collective-permute-start) | collective-permute-done | bytes 73760 | tf_op jit(solution)/shard_map/ppermute | solution.py:494
  25.5 4.0 %shard_map.112 = bf16[512,64]{1,0:T(8,128)(2,1)S(1)} custom-call(s32[1]{0:T(128)} %bitcast.dir_ref, bf16[512,128]{1,0:T(8,128)(2,1)S(1)} %bitcast.36, bf16[512,64]{1,0:T(8,128)(2,1)S(1)} %bitcast.33, f32[8,1,64]{2,1,0:T(1,128)S(1)} %add.48.r_ref, f32[64,256]{1,0:T(8,128)S(1)} %dynamic-slice_bitcast_fusion.1.w1_ref, ...), custom_call_target="tpu_custom_call" | custom-call | flops 100000000 | bytes 1000000 | tf_op jit(solution)/shard_map/pallas_call | solution.py:381
  29.6 0.1 pad_maximum_fusion.1
  29.7 0.0 copy-start.1
  29.7 8.5 %all_to_all.10.back_ref = bf16[16,16,128]{2,1,0:T(8,128)(2,1)S(1)} all-to-all(bf16[16,16,128]{2,1,0:T(8,128)(2,1)S(1)} %pad_maximum_fusion.1), channel_id=1, replica_groups={{0,8,16,24,1,9,17,25,2,10,18,26,3,11,19,27},{4,12,20,28,5,13,21,29,6,14..., dimensions={0} | all-to-all | bytes 131072 | tf_op jit(solution)/shard_map/all_to_all | solution.py:435
  38.2 0.0 copy-done.1
  38.2 0.7 %shard_map.113 = bf16[32,768]{1,0:T(8,128)(2,1)} custom-call(bf16[16,16,128]{2,1,0:T(8,128)(2,1)S(1)} %all_to_all.10.back_ref, bf16[32,768]{1,0:T(8,128)(2,1)S(1)} %copy-done.1), custom_call_target="tpu_custom_call" | custom-call | tf_op jit(solution)/shard_map/pallas_call | solution.py:514
  (9 shorter events, 0.1 us)
Async XLA Ops:
  0.0 10.1 %copy-start = (f32[3,64,256]{2,1,0:T(8,128)S(1)}, f32[3,64,256]{2,1,0:T(8,128)}, u32[]{:S(2)}) copy-start(f32[3,64,256]{2,1,0:T(8,128)} %param.16) | copy-start | bytes 589828
  1.7 13.7 %all-to-all-start = ((bf16[16,56,128]{2,1,0:T(8,128)(2,1)}), bf16[16,56,128]{2,1,0:T(8,128)(2,1)S(1)}, u32[]{:S(2)}, u32[]{:S(2)}) async-start(bf16[16,56,128]{2,1,0:T(8,128)(2,1)} %shard_map.109), calls=%async_computation | async-start | bytes 458752 | tf_op jit(solution)/shard_map/all_to_all | solution.py:435
  19.4 6.1 %collective-permute-start = (bf16[144,256]{1,0:T(8,128)(2,1)S(1)}, bf16[144,256]{1,0:T(8,128)(2,1)S(1)}, u32[]{:S(2)}, u32[]{:S(2)}) collective-permute-start(bf16[144,256]{1,0:T(8,128)(2,1)S(1)} %get-tuple-element.20), channel_id=1, source_target_pairs={{0,4},{1,5},{2,6},{3,7},{4,0},{5,1},{6,2},{7,3},{8,12},{9,13},{10,... | collective-permute-start | bytes 221192 | tf_op jit(solution)/shard_map/ppermute | solution.py:494
  29.7 8.6 %copy-start.1 = (bf16[32,768]{1,0:T(8,128)(2,1)S(1)}, bf16[32,768]{1,0:T(8,128)(2,1)}, u32[]{:S(2)}) copy-start(bf16[32,768]{1,0:T(8,128)(2,1)} %gate_ref.1) | copy-start | bytes 147460

commit v4 on v3

--- a/solution.py
+++ b/solution.py
@@ -111,17 +111,19 @@
     return made
 
 
-def finish(waiting, backward, gain, shift, emit):
+def finish(waiting, second_high, bias_two, backward, gain, shift, emit):
     count = len(waiting)
     shape = (count * MINI, count * MINI)
     rows, columns = (lax.broadcasted_iota(jnp.int32, shape, dim) // MINI for dim in range(2))
-    unseen = jnp.logical_and(rows == columns, order_of(backward, shape) < 0)
+    later = jnp.logical_and(rows == columns, order_of(backward, shape) < 0)
+    unseen = jnp.logical_or(rows < columns, later)
     dual, acts, weighted = (jnp.concatenate([one[at] for one in waiting], axis=0) for at in (1, 2, 3))
     hidden = mm(jnp.where(unseen, mm_turned(dual, acts) + 1.0, 0.0).astype(bf16), weighted)
+    dual_two = mm_turned(dual, second_high) + bias_two + hidden
+    spread = lax.rsqrt(row_mean(dual_two * dual_two) + eps_norm)
+    found = gain * (dual_two * spread) + shift
     for at, one in enumerate(waiting):
-        dual_two = one[4] + hidden[at * MINI : (at + 1) * MINI]
-        spread = lax.rsqrt(row_mean(dual_two * dual_two) + eps_norm)
-        emit(one[0], gain * (dual_two * spread) + shift)
+        emit(one[0], found[at * MINI : (at + 1) * MINI])
 
 
 def run_chunk(backward, tokens, state, gain, shift, emit, ready=None, keep_last=False):
@@ -145,25 +147,26 @@
     bias_column = jnp.broadcast_to(bias_two, (MINI, D_HEAD)).T
     made = [] if ready is not None else prepare(0, backward, tokens, gain, shift, columns)
     waiting = []
-    dual_high = None
     for step in range(steps):
         plain, mixer, pull, pull_turned, pull_row = made[step] if ready is None else ready(step)
         rate = rates[step]
         second_high = second_turned.astype(bf16)
-        stacked = act_high if dual_high is None else jnp.concatenate([act_high, dual_high], axis=0)
-        passed = mm_turned(stacked, second_high)
-        if dual_high is not None:
-            waiting[-1] = waiting[-1] + (passed[MINI:] + bias_two,)
-        centred = passed[:MINI] + bias_two
+        centred = mm_turned(act_high, second_high) + bias_two
+        turned = mm_turned(second_high, act_high) + bias_column
+        bias_before = bias_two
         scaled = gain_square * centred
-        back = mm(jnp.concatenate([part.astype(bf16) for part in (pull, centred, scaled)], axis=0), second_high)
+        both = [part.astype(bf16) for part in (centred, scaled)]
+        woven = [part[at : at + 16] for at in range(0, MINI, 16) for part in both]
+        back = mm(jnp.concatenate([pull.astype(bf16)] + woven, axis=0), second_high)
+        back_plain = jnp.concatenate([back[MINI + at : MINI + at + 16] for at in range(0, 2 * MINI, 32)], axis=0)
+        back_scaled = jnp.concatenate([back[MINI + at : MINI + at + 16] for at in range(16, 2 * MINI, 32)], axis=0)
         first_high = weight_one.astype(bf16)
         first_low = (weight_one - first_high.astype(f32)).astype(bf16)
         inverse = lax.rsqrt(row_mean(centred * centred) + eps_norm)
         mean_an = inverse * (inverse * row_mean(scaled * centred) + row_mean(pull * centred))
-        grad_one = inverse * (inverse * (back[2 * MINI :] - mean_an * back[MINI : 2 * MINI]) + back[:MINI]) * slope
+        front = inverse * slope
+        grad_one = (front * inverse) * (back_scaled - mean_an * back_plain) + front * back[:MINI]
         grad_one = grad_one.astype(bf16)
-        turned = mm_turned(second_high, act_high) + bias_column
         scaled_turned = square_column * turned
         inverse_row = lax.rsqrt(jnp.mean(turned * turned, axis=0, keepdims=True) + eps_norm)
         mean_a_row = inverse_row * jnp.mean(scaled_turned, axis=0, keepdims=True) + pull_row
@@ -182,7 +185,7 @@
         bias_column = bias_column - jnp.sum(weighted_turned, axis=1, keepdims=True)
         bias_two = bias_two - jnp.sum(weighted, axis=0, keepdims=True)
         if len(waiting) == 2:
-            finish(waiting, backward, gain, shift, emit)
+            finish(waiting, second_high, bias_before, backward, gain, shift, emit)
             waiting = []
         if ready is None and step % 2 == 0 and step + 2 < steps:
             made = made + prepare(step + 2, backward, tokens, gain, shift, columns)
@@ -193,8 +196,7 @@
         weight_one = weight_one + mixed[2 * MINI : 3 * MINI]
         bias_one = bias_one + mixed[3 * MINI : 3 * MINI + 1]
     if not keep_last:
-        waiting[-1] = waiting[-1] + (mm_turned(dual_high, second_turned.astype(bf16)) + bias_two,)
-        finish(waiting, backward, gain, shift, emit)
+        finish(waiting, second_turned.astype(bf16), bias_two, backward, gain, shift, emit)
     return (weight_one, bias_one, second_turned, bias_two), waiting
 
 
@@ -229,13 +231,12 @@
         y_ref[pl.ds(pl.multiple_of(spot * MINI, MINI), MINI), :] = rows
 
     if total <= CHUNK:
-        dual_ref, act_ref, weighted_ref, two_ref, second_ref, bias_ref = refs
+        dual_ref, act_ref, weighted_ref, second_ref, bias_ref = refs
         tokens = tokens_of(0, total, total, backward, qk_ref, v_ref, r_ref)
         end, waiting = run_chunk(backward, tokens, start, gain, shift, emit, keep_last=True)
         for at, one in enumerate(waiting):
             spots = slice(at * MINI, (at + 1) * MINI)
             dual_ref[spots, :], act_ref[spots, :], weighted_ref[spots, :] = one[1:4]
-        two_ref[...] = waiting[0][4]
         second_ref[...] = end[2].astype(bf16)
         bias_ref[...] = end[3]
     else:
@@ -252,7 +253,7 @@
     ).astype(bf16)
 
 
-def between_phases(total, dir_ref, qk_ref, v_ref, r_ref, gain_ref, shift_ref, dual_ref, act_ref, weighted_ref, two_ref,
+def between_phases(total, dir_ref, qk_ref, v_ref, r_ref, gain_ref, shift_ref, dual_ref, act_ref, weighted_ref,
                    second_ref, bias_ref, tail_ref, plain_ref, mixer_ref, pull_ref, turned_ref, row_ref):
     gain, shift = gain_ref[...], shift_ref[...]
     backward = 1 - dir_ref[0]
@@ -262,16 +263,15 @@
         for at, made in enumerate(prepare(one, backward, tokens, gain, shift, columns)):
             for ref, part in zip((plain_ref, mixer_ref, pull_ref, turned_ref, row_ref), made):
                 ref[one + at] = part
-    last_two = mm_turned(dual_ref[MINI:, :], second_ref[...]) + bias_ref[...]
     waiting = []
-    for at, plain_two in enumerate((two_ref[...], last_two)):
+    for at in range(2):
         spots = slice(at * MINI, (at + 1) * MINI)
-        waiting.append((at, dual_ref[spots, :], act_ref[spots, :], weighted_ref[spots, :], plain_two))
+        waiting.append((at, dual_ref[spots, :], act_ref[spots, :], weighted_ref[spots, :]))
 
     def emit(at, rows):
         tail_ref[at * MINI : (at + 1) * MINI, :] = rows
 
-    finish(waiting, dir_ref[0], gain, shift, emit)
+    finish(waiting, second_ref[...], bias_ref[...], dir_ref[0], gain, shift, emit)
 
 
 def second_phase(total, dir_ref, qk_ref, v_ref, r_ref, w1_ref, c1_ref, w2t_ref, c2_ref, gain_ref, shift_ref, y_ref,
@@ -484,7 +484,6 @@
             shape((2 * MINI, INNER), bf16),
             shape((2 * MINI, INNER), bf16),
             shape((2 * MINI, D_HEAD), bf16),
-            shape((MINI, D_HEAD), f32),
             shape((D_HEAD, INNER), bf16),
             shape((1, D_HEAD), f32),
         ]

time: 39.3 us -> 39 us (level)
  no operation moved by 1% of the time
where the time goes in v4:
time: 39 us; the launch traced here: 38.6 us
  Pallas kernels  10.5 us (27%)
  starting transfers between devices  8.95 us (23%)
  blocking collectives  8.54 us (22%)
  waiting for transfers between devices  7.21 us (18%)
  local copies, waits for them, and re-layouts  3.16 us (8%)
    all_to_all x1, blocking collectives, exchange(): lax.all_to_all(blocks, ('seq', 'head'), 0, 0, axis_index_groups=halves)  8.54 us
    pallas_call x3, Pallas kernels, call_phase(): pl.pallas_call(kernel, out_shape=outs, in_specs=[pl.BlockSpec(memory_spac...  8.1 us
    all_to_all x1, starting transfers between devices, exchange(): lax.all_to_all(blocks, ('seq', 'head'), 0, 0, axis_index_groups=halves)  6.3 us
    all_to_all x1, waiting for transfers between devices, exchange(): lax.all_to_all(blocks, ('seq', 'head'), 0, 0, axis_index_groups=halves)  4.41 us
    ppermute x1, waiting for transfers between devices, local(): delta = lax.ppermute(delta, 'seq', route)  2.8 us
    ppermute x1, starting transfers between devices, local(): delta = lax.ppermute(delta, 'seq', route)  2.66 us
    dynamic_slice x3, local copies, waits for them, and re-layouts, pick(): return lax.dynamic_index_in_dim(array_in, slot, 0, keepdims=False)  2.08 us
    pallas_call x1, Pallas kernels, local(): pl.pallas_call(functools.partial(pack_kernel, head_size, heads_local), ou...  1.7 us
  transfers between devices with their start and end apart: 2, of which 2 were waited for; matrix products, arithmetic and copies ran while one was open for 8% of the time, Pallas kernels for 2%

profile of v4, /device:TPU:0, one launch (start us, length us, event | category | flops | bytes accessed | tf_op | source)
XLA Modules:
  0.0 38.6 jit_solution(9382857469842853184)
XLA Ops:
  0.0 0.0 copy-start
  0.0 1.7 %shard_map.109 = bf16[16,56,128]{2,1,0:T(8,128)(2,1)} custom-call(bf16[32,768]{1,0:T(8,128)(2,1)} %query_hbm.1, bf16[32,768]{1,0:T(8,128)(2,1)} %key_hbm.1, bf16[32,768]{1,0:T(8,128)(2,1)} %value_hbm.1, f32[3,128]{1,0:T(4,128)} %bitcast.39), custom_call_target="tpu_custom_call" | custom-call | tf_op jit(solution)/shard_map/pallas_call | solution.py:440
  1.7 6.3 %all-to-all-start = ((bf16[16,56,128]{2,1,0:T(8,128)(2,1)}), bf16[16,56,128]{2,1,0:T(8,128)(2,1)S(1)}, u32[]{:S(2)}, u32[]{:S(2)}) async-start(bf16[16,56,128]{2,1,0:T(8,128)(2,1)} %shard_map.109), calls=%async_computation | async-start | bytes 458752 | tf_op jit(solution)/shard_map/all_to_all | solution.py:435
  8.0 0.7 %constant_dynamic-slice_fusion.3.c1_ref = f32[1,256]{1,0:T(1,128)S(1)} fusion(f32[3,256]{1,0:T(4,128)} %param.17, s32[]{:T(128)S(6)} %select_n.30), kind=kLoop, calls=%fused_computation.15 | loop fusion | bytes 2052 | tf_op jit(solution)/shard_map/jit(dynamic_index_in_dim)/dynamic_slice | solution.py:468
  8.7 0.7 %constant_dynamic-slice_fusion.2.c2_ref = f32[1,64]{1,0:T(1,128)S(1)} fusion(f32[3,64]{1,0:T(4,128)} %param.19, s32[]{:T(128)S(6)} %select_n.30), kind=kLoop, calls=%fused_computation.14 | loop fusion | bytes 516 | tf_op jit(solution)/shard_map/jit(dynamic_index_in_dim)/dynamic_slice | solution.py:468
  9.4 0.7 %constant_dynamic-slice_fusion = (f32[1,64]{1,0:T(1,128)S(1)}, f32[1,64]{1,0:T(1,128)S(1)}) fusion(f32[3,64]{1,0:T(4,128)} %param.21, s32[]{:T(128)S(6)} %select_n.30, f32[3,64]{1,0:T(4,128)} %param.20), kind=kLoop, calls=%fused_computation.12 | loop fusion | bytes 1028 | tf_op jit(solution)/shard_map/jit(dynamic_index_in_dim)/dynamic_slice | solution.py:468
  10.1 0.0 copy-done
  10.1 0.9 %dynamic-slice_bitcast_fusion.w2t_ref = f32[64,256]{1,0:T(8,128)S(1)} fusion(f32[3,256,64]{1,2,0:T(8,128)} %param.18, s32[]{:T(128)S(6)} %select_n.30), kind=kLoop, calls=%fused_computation.6 | loop fusion | bytes 131076 | tf_op jit(solution)/shard_map/transpose | solution.py:473
  11.0 4.4 %all-to-all-done = bf16[16,56,128]{2,1,0:T(8,128)(2,1)S(1)} async-done(((bf16[16,56,128]{2,1,0:T(8,128)(2,1)}), bf16[16,56,128]{2,1,0:T(8,128)(2,1)S(1)}, u32[]{:S(2)}, u32[]{:S(2)}) %all-to-all-start) | async-done | bytes 229408 | tf_op jit(solution)/shard_map/all_to_all | solution.py:435
  15.4 0.1 add.48.r_ref
  15.5 0.1 slice_bitcast_fusion.3
  15.7 3.6 %shard_map.110 = (f32[512,64]{1,0:T(8,128)S(1)}, bf16[144,256]{1,0:T(8,128)(2,1)S(1)}, bf16[128,256]{1,0:T(8,128)(2,1)S(1)}, bf16[128,256]{1,0:T(8,128)(2,1)S(1)...) custom-call(s32[1]{0:T(128)} %bitcast.dir_ref, bf16[512,128]{1,0:T(8,128)(2,1)S(1)} %bitcast.34, ...), custom_call_target="tpu_custom_call" | custom-call | flops 100000000 | bytes 1000000 | tf_op jit(solution)/shard_map/pallas_call | solution.py:381
  19.3 2.7 %collective-permute-start = (bf16[144,256]{1,0:T(8,128)(2,1)S(1)}, bf16[144,256]{1,0:T(8,128)(2,1)S(1)}, u32[]{:S(2)}, u32[]{:S(2)}) collective-permute-start(bf16[144,256]{1,0:T(8,128)(2,1)S(1)} %get-tuple-element.19), channel_id=1, source_target_pairs={{0,4},{1,5},{2,6},{3,7},{4,0},{5,1},{6,2},{7,3},{8,12},{9,13},{10,... | collective-permute-start | bytes 221192 | tf_op jit(solution)/shard_map/ppermute | solution.py:493
  21.9 0.6 %shard_map.111 = (f32[128,64]{1,0:T(8,128)S(1)}, bf16[8,208,128]{2,1,0:T(8,128)(2,1)S(1)}, bf16[8,208,64]{2,1,0:T(8,128)(2,1)S(1)}, f32[8,64,64]{2,1,0:T(8,128)S...) custom-call(s32[1]{0:T(128)} %bitcast.dir_ref, bf16[512,128]{1,0:T(8,128)(2,1)S(1)} %bitcast.35, ...), custom_call_target="tpu_custom_call" | custom-call | flops 100000000 | bytes 1000000 | tf_op jit(solution)/shard_map/pallas_call | solution.py:381
  22.6 2.8 %collective-permute-done.delta_ref = bf16[144,256]{1,0:T(8,128)(2,1)S(1)} collective-permute-done((bf16[144,256]{1,0:T(8,128)(2,1)S(1)}, bf16[144,256]{1,0:T(8,128)(2,1)S(1)}, u32[]{:S(2)}, u32[]{:S(2)}) %collective-permute-start) | collective-permute-done | bytes 73760 | tf_op jit(solution)/shard_map/ppermute | solution.py:493
  25.4 3.9 %shard_map.112 = bf16[512,64]{1,0:T(8,128)(2,1)S(1)} custom-call(s32[1]{0:T(128)} %bitcast.dir_ref, bf16[512,128]{1,0:T(8,128)(2,1)S(1)} %bitcast.36, bf16[512,64]{1,0:T(8,128)(2,1)S(1)} %bitcast.33, f32[8,1,64]{2,1,0:T(1,128)S(1)} %add.48.r_ref, f32[64,256]{1,0:T(8,128)S(1)} %dynamic-slice_bitcast_fusion.1.w1_ref, ...), custom_call_target="tpu_custom_call" | custom-call | flops 100000000 | bytes 1000000 | tf_op jit(solution)/shard_map/pallas_call | solution.py:381
  29.3 0.1 pad_maximum_fusion.1
  29.4 0.0 copy-start.1
  29.4 8.5 %all_to_all.10.back_ref = bf16[16,16,128]{2,1,0:T(8,128)(2,1)S(1)} all-to-all(bf16[16,16,128]{2,1,0:T(8,128)(2,1)S(1)} %pad_maximum_fusion.1), channel_id=1, replica_groups={{0,8,16,24,1,9,17,25,2,10,18,26,3,11,19,27},{4,12,20,28,5,13,21,29,6,14..., dimensions={0} | all-to-all | bytes 131072 | tf_op jit(solution)/shard_map/all_to_all | solution.py:435
  37.9 0.0 copy-done.1
  37.9 0.7 %shard_map.113 = bf16[32,768]{1,0:T(8,128)(2,1)} custom-call(bf16[16,16,128]{2,1,0:T(8,128)(2,1)S(1)} %all_to_all.10.back_ref, bf16[32,768]{1,0:T(8,128)(2,1)S(1)} %copy-done.1), custom_call_target="tpu_custom_call" | custom-call | tf_op jit(solution)/shard_map/pallas_call | solution.py:513
  (9 shorter events, 0.1 us)
Async XLA Ops:
  0.0 10.1 %copy-start = (f32[3,64,256]{2,1,0:T(8,128)S(1)}, f32[3,64,256]{2,1,0:T(8,128)}, u32[]{:S(2)}) copy-start(f32[3,64,256]{2,1,0:T(8,128)} %param.16) | copy-start | bytes 589828
  1.7 13.7 %all-to-all-start = ((bf16[16,56,128]{2,1,0:T(8,128)(2,1)}), bf16[16,56,128]{2,1,0:T(8,128)(2,1)S(1)}, u32[]{:S(2)}, u32[]{:S(2)}) async-start(bf16[16,56,128]{2,1,0:T(8,128)(2,1)} %shard_map.109), calls=%async_computation | async-start | bytes 458752 | tf_op jit(solution)/shard_map/all_to_all | solution.py:435
  19.3 6.1 %collective-permute-start = (bf16[144,256]{1,0:T(8,128)(2,1)S(1)}, bf16[144,256]{1,0:T(8,128)(2,1)S(1)}, u32[]{:S(2)}, u32[]{:S(2)}) collective-permute-start(bf16[144,256]{1,0:T(8,128)(2,1)S(1)} %get-tuple-element.19), channel_id=1, source_target_pairs={{0,4},{1,5},{2,6},{3,7},{4,0},{5,1},{6,2},{7,3},{8,12},{9,13},{10,... | collective-permute-start | bytes 221192 | tf_op jit(solution)/shard_map/ppermute | solution.py:493
  29.4 8.6 %copy-start.1 = (bf16[32,768]{1,0:T(8,128)(2,1)S(1)}, bf16[32,768]{1,0:T(8,128)(2,1)}, u32[]{:S(2)}) copy-start(bf16[32,768]{1,0:T(8,128)(2,1)} %gate_ref.1) | copy-start | bytes 147460

commit v5 on v4

--- a/solution.py
+++ b/solution.py
@@ -58,8 +58,20 @@
         pairs.append(pair)
         queries.append(jnp.where(lower, pair, turned))
         keys.append(jnp.where(lower, turned, pair))
-        values.append(v_ref[spots, :])
-        rates.append(r_ref[spot])
+        rate = r_ref[lax.div(spot, 2)]
+        rate_turned = jnp.concatenate([rate[:, MINI:], rate[:, :MINI]], axis=1)
+        rates.append(jnp.where(lax.rem(spot, 2) == 0, rate, rate_turned)[:, :MINI])
+        if v_ref is None:
+            continue
+        if len(v_ref.shape) == 2:
+            value = v_ref[spots, :]
+            values.append(jnp.concatenate([value, value], axis=1))
+            continue
+        halves = []
+        for block in range(MINI // (2 * v_ref.shape[1])):
+            folded = v_ref[spot * (MINI // (2 * v_ref.shape[1])) + block]
+            halves += [folded, jnp.concatenate([folded[:, D_HEAD:], folded[:, :D_HEAD]], axis=1)]
+        values.append(jnp.concatenate(halves, axis=0))
     return places, pairs, queries, keys, values, rates
 
 
@@ -92,7 +104,7 @@
         rate = rates[step]
         here = attend[:, 2 * at * MINI : (2 * at + 1) * MINI] * rate
         value, key = values[step].astype(f32), keys[step].astype(f32)
-        both = jnp.where(lower, jnp.concatenate([value, value], axis=1), key).T
+        both = jnp.where(lower, value, key).T
         value_turned, key_turned = both[:D_HEAD], both[D_HEAD:]
         mixer = jnp.concatenate(
             [
@@ -104,22 +116,26 @@
             axis=0,
         )
         plain = jnp.concatenate([nexts[at], queries[step], none, none[:16]], axis=0)
-        pull = gain * (shift - value + key[:, :D_HEAD])
+        pull = gain * (shift - value[:, :D_HEAD] + key[:, :D_HEAD])
         pull_turned = gain_column * (shift_column - value_turned + key_turned)
         pull_row = jnp.mean(pull_turned, axis=0, keepdims=True)
         made.append((plain, mixer, pull, pull_turned, pull_row))
     return made
 
 
-def finish(waiting, second_high, bias_two, backward, gain, shift, emit):
+def finish(waiting, second_turned, bias_two, backward, gain, shift, emit):
     count = len(waiting)
     shape = (count * MINI, count * MINI)
     rows, columns = (lax.broadcasted_iota(jnp.int32, shape, dim) // MINI for dim in range(2))
     later = jnp.logical_and(rows == columns, order_of(backward, shape) < 0)
     unseen = jnp.logical_or(rows < columns, later)
-    dual, acts, weighted = (jnp.concatenate([one[at] for one in waiting], axis=0) for at in (1, 2, 3))
+    dual, dual_low, acts, weighted = (jnp.concatenate([one[at] for one in waiting], axis=0) for at in (1, 2, 3, 4))
+    second_high = second_turned.astype(bf16)
     hidden = mm(jnp.where(unseen, mm_turned(dual, acts) + 1.0, 0.0).astype(bf16), weighted)
-    dual_two = mm_turned(dual, second_high) + bias_two + hidden
+    plain = mm_turned(jnp.concatenate([dual, dual_low], axis=0), second_high)
+    dual_two = plain[: count * MINI] + plain[count * MINI :] + bias_two + hidden
+    second_low = (second_turned - second_high.astype(f32)).astype(bf16)
+    dual_two = dual_two + mm_turned(dual, second_low)
     spread = lax.rsqrt(row_mean(dual_two * dual_two) + eps_norm)
     found = gain * (dual_two * spread) + shift
     for at, one in enumerate(waiting):
@@ -151,9 +167,11 @@
         plain, mixer, pull, pull_turned, pull_row = made[step] if ready is None else ready(step)
         rate = rates[step]
         second_high = second_turned.astype(bf16)
+        second_low = (second_turned - second_high.astype(f32)).astype(bf16)
         centred = mm_turned(act_high, second_high) + bias_two
-        turned = mm_turned(second_high, act_high) + bias_column
-        bias_before = bias_two
+        turned = mm_turned(jnp.concatenate([second_high, second_low], axis=0), act_high)
+        turned = turned[:D_HEAD] + turned[D_HEAD:] + bias_column
+        second_before, bias_before = second_turned, bias_two
         scaled = gain_square * centred
         both = [part.astype(bf16) for part in (centred, scaled)]
         woven = [part[at : at + 16] for at in range(0, MINI, 16) for part in both]
@@ -177,7 +195,10 @@
         weighted_turned = (rate * inverse_row) * (
             (square_column - mean_an_row) * (inverse_row * turned) + (pull_turned - mean_a_row)
         )
-        second_turned = second_turned - mm(weighted_turned.astype(bf16), act_high)
+        weighted_high = weighted_turned.astype(bf16)
+        weighted_low = (weighted_turned - weighted_high.astype(f32)).astype(bf16)
+        change = mm(jnp.concatenate([weighted_high, weighted_low], axis=0), act_high)
+        second_turned = second_turned - (change[:D_HEAD] + change[D_HEAD:])
         mixed = mm(
             jnp.concatenate([plain, mixer], axis=1), jnp.concatenate([first_high, first_low, grad_one], axis=0)
         )
@@ -185,18 +206,20 @@
         bias_column = bias_column - jnp.sum(weighted_turned, axis=1, keepdims=True)
         bias_two = bias_two - jnp.sum(weighted, axis=0, keepdims=True)
         if len(waiting) == 2:
-            finish(waiting, second_high, bias_before, backward, gain, shift, emit)
+            finish(waiting, second_before, bias_before, backward, gain, shift, emit)
             waiting = []
         if ready is None and step % 2 == 0 and step + 2 < steps:
             made = made + prepare(step + 2, backward, tokens, gain, shift, columns)
-        dual_high = gelu(mixed[MINI : 2 * MINI] + bias_one).astype(bf16)
-        waiting.append((places[step], dual_high, act_high, weighted.astype(bf16)))
+        dual = gelu(mixed[MINI : 2 * MINI] + bias_one)
+        dual_high = dual.astype(bf16)
+        dual_low = (dual - dual_high.astype(f32)).astype(bf16)
+        waiting.append((places[step], dual_high, dual_low, act_high, weighted.astype(bf16)))
         act, slope = gelu_and_slope(mixed[:MINI] + bias_one)
         act_high = act.astype(bf16)
         weight_one = weight_one + mixed[2 * MINI : 3 * MINI]
         bias_one = bias_one + mixed[3 * MINI : 3 * MINI + 1]
     if not keep_last:
-        finish(waiting, second_turned.astype(bf16), bias_two, backward, gain, shift, emit)
+        finish(waiting, second_turned, bias_two, backward, gain, shift, emit)
     return (weight_one, bias_one, second_turned, bias_two), waiting
 
 
@@ -231,13 +254,14 @@
         y_ref[pl.ds(pl.multiple_of(spot * MINI, MINI), MINI), :] = rows
 
     if total <= CHUNK:
-        dual_ref, act_ref, weighted_ref, second_ref, bias_ref = refs
+        *kept_refs, second_ref, bias_ref = refs
         tokens = tokens_of(0, total, total, backward, qk_ref, v_ref, r_ref)
         end, waiting = run_chunk(backward, tokens, start, gain, shift, emit, keep_last=True)
         for at, one in enumerate(waiting):
             spots = slice(at * MINI, (at + 1) * MINI)
-            dual_ref[spots, :], act_ref[spots, :], weighted_ref[spots, :] = one[1:4]
-        second_ref[...] = end[2].astype(bf16)
+            for ref, part in zip(kept_refs, one[1:]):
+                ref[spots, :] = part
+        second_ref[...] = end[2]
         bias_ref[...] = end[3]
     else:
         for ref, part in zip(refs, start):
@@ -253,7 +277,7 @@
     ).astype(bf16)
 
 
-def between_phases(total, dir_ref, qk_ref, v_ref, r_ref, gain_ref, shift_ref, dual_ref, act_ref, weighted_ref,
+def between_phases(total, dir_ref, qk_ref, v_ref, r_ref, gain_ref, shift_ref, dual_ref, low_ref, act_ref, weighted_ref,
                    second_ref, bias_ref, tail_ref, plain_ref, mixer_ref, pull_ref, turned_ref, row_ref):
     gain, shift = gain_ref[...], shift_ref[...]
     backward = 1 - dir_ref[0]
@@ -266,7 +290,8 @@
     waiting = []
     for at in range(2):
         spots = slice(at * MINI, (at + 1) * MINI)
-        waiting.append((at, dual_ref[spots, :], act_ref[spots, :], weighted_ref[spots, :]))
+        kept = (ref[spots, :] for ref in (dual_ref, low_ref, act_ref, weighted_ref))
+        waiting.append((at, *kept))
 
     def emit(at, rows):
         tail_ref[at * MINI : (at + 1) * MINI, :] = rows
@@ -274,7 +299,7 @@
     finish(waiting, second_ref[...], bias_ref[...], dir_ref[0], gain, shift, emit)
 
 
-def second_phase(total, dir_ref, qk_ref, v_ref, r_ref, w1_ref, c1_ref, w2t_ref, c2_ref, gain_ref, shift_ref, y_ref,
+def second_phase(total, fold, dir_ref, qk_ref, v_ref, r_ref, w1_ref, c1_ref, w2t_ref, c2_ref, gain_ref, shift_ref, y_ref,
                  delta_ref, *refs):
     backward = 1 - dir_ref[0]
     gain, shift = gain_ref[...], shift_ref[...]
@@ -289,7 +314,7 @@
     state = tuple(part + delta for part, delta in zip(start, deltas))
     if total <= CHUNK:
         tail_ref, *ready_refs, out_ref = refs
-        tokens = tokens_of(0, total, total, backward, qk_ref, v_ref, r_ref)
+        tokens = tokens_of(0, total, total, backward, qk_ref, None, r_ref)
         done = []
 
         def emit(spot, rows):
@@ -300,7 +325,14 @@
                 first = tail_ref[(1 - step) * MINI : (2 - step) * MINI, :]
             else:
                 first = y_ref[spots, :]
-            out_ref[spots, :] = (first + rows).astype(bf16)
+            summed = (first + rows).astype(bf16)
+            if fold is None:
+                out_ref[spots, :] = summed
+                return
+            for block in range(MINI // (2 * fold)):
+                at = block * 2 * fold
+                folded = jnp.concatenate([summed[at : at + fold], summed[at + fold : at + 2 * fold]], axis=1)
+                out_ref[spot * (MINI // (2 * fold)) + block] = folded
 
         def ready(step):
             return tuple(ref[step] for ref in ready_refs)
@@ -459,10 +491,14 @@
 
     qk_all = got[:, :rows_here].reshape(half_tokens, 2 * D_HEAD)
     got_value = got[:, rows_here : rows_here + rows_here // 2]
-    v_all = jnp.stack([got_value[..., :D_HEAD], got_value[..., D_HEAD:]], axis=1).reshape(half_tokens, D_HEAD)
+    short = total <= CHUNK
+    fold = rows_here // 2 if kernels_fit and short else None
+    v_all = got_value
+    if fold is None:
+        v_all = jnp.stack([got_value[..., :D_HEAD], got_value[..., D_HEAD:]], axis=1).reshape(half_tokens, D_HEAD)
     got_rate = got[:, rows_here + rows_here // 2 :].reshape(half_seq, head_size, 8, token_block)
     got_rate = lax.dynamic_index_in_dim(got_rate, group_at, 1, keepdims=False).astype(f32)
-    r_all = (got_rate[:, 0] + got_rate[:, 1] + got_rate[:, 2]).reshape(total, 1, MINI)
+    r_all = (got_rate[:, 0] + got_rate[:, 1] + got_rate[:, 2]).reshape(half_seq, 1, 2 * MINI)
 
     def pick(array_in):
         return lax.dynamic_index_in_dim(array_in, slot, 0, keepdims=False)
@@ -476,15 +512,15 @@
         pick(norm_shift)[None],
     )
     ahead = half.astype(jnp.int32).reshape(1)
-    short = total <= CHUNK
     shape = jax.ShapeDtypeStruct
     outs = [shape((half_tokens, D_HEAD), f32), shape((2 * D_HEAD + 16, INNER), bf16)]
     if short:
         outs += [
             shape((2 * MINI, INNER), bf16),
             shape((2 * MINI, INNER), bf16),
+            shape((2 * MINI, INNER), bf16),
             shape((2 * MINI, D_HEAD), bf16),
-            shape((D_HEAD, INNER), bf16),
+            shape((D_HEAD, INNER), f32),
             shape((1, D_HEAD), f32),
         ]
     tokens = (ahead, qk_all, v_all, r_all)
@@ -503,12 +539,14 @@
         ]
         extra = call_phase(functools.partial(between_phases, total), outs, False, *tokens, *params[4:], *left)
     (summed,) = call_phase(
-        functools.partial(second_phase, total),
-        [shape((half_tokens, D_HEAD), bf16)],
+        functools.partial(second_phase, total, fold),
+        [shape((half_tokens, D_HEAD) if fold is None else (group, fold, 2 * D_HEAD), bf16)],
         not short, *tokens, *params, y_first, delta, *extra,
     )
-    summed = summed.reshape(group, 2, rows_here // 2, D_HEAD)
-    back = exchange(jnp.concatenate([summed[:, 0], summed[:, 1]], axis=2))
+    if fold is None:
+        summed = summed.reshape(group, 2, rows_here // 2, D_HEAD)
+        summed = jnp.concatenate([summed[:, 0], summed[:, 1]], axis=2)
+    back = exchange(summed)
     if kernels_fit:
         return pl.pallas_call(
             functools.partial(join_kernel, head_size, heads_local),

time: 39 us -> 38.8 us (level)
  no operation moved by 1% of the time
where the time goes in v5:
time: 38.8 us; the launch traced here: 38.4 us
  Pallas kernels  10.7 us (28%)
  starting transfers between devices  8.96 us (23%)
  blocking collectives  8.53 us (22%)
  waiting for transfers between devices  7.14 us (18%)
  local copies, waits for them, and re-layouts  2.97 us (8%)
    all_to_all x1, blocking collectives, exchange(): lax.all_to_all(blocks, ('seq', 'head'), 0, 0, axis_index_groups=halves)  8.53 us
    pallas_call x3, Pallas kernels, call_phase(): pl.pallas_call(kernel, out_shape=outs, in_specs=[pl.BlockSpec(memory_spac...  8.33 us
    all_to_all x1, starting transfers between devices, exchange(): lax.all_to_all(blocks, ('seq', 'head'), 0, 0, axis_index_groups=halves)  6.3 us
    all_to_all x1, waiting for transfers between devices, exchange(): lax.all_to_all(blocks, ('seq', 'head'), 0, 0, axis_index_groups=halves)  4.41 us
    ppermute x1, waiting for transfers between devices, local(): delta = lax.ppermute(delta, 'seq', route)  2.73 us
    ppermute x1, starting transfers between devices, local(): delta = lax.ppermute(delta, 'seq', route)  2.66 us
    dynamic_slice x3, local copies, waits for them, and re-layouts, pick(): return lax.dynamic_index_in_dim(array_in, slot, 0, keepdims=False)  2.08 us
    pallas_call x1, Pallas kernels, local(): pl.pallas_call(functools.partial(pack_kernel, head_size, heads_local), ou...  1.7 us
  transfers between devices with their start and end apart: 2, of which 2 were waited for; matrix products, arithmetic and copies ran while one was open for 8% of the time, Pallas kernels for 2%

profile of v5, /device:TPU:0, one launch (start us, length us, event | category | flops | bytes accessed | tf_op | source)
XLA Modules:
  0.0 38.4 jit_solution(7958912474262326556)
XLA Ops:
  0.0 0.0 copy-start
  0.0 1.7 %shard_map.109 = bf16[16,56,128]{2,1,0:T(8,128)(2,1)} custom-call(bf16[32,768]{1,0:T(8,128)(2,1)} %query_hbm.1, bf16[32,768]{1,0:T(8,128)(2,1)} %key_hbm.1, bf16[32,768]{1,0:T(8,128)(2,1)} %value_hbm.1, f32[3,128]{1,0:T(4,128)} %bitcast.19), custom_call_target="tpu_custom_call" | custom-call | tf_op jit(solution)/shard_map/pallas_call | solution.py:472
  1.7 6.3 %all-to-all-start = ((bf16[16,56,128]{2,1,0:T(8,128)(2,1)}), bf16[16,56,128]{2,1,0:T(8,128)(2,1)S(1)}, u32[]{:S(2)}, u32[]{:S(2)}) async-start(bf16[16,56,128]{2,1,0:T(8,128)(2,1)} %shard_map.109), calls=%async_computation | async-start | bytes 458752 | tf_op jit(solution)/shard_map/all_to_all | solution.py:467
  8.0 0.7 %constant_dynamic-slice_fusion.3.c1_ref = f32[1,256]{1,0:T(1,128)S(1)} fusion(f32[3,256]{1,0:T(4,128)} %param.17, s32[]{:T(128)S(6)} %select_n.30), kind=kLoop, calls=%fused_computation.8 | loop fusion | bytes 2052 | tf_op jit(solution)/shard_map/jit(dynamic_index_in_dim)/dynamic_slice | solution.py:504
  8.7 0.7 %constant_dynamic-slice_fusion.2.c2_ref = f32[1,64]{1,0:T(1,128)S(1)} fusion(f32[3,64]{1,0:T(4,128)} %param.19, s32[]{:T(128)S(6)} %select_n.30), kind=kLoop, calls=%fused_computation.7 | loop fusion | bytes 516 | tf_op jit(solution)/shard_map/jit(dynamic_index_in_dim)/dynamic_slice | solution.py:504
  9.4 0.7 %constant_dynamic-slice_fusion = (f32[1,64]{1,0:T(1,128)S(1)}, f32[1,64]{1,0:T(1,128)S(1)}) fusion(f32[3,64]{1,0:T(4,128)} %param.21, s32[]{:T(128)S(6)} %select_n.30, f32[3,64]{1,0:T(4,128)} %param.20), kind=kLoop, calls=%fused_computation.5 | loop fusion | bytes 1028 | tf_op jit(solution)/shard_map/jit(dynamic_index_in_dim)/dynamic_slice | solution.py:504
  10.1 0.0 copy-done
  10.1 0.9 %dynamic-slice_bitcast_fusion.w2t_ref = f32[64,256]{1,0:T(8,128)S(1)} fusion(f32[3,256,64]{1,2,0:T(8,128)} %param.18, s32[]{:T(128)S(6)} %select_n.30), kind=kLoop, calls=%fused_computation | loop fusion | bytes 131076 | tf_op jit(solution)/shard_map/transpose | solution.py:509
  11.0 4.4 %all-to-all-done = bf16[16,56,128]{2,1,0:T(8,128)(2,1)S(1)} async-done(((bf16[16,56,128]{2,1,0:T(8,128)(2,1)}), bf16[16,56,128]{2,1,0:T(8,128)(2,1)S(1)}, u32[]{:S(2)}, u32[]{:S(2)}) %all-to-all-start) | async-done | bytes 229408 | tf_op jit(solution)/shard_map/all_to_all | solution.py:467
  15.5 3.6 %shard_map.110 = (f32[512,64]{1,0:T(8,128)S(1)}, bf16[144,256]{1,0:T(8,128)(2,1)S(1)}, bf16[128,256]{1,0:T(8,128)(2,1)S(1)}, bf16[128,256]{1,0:T(8,128)(2,1)S(1)...) custom-call(s32[1]{0:T(128)} %bitcast.dir_ref, ...), custom_call_target="tpu_custom_call" | custom-call | flops 100000000 | bytes 1000000 | tf_op jit(solution)/shard_map/pallas_call | solution.py:413
  19.1 2.7 %collective-permute-start = (bf16[144,256]{1,0:T(8,128)(2,1)S(1)}, bf16[144,256]{1,0:T(8,128)(2,1)S(1)}, u32[]{:S(2)}, u32[]{:S(2)}) collective-permute-start(bf16[144,256]{1,0:T(8,128)(2,1)S(1)} %get-tuple-element.20), channel_id=1, source_target_pairs={{0,4},{1,5},{2,6},{3,7},{4,0},{5,1},{6,2},{7,3},{8,12},{9,13},{10,... | collective-permute-start | bytes 221192 | tf_op jit(solution)/shard_map/ppermute | solution.py:529
  21.7 0.7 %shard_map.111 = (f32[128,64]{1,0:T(8,128)S(1)}, bf16[8,208,128]{2,1,0:T(8,128)(2,1)S(1)}, bf16[8,208,64]{2,1,0:T(8,128)(2,1)S(1)}, f32[8,64,64]{2,1,0:T(8,128)S...) custom-call(s32[1]{0:T(128)} %bitcast.dir_ref, bf16[512,128]{1,0:T(8,128)(2,1)S(1)} %bitcast.16, ...), custom_call_target="tpu_custom_call" | custom-call | flops 100000000 | bytes 1000000 | tf_op jit(solution)/shard_map/pallas_call | solution.py:413
  22.5 2.7 %collective-permute-done.delta_ref = bf16[144,256]{1,0:T(8,128)(2,1)S(1)} collective-permute-done((bf16[144,256]{1,0:T(8,128)(2,1)S(1)}, bf16[144,256]{1,0:T(8,128)(2,1)S(1)}, u32[]{:S(2)}, u32[]{:S(2)}) %collective-permute-start) | collective-permute-done | bytes 73760 | tf_op jit(solution)/shard_map/ppermute | solution.py:529
  25.2 4.0 %shard_map.112 = bf16[16,16,128]{2,1,0:T(8,128)(2,1)S(1)} custom-call(s32[1]{0:T(128)} %bitcast.dir_ref, bf16[512,128]{1,0:T(8,128)(2,1)S(1)} %bitcast.17, bf16[16,16,128]{2,1,0:T(8,128)(2,1)S(1)} %slice.25.v_ref, f32[4,1,128]{2,1,0:T(1,128)S(1)} %slice_add_fusion.r_ref, f32[64,256]{1,0:T(8,128)S(1)} %dynamic-slice_bitcast_fusion.1.w1_ref, ...), custom_call_target="tpu_custom_call" | custom-call | flops 100000000 | bytes 1000000 | tf_op jit(solution)/shard_map/pallas_call | solution.py:413
  29.2 0.0 copy-start.1
  29.2 8.5 %all_to_all.10.back_ref = bf16[16,16,128]{2,1,0:T(8,128)(2,1)S(1)} all-to-all(bf16[16,16,128]{2,1,0:T(8,128)(2,1)S(1)} %shard_map.112), channel_id=1, replica_groups={{0,8,16,24,1,9,17,25,2,10,18,26,3,11,19,27},{4,12,20,28,5,13,21,29,6,14..., dimensions={0} | all-to-all | bytes 131072 | tf_op jit(solution)/shard_map/all_to_all | solution.py:467
  37.7 0.0 copy-done.1
  37.7 0.7 %shard_map.113 = bf16[32,768]{1,0:T(8,128)(2,1)} custom-call(bf16[16,16,128]{2,1,0:T(8,128)(2,1)S(1)} %all_to_all.10.back_ref, bf16[32,768]{1,0:T(8,128)(2,1)S(1)} %copy-done.1), custom_call_target="tpu_custom_call" | custom-call | tf_op jit(solution)/shard_map/pallas_call | solution.py:551
  (6 shorter events, 0.0 us)
Async XLA Ops:
  0.0 10.1 %copy-start = (f32[3,64,256]{2,1,0:T(8,128)S(1)}, f32[3,64,256]{2,1,0:T(8,128)}, u32[]{:S(2)}) copy-start(f32[3,64,256]{2,1,0:T(8,128)} %param.16) | copy-start | bytes 589828
  1.7 13.7 %all-to-all-start = ((bf16[16,56,128]{2,1,0:T(8,128)(2,1)}), bf16[16,56,128]{2,1,0:T(8,128)(2,1)S(1)}, u32[]{:S(2)}, u32[]{:S(2)}) async-start(bf16[16,56,128]{2,1,0:T(8,128)(2,1)} %shard_map.109), calls=%async_computation | async-start | bytes 458752 | tf_op jit(solution)/shard_map/all_to_all | solution.py:467
  19.1 6.1 %collective-permute-start = (bf16[144,256]{1,0:T(8,128)(2,1)S(1)}, bf16[144,256]{1,0:T(8,128)(2,1)S(1)}, u32[]{:S(2)}, u32[]{:S(2)}) collective-permute-start(bf16[144,256]{1,0:T(8,128)(2,1)S(1)} %get-tuple-element.20), channel_id=1, source_target_pairs={{0,4},{1,5},{2,6},{3,7},{4,0},{5,1},{6,2},{7,3},{8,12},{9,13},{10,... | collective-permute-start | bytes 221192 | tf_op jit(solution)/shard_map/ppermute | solution.py:529
  29.2 8.5 %copy-start.1 = (bf16[32,768]{1,0:T(8,128)(2,1)S(1)}, bf16[32,768]{1,0:T(8,128)(2,1)}, u32[]{:S(2)}) copy-start(bf16[32,768]{1,0:T(8,128)(2,1)} %gate_ref.1) | copy-start | bytes 147460

commit v6 on v5

--- a/solution.py
+++ b/solution.py
@@ -269,12 +269,10 @@
         end = run_chunks(total, backward, qk_ref, v_ref, r_ref, refs, gain, shift, emit)
     start = centre_start(w1_ref, c1_ref, w2t_ref, c2_ref)
     ends = [part - first for part, first in zip(end, start)]
-    delta_ref[0:D_HEAD, :] = ends[0].astype(bf16)
-    delta_ref[D_HEAD : 2 * D_HEAD, :] = ends[2].astype(bf16)
     wide = jnp.concatenate([ends[3], jnp.zeros((1, INNER - D_HEAD), f32)], axis=1)
-    delta_ref[2 * D_HEAD : 2 * D_HEAD + 16, :] = jnp.concatenate(
-        [jnp.broadcast_to(ends[1], (8, INNER)), jnp.broadcast_to(wide, (8, INNER))], axis=0
-    ).astype(bf16)
+    at = lax.broadcasted_iota(jnp.int32, (8, INNER), 0)
+    biases = jnp.where(at == 0, ends[1], jnp.where(at == 1, wide, 0.0))
+    delta_ref[...] = jnp.concatenate([ends[0], ends[2], biases], axis=0).astype(bf16)
 
 
 def between_phases(total, dir_ref, qk_ref, v_ref, r_ref, gain_ref, shift_ref, dual_ref, low_ref, act_ref, weighted_ref,
@@ -303,12 +301,12 @@
                  delta_ref, *refs):
     backward = 1 - dir_ref[0]
     gain, shift = gain_ref[...], shift_ref[...]
-    biases = delta_ref[2 * D_HEAD : 2 * D_HEAD + 16, :].astype(f32)
+    delta = delta_ref[...].astype(f32)
     deltas = (
-        delta_ref[0:D_HEAD, :].astype(f32),
-        biases[0:1],
-        delta_ref[D_HEAD : 2 * D_HEAD, :].astype(f32),
-        biases[8:9, :D_HEAD],
+        delta[:D_HEAD],
+        delta[2 * D_HEAD : 2 * D_HEAD + 1],
+        delta[D_HEAD : 2 * D_HEAD],
+        delta[2 * D_HEAD + 1 : 2 * D_HEAD + 2, :D_HEAD],
     )
     start = centre_start(w1_ref, c1_ref, w2t_ref, c2_ref)
     state = tuple(part + delta for part, delta in zip(start, deltas))
@@ -513,7 +511,7 @@
     )
     ahead = half.astype(jnp.int32).reshape(1)
     shape = jax.ShapeDtypeStruct
-    outs = [shape((half_tokens, D_HEAD), f32), shape((2 * D_HEAD + 16, INNER), bf16)]
+    outs = [shape((half_tokens, D_HEAD), f32), shape((2 * D_HEAD + 8, INNER), bf16)]
     if short:
         outs += [
             shape((2 * MINI, INNER), bf16),

time: 38.8 us -> 38.8 us (level)
  no operation moved by 1% of the time
where the time goes in v6:
time: 38.8 us; the launch traced here: 38.3 us
  Pallas kernels  10.7 us (28%)
  starting transfers between devices  8.96 us (23%)
  blocking collectives  8.53 us (22%)
  waiting for transfers between devices  7.05 us (18%)
  local copies, waits for them, and re-layouts  2.97 us (8%)
    all_to_all x1, blocking collectives, exchange(): lax.all_to_all(blocks, ('seq', 'head'), 0, 0, axis_index_groups=halves)  8.53 us
    pallas_call x3, Pallas kernels, call_phase(): pl.pallas_call(kernel, out_shape=outs, in_specs=[pl.BlockSpec(memory_spac...  8.33 us
    all_to_all x1, starting transfers between devices, exchange(): lax.all_to_all(blocks, ('seq', 'head'), 0, 0, axis_index_groups=halves)  6.3 us
    all_to_all x1, waiting for transfers between devices, exchange(): lax.all_to_all(blocks, ('seq', 'head'), 0, 0, axis_index_groups=halves)  4.41 us
    ppermute x1, starting transfers between devices, local(): delta = lax.ppermute(delta, 'seq', route)  2.66 us
    ppermute x1, waiting for transfers between devices, local(): delta = lax.ppermute(delta, 'seq', route)  2.64 us
    dynamic_slice x3, local copies, waits for them, and re-layouts, pick(): return lax.dynamic_index_in_dim(array_in, slot, 0, keepdims=False)  2.08 us
    pallas_call x1, Pallas kernels, local(): pl.pallas_call(functools.partial(pack_kernel, head_size, heads_local), ou...  1.7 us
  transfers between devices with their start and end apart: 2, of which 2 were waited for; matrix products, arithmetic and copies ran while one was open for 8% of the time, Pallas kernels for 2%

profile of v6, /device:TPU:0, one launch (start us, length us, event | category | flops | bytes accessed | tf_op | source)
XLA Modules:
  0.0 38.3 jit_solution(6343809454957329834)
XLA Ops:
  0.0 0.0 copy-start
  0.0 1.7 %shard_map.109 = bf16[16,56,128]{2,1,0:T(8,128)(2,1)} custom-call(bf16[32,768]{1,0:T(8,128)(2,1)} %query_hbm.1, bf16[32,768]{1,0:T(8,128)(2,1)} %key_hbm.1, bf16[32,768]{1,0:T(8,128)(2,1)} %value_hbm.1, f32[3,128]{1,0:T(4,128)} %bitcast.19), custom_call_target="tpu_custom_call" | custom-call | tf_op jit(solution)/shard_map/pallas_call | solution.py:470
  1.7 6.3 %all-to-all-start = ((bf16[16,56,128]{2,1,0:T(8,128)(2,1)}), bf16[16,56,128]{2,1,0:T(8,128)(2,1)S(1)}, u32[]{:S(2)}, u32[]{:S(2)}) async-start(bf16[16,56,128]{2,1,0:T(8,128)(2,1)} %shard_map.109), calls=%async_computation | async-start | bytes 458752 | tf_op jit(solution)/shard_map/all_to_all | solution.py:465
  8.0 0.7 %constant_dynamic-slice_fusion.3.c1_ref = f32[1,256]{1,0:T(1,128)S(1)} fusion(f32[3,256]{1,0:T(4,128)} %param.17, s32[]{:T(128)S(6)} %select_n.30), kind=kLoop, calls=%fused_computation.8 | loop fusion | bytes 2052 | tf_op jit(solution)/shard_map/jit(dynamic_index_in_dim)/dynamic_slice | solution.py:502
  8.7 0.7 %constant_dynamic-slice_fusion.2.c2_ref = f32[1,64]{1,0:T(1,128)S(1)} fusion(f32[3,64]{1,0:T(4,128)} %param.19, s32[]{:T(128)S(6)} %select_n.30), kind=kLoop, calls=%fused_computation.7 | loop fusion | bytes 516 | tf_op jit(solution)/shard_map/jit(dynamic_index_in_dim)/dynamic_slice | solution.py:502
  9.4 0.7 %constant_dynamic-slice_fusion = (f32[1,64]{1,0:T(1,128)S(1)}, f32[1,64]{1,0:T(1,128)S(1)}) fusion(f32[3,64]{1,0:T(4,128)} %param.21, s32[]{:T(128)S(6)} %select_n.30, f32[3,64]{1,0:T(4,128)} %param.20), kind=kLoop, calls=%fused_computation.5 | loop fusion | bytes 1028 | tf_op jit(solution)/shard_map/jit(dynamic_index_in_dim)/dynamic_slice | solution.py:502
  10.1 0.0 copy-done
  10.1 0.9 %dynamic-slice_bitcast_fusion.w2t_ref = f32[64,256]{1,0:T(8,128)S(1)} fusion(f32[3,256,64]{1,2,0:T(8,128)} %param.18, s32[]{:T(128)S(6)} %select_n.30), kind=kLoop, calls=%fused_computation | loop fusion | bytes 131076 | tf_op jit(solution)/shard_map/transpose | solution.py:507
  11.0 4.4 %all-to-all-done = bf16[16,56,128]{2,1,0:T(8,128)(2,1)S(1)} async-done(((bf16[16,56,128]{2,1,0:T(8,128)(2,1)}), bf16[16,56,128]{2,1,0:T(8,128)(2,1)S(1)}, u32[]{:S(2)}, u32[]{:S(2)}) %all-to-all-start) | async-done | bytes 229408 | tf_op jit(solution)/shard_map/all_to_all | solution.py:465
  15.5 3.6 %shard_map.110 = (f32[512,64]{1,0:T(8,128)S(1)}, bf16[136,256]{1,0:T(8,128)(2,1)S(1)}, bf16[128,256]{1,0:T(8,128)(2,1)S(1)}, bf16[128,256]{1,0:T(8,128)(2,1)S(1)...) custom-call(s32[1]{0:T(128)} %bitcast.dir_ref, ...), custom_call_target="tpu_custom_call" | custom-call | flops 100000000 | bytes 1000000 | tf_op jit(solution)/shard_map/pallas_call | solution.py:411
  19.1 2.7 %collective-permute-start = (bf16[136,256]{1,0:T(8,128)(2,1)S(1)}, bf16[136,256]{1,0:T(8,128)(2,1)S(1)}, u32[]{:S(2)}, u32[]{:S(2)}) collective-permute-start(bf16[136,256]{1,0:T(8,128)(2,1)S(1)} %get-tuple-element.20), channel_id=1, source_target_pairs={{0,4},{1,5},{2,6},{3,7},{4,0},{5,1},{6,2},{7,3},{8,12},{9,13},{10,... | collective-permute-start | bytes 208904 | tf_op jit(solution)/shard_map/ppermute | solution.py:527
  21.8 0.7 %shard_map.111 = (f32[128,64]{1,0:T(8,128)S(1)}, bf16[8,208,128]{2,1,0:T(8,128)(2,1)S(1)}, bf16[8,208,64]{2,1,0:T(8,128)(2,1)S(1)}, f32[8,64,64]{2,1,0:T(8,128)S...) custom-call(s32[1]{0:T(128)} %bitcast.dir_ref, bf16[512,128]{1,0:T(8,128)(2,1)S(1)} %bitcast.16, ...), custom_call_target="tpu_custom_call" | custom-call | flops 100000000 | bytes 1000000 | tf_op jit(solution)/shard_map/pallas_call | solution.py:411
  22.5 2.6 %collective-permute-done.delta_ref = bf16[136,256]{1,0:T(8,128)(2,1)S(1)} collective-permute-done((bf16[136,256]{1,0:T(8,128)(2,1)S(1)}, bf16[136,256]{1,0:T(8,128)(2,1)S(1)}, u32[]{:S(2)}, u32[]{:S(2)}) %collective-permute-start) | collective-permute-done | bytes 69664 | tf_op jit(solution)/shard_map/ppermute | solution.py:527
  25.1 4.0 %shard_map.112 = bf16[16,16,128]{2,1,0:T(8,128)(2,1)S(1)} custom-call(s32[1]{0:T(128)} %bitcast.dir_ref, bf16[512,128]{1,0:T(8,128)(2,1)S(1)} %bitcast.17, bf16[16,16,128]{2,1,0:T(8,128)(2,1)S(1)} %slice.25.v_ref, f32[4,1,128]{2,1,0:T(1,128)S(1)} %slice_add_fusion.r_ref, f32[64,256]{1,0:T(8,128)S(1)} %dynamic-slice_bitcast_fusion.1.w1_ref, ...), custom_call_target="tpu_custom_call" | custom-call | flops 100000000 | bytes 1000000 | tf_op jit(solution)/shard_map/pallas_call | solution.py:411
  29.1 0.0 copy-start.1
  29.1 8.5 %all_to_all.10.back_ref = bf16[16,16,128]{2,1,0:T(8,128)(2,1)S(1)} all-to-all(bf16[16,16,128]{2,1,0:T(8,128)(2,1)S(1)} %shard_map.112), channel_id=1, replica_groups={{0,8,16,24,1,9,17,25,2,10,18,26,3,11,19,27},{4,12,20,28,5,13,21,29,6,14..., dimensions={0} | all-to-all | bytes 131072 | tf_op jit(solution)/shard_map/all_to_all | solution.py:465
  37.6 0.0 copy-done.1
  37.6 0.7 %shard_map.113 = bf16[32,768]{1,0:T(8,128)(2,1)} custom-call(bf16[16,16,128]{2,1,0:T(8,128)(2,1)S(1)} %all_to_all.10.back_ref, bf16[32,768]{1,0:T(8,128)(2,1)S(1)} %copy-done.1), custom_call_target="tpu_custom_call" | custom-call | tf_op jit(solution)/shard_map/pallas_call | solution.py:549
  (6 shorter events, 0.0 us)
Async XLA Ops:
  0.0 10.1 %copy-start = (f32[3,64,256]{2,1,0:T(8,128)S(1)}, f32[3,64,256]{2,1,0:T(8,128)}, u32[]{:S(2)}) copy-start(f32[3,64,256]{2,1,0:T(8,128)} %param.16) | copy-start | bytes 589828
  1.7 13.7 %all-to-all-start = ((bf16[16,56,128]{2,1,0:T(8,128)(2,1)}), bf16[16,56,128]{2,1,0:T(8,128)(2,1)S(1)}, u32[]{:S(2)}, u32[]{:S(2)}) async-start(bf16[16,56,128]{2,1,0:T(8,128)(2,1)} %shard_map.109), calls=%async_computation | async-start | bytes 458752 | tf_op jit(solution)/shard_map/all_to_all | solution.py:465
  19.1 6.0 %collective-permute-start = (bf16[136,256]{1,0:T(8,128)(2,1)S(1)}, bf16[136,256]{1,0:T(8,128)(2,1)S(1)}, u32[]{:S(2)}, u32[]{:S(2)}) collective-permute-start(bf16[136,256]{1,0:T(8,128)(2,1)S(1)} %get-tuple-element.20), channel_id=1, source_target_pairs={{0,4},{1,5},{2,6},{3,7},{4,0},{5,1},{6,2},{7,3},{8,12},{9,13},{10,... | collective-permute-start | bytes 208904 | tf_op jit(solution)/shard_map/ppermute | solution.py:527
  29.1 8.5 %copy-start.1 = (bf16[32,768]{1,0:T(8,128)(2,1)S(1)}, bf16[32,768]{1,0:T(8,128)(2,1)}, u32[]{:S(2)}) copy-start(bf16[32,768]{1,0:T(8,128)(2,1)} %gate_ref.1) | copy-start | bytes 147460

commit v7 on v6

--- a/solution.py
+++ b/solution.py
@@ -142,7 +142,7 @@
         emit(one[0], found[at * MINI : (at + 1) * MINI])
 
 
-def run_chunk(backward, tokens, state, gain, shift, emit, ready=None, keep_last=False):
+def run_chunk(backward, tokens, state, gain, shift, emit, ready=None, keep_last=False, ends=False):
     weight_one, bias_one, second_turned, bias_two = state
     places, pairs, queries, keys, values, rates = tokens
     steps = len(places)
@@ -199,9 +199,14 @@
         weighted_low = (weighted_turned - weighted_high.astype(f32)).astype(bf16)
         change = mm(jnp.concatenate([weighted_high, weighted_low], axis=0), act_high)
         second_turned = second_turned - (change[:D_HEAD] + change[D_HEAD:])
+        last = step + 1 == steps
+        first = MINI if last else 0
+        rows = slice(first, 2 * MINI if last and ends else None)
         mixed = mm(
-            jnp.concatenate([plain, mixer], axis=1), jnp.concatenate([first_high, first_low, grad_one], axis=0)
+            jnp.concatenate([plain[rows], mixer[rows]], axis=1),
+            jnp.concatenate([first_high, first_low, grad_one], axis=0),
         )
+        mixed_query = mixed[MINI - first : 2 * MINI - first]
         weighted = weighted_turned.T
         bias_column = bias_column - jnp.sum(weighted_turned, axis=1, keepdims=True)
         bias_two = bias_two - jnp.sum(weighted, axis=0, keepdims=True)
@@ -210,14 +215,17 @@
             waiting = []
         if ready is None and step % 2 == 0 and step + 2 < steps:
             made = made + prepare(step + 2, backward, tokens, gain, shift, columns)
-        dual = gelu(mixed[MINI : 2 * MINI] + bias_one)
+        dual = gelu(mixed_query + bias_one)
         dual_high = dual.astype(bf16)
         dual_low = (dual - dual_high.astype(f32)).astype(bf16)
         waiting.append((places[step], dual_high, dual_low, act_high, weighted.astype(bf16)))
-        act, slope = gelu_and_slope(mixed[:MINI] + bias_one)
-        act_high = act.astype(bf16)
-        weight_one = weight_one + mixed[2 * MINI : 3 * MINI]
-        bias_one = bias_one + mixed[3 * MINI : 3 * MINI + 1]
+        if not last:
+            act, slope = gelu_and_slope(mixed[:MINI] + bias_one)
+            act_high = act.astype(bf16)
+        if last and ends:
+            continue
+        weight_one = weight_one + mixed[2 * MINI - first : 3 * MINI - first]
+        bias_one = bias_one + mixed[3 * MINI - first : 3 * MINI - first + 1]
     if not keep_last:
         finish(waiting, second_turned, bias_two, backward, gain, shift, emit)
     return (weight_one, bias_one, second_turned, bias_two), waiting
@@ -335,7 +343,7 @@
         def ready(step):
             return tuple(ref[step] for ref in ready_refs)
 
-        run_chunk(backward, tokens, state, gain, shift, emit, ready)
+        run_chunk(backward, tokens, state, gain, shift, emit, ready, ends=True)
     else:
         out_ref, *state_refs = refs
         for ref, part in zip(state_refs, state):

time: 38.8 us -> 38.8 us (level)
  no operation moved by 1% of the time
where the time goes in v7:
time: 38.8 us; the launch traced here: 38.3 us
  Pallas kernels  10.7 us (28%)
  starting transfers between devices  8.96 us (23%)
  blocking collectives  8.53 us (22%)
  waiting for transfers between devices  7.05 us (18%)
  local copies, waits for them, and re-layouts  2.97 us (8%)
    all_to_all x1, blocking collectives, exchange(): lax.all_to_all(blocks, ('seq', 'head'), 0, 0, axis_index_groups=halves)  8.53 us
    pallas_call x3, Pallas kernels, call_phase(): pl.pallas_call(kernel, out_shape=outs, in_specs=[pl.BlockSpec(memory_spac...  8.33 us
    all_to_all x1, starting transfers between devices, exchange(): lax.all_to_all(blocks, ('seq', 'head'), 0, 0, axis_index_groups=halves)  6.3 us
    all_to_all x1, waiting for transfers between devices, exchange(): lax.all_to_all(blocks, ('seq', 'head'), 0, 0, axis_index_groups=halves)  4.41 us
    ppermute x1, starting transfers between devices, local(): delta = lax.ppermute(delta, 'seq', route)  2.66 us
    ppermute x1, waiting for transfers between devices, local(): delta = lax.ppermute(delta, 'seq', route)  2.64 us
    dynamic_slice x3, local copies, waits for them, and re-layouts, pick(): return lax.dynamic_index_in_dim(array_in, slot, 0, keepdims=False)  2.08 us
    pallas_call x1, Pallas kernels, local(): pl.pallas_call(functools.partial(pack_kernel, head_size, heads_local), ou...  1.7 us
  transfers between devices with their start and end apart: 2, of which 2 were waited for; matrix products, arithmetic and copies ran while one was open for 8% of the time, Pallas kernels for 2%

profile of v7, /device:TPU:0, one launch (start us, length us, event | category | flops | bytes accessed | tf_op | source)
XLA Modules:
  0.0 38.3 jit_solution(8906907459550216215)
XLA Ops:
  0.0 0.0 copy-start
  0.0 1.7 %shard_map.109 = bf16[16,56,128]{2,1,0:T(8,128)(2,1)} custom-call(bf16[32,768]{1,0:T(8,128)(2,1)} %query_hbm.1, bf16[32,768]{1,0:T(8,128)(2,1)} %key_hbm.1, bf16[32,768]{1,0:T(8,128)(2,1)} %value_hbm.1, f32[3,128]{1,0:T(4,128)} %bitcast.19), custom_call_target="tpu_custom_call" | custom-call | tf_op jit(solution)/shard_map/pallas_call | solution.py:478
  1.7 6.3 %all-to-all-start = ((bf16[16,56,128]{2,1,0:T(8,128)(2,1)}), bf16[16,56,128]{2,1,0:T(8,128)(2,1)S(1)}, u32[]{:S(2)}, u32[]{:S(2)}) async-start(bf16[16,56,128]{2,1,0:T(8,128)(2,1)} %shard_map.109), calls=%async_computation | async-start | bytes 458752 | tf_op jit(solution)/shard_map/all_to_all | solution.py:473
  8.0 0.7 %constant_dynamic-slice_fusion.3.c1_ref = f32[1,256]{1,0:T(1,128)S(1)} fusion(f32[3,256]{1,0:T(4,128)} %param.17, s32[]{:T(128)S(6)} %select_n.30), kind=kLoop, calls=%fused_computation.8 | loop fusion | bytes 2052 | tf_op jit(solution)/shard_map/jit(dynamic_index_in_dim)/dynamic_slice | solution.py:510
  8.7 0.7 %constant_dynamic-slice_fusion.2.c2_ref = f32[1,64]{1,0:T(1,128)S(1)} fusion(f32[3,64]{1,0:T(4,128)} %param.19, s32[]{:T(128)S(6)} %select_n.30), kind=kLoop, calls=%fused_computation.7 | loop fusion | bytes 516 | tf_op jit(solution)/shard_map/jit(dynamic_index_in_dim)/dynamic_slice | solution.py:510
  9.4 0.7 %constant_dynamic-slice_fusion = (f32[1,64]{1,0:T(1,128)S(1)}, f32[1,64]{1,0:T(1,128)S(1)}) fusion(f32[3,64]{1,0:T(4,128)} %param.21, s32[]{:T(128)S(6)} %select_n.30, f32[3,64]{1,0:T(4,128)} %param.20), kind=kLoop, calls=%fused_computation.5 | loop fusion | bytes 1028 | tf_op jit(solution)/shard_map/jit(dynamic_index_in_dim)/dynamic_slice | solution.py:510
  10.1 0.0 copy-done
  10.1 0.9 %dynamic-slice_bitcast_fusion.w2t_ref = f32[64,256]{1,0:T(8,128)S(1)} fusion(f32[3,256,64]{1,2,0:T(8,128)} %param.18, s32[]{:T(128)S(6)} %select_n.30), kind=kLoop, calls=%fused_computation | loop fusion | bytes 131076 | tf_op jit(solution)/shard_map/transpose | solution.py:515
  11.0 4.4 %all-to-all-done = bf16[16,56,128]{2,1,0:T(8,128)(2,1)S(1)} async-done(((bf16[16,56,128]{2,1,0:T(8,128)(2,1)}), bf16[16,56,128]{2,1,0:T(8,128)(2,1)S(1)}, u32[]{:S(2)}, u32[]{:S(2)}) %all-to-all-start) | async-done | bytes 229408 | tf_op jit(solution)/shard_map/all_to_all | solution.py:473
  15.5 3.6 %shard_map.110 = (f32[512,64]{1,0:T(8,128)S(1)}, bf16[136,256]{1,0:T(8,128)(2,1)S(1)}, bf16[128,256]{1,0:T(8,128)(2,1)S(1)}, bf16[128,256]{1,0:T(8,128)(2,1)S(1)...) custom-call(s32[1]{0:T(128)} %bitcast.dir_ref, ...), custom_call_target="tpu_custom_call" | custom-call | flops 100000000 | bytes 1000000 | tf_op jit(solution)/shard_map/pallas_call | solution.py:419
  19.1 2.7 %collective-permute-start = (bf16[136,256]{1,0:T(8,128)(2,1)S(1)}, bf16[136,256]{1,0:T(8,128)(2,1)S(1)}, u32[]{:S(2)}, u32[]{:S(2)}) collective-permute-start(bf16[136,256]{1,0:T(8,128)(2,1)S(1)} %get-tuple-element.20), channel_id=1, source_target_pairs={{0,4},{1,5},{2,6},{3,7},{4,0},{5,1},{6,2},{7,3},{8,12},{9,13},{10,... | collective-permute-start | bytes 208904 | tf_op jit(solution)/shard_map/ppermute | solution.py:535
  21.7 0.7 %shard_map.111 = (f32[128,64]{1,0:T(8,128)S(1)}, bf16[8,208,128]{2,1,0:T(8,128)(2,1)S(1)}, bf16[8,208,64]{2,1,0:T(8,128)(2,1)S(1)}, f32[8,64,64]{2,1,0:T(8,128)S...) custom-call(s32[1]{0:T(128)} %bitcast.dir_ref, bf16[512,128]{1,0:T(8,128)(2,1)S(1)} %bitcast.16, ...), custom_call_target="tpu_custom_call" | custom-call | flops 100000000 | bytes 1000000 | tf_op jit(solution)/shard_map/pallas_call | solution.py:419
  22.5 2.6 %collective-permute-done.delta_ref = bf16[136,256]{1,0:T(8,128)(2,1)S(1)} collective-permute-done((bf16[136,256]{1,0:T(8,128)(2,1)S(1)}, bf16[136,256]{1,0:T(8,128)(2,1)S(1)}, u32[]{:S(2)}, u32[]{:S(2)}) %collective-permute-start) | collective-permute-done | bytes 69664 | tf_op jit(solution)/shard_map/ppermute | solution.py:535
  25.1 4.0 %shard_map.112 = bf16[16,16,128]{2,1,0:T(8,128)(2,1)S(1)} custom-call(s32[1]{0:T(128)} %bitcast.dir_ref, bf16[512,128]{1,0:T(8,128)(2,1)S(1)} %bitcast.17, bf16[16,16,128]{2,1,0:T(8,128)(2,1)S(1)} %slice.25.v_ref, f32[4,1,128]{2,1,0:T(1,128)S(1)} %slice_add_fusion.r_ref, f32[64,256]{1,0:T(8,128)S(1)} %dynamic-slice_bitcast_fusion.1.w1_ref, ...), custom_call_target="tpu_custom_call" | custom-call | flops 100000000 | bytes 1000000 | tf_op jit(solution)/shard_map/pallas_call | solution.py:419
  29.1 0.0 copy-start.1
  29.1 8.5 %all_to_all.10.back_ref = bf16[16,16,128]{2,1,0:T(8,128)(2,1)S(1)} all-to-all(bf16[16,16,128]{2,1,0:T(8,128)(2,1)S(1)} %shard_map.112), channel_id=1, replica_groups={{0,8,16,24,1,9,17,25,2,10,18,26,3,11,19,27},{4,12,20,28,5,13,21,29,6,14..., dimensions={0} | all-to-all | bytes 131072 | tf_op jit(solution)/shard_map/all_to_all | solution.py:473
  37.6 0.0 copy-done.1
  37.6 0.7 %shard_map.113 = bf16[32,768]{1,0:T(8,128)(2,1)} custom-call(bf16[16,16,128]{2,1,0:T(8,128)(2,1)S(1)} %all_to_all.10.back_ref, bf16[32,768]{1,0:T(8,128)(2,1)S(1)} %copy-done.1), custom_call_target="tpu_custom_call" | custom-call | tf_op jit(solution)/shard_map/pallas_call | solution.py:557
  (6 shorter events, 0.0 us)
Async XLA Ops:
  0.0 10.1 %copy-start = (f32[3,64,256]{2,1,0:T(8,128)S(1)}, f32[3,64,256]{2,1,0:T(8,128)}, u32[]{:S(2)}) copy-start(f32[3,64,256]{2,1,0:T(8,128)} %param.16) | copy-start | bytes 589828
  1.7 13.7 %all-to-all-start = ((bf16[16,56,128]{2,1,0:T(8,128)(2,1)}), bf16[16,56,128]{2,1,0:T(8,128)(2,1)S(1)}, u32[]{:S(2)}, u32[]{:S(2)}) async-start(bf16[16,56,128]{2,1,0:T(8,128)(2,1)} %shard_map.109), calls=%async_computation | async-start | bytes 458752 | tf_op jit(solution)/shard_map/all_to_all | solution.py:473
  19.1 6.0 %collective-permute-start = (bf16[136,256]{1,0:T(8,128)(2,1)S(1)}, bf16[136,256]{1,0:T(8,128)(2,1)S(1)}, u32[]{:S(2)}, u32[]{:S(2)}) collective-permute-start(bf16[136,256]{1,0:T(8,128)(2,1)S(1)} %get-tuple-element.20), channel_id=1, source_target_pairs={{0,4},{1,5},{2,6},{3,7},{4,0},{5,1},{6,2},{7,3},{8,12},{9,13},{10,... | collective-permute-start | bytes 208904 | tf_op jit(solution)/shard_map/ppermute | solution.py:535
  29.1 8.5 %copy-start.1 = (bf16[32,768]{1,0:T(8,128)(2,1)S(1)}, bf16[32,768]{1,0:T(8,128)(2,1)}, u32[]{:S(2)}) copy-start(bf16[32,768]{1,0:T(8,128)(2,1)} %gate_ref.1) | copy-start | bytes 147460

commit v8 on v7

--- a/solution.py
+++ b/solution.py
@@ -142,23 +142,25 @@
         emit(one[0], found[at * MINI : (at + 1) * MINI])
 
 
-def run_chunk(backward, tokens, state, gain, shift, emit, ready=None, keep_last=False, ends=False):
+def first_product(pair, weight_one):
+    blank = jnp.zeros((D_HEAD, INNER), bf16)
+    first_high = weight_one.astype(bf16)
+    first_low = (weight_one - first_high.astype(f32)).astype(bf16)
+    return mm(
+        jnp.concatenate([pair, pair], axis=1), jnp.concatenate([blank, first_high, blank, first_low], axis=0)
+    )
+
+
+def run_chunk(backward, tokens, state, gain, shift, emit, ready=None, keep_last=False, ends=False, pre_one=None):
     weight_one, bias_one, second_turned, bias_two = state
     places, pairs, queries, keys, values, rates = tokens
     steps = len(places)
     gain_square = gain * gain
     columns = columns_of(gain, shift)
     square_column = columns[0] * columns[0]
-    blank = jnp.zeros((D_HEAD, INNER), bf16)
-    first_high = weight_one.astype(bf16)
-    first_low = (weight_one - first_high.astype(f32)).astype(bf16)
-    act, slope = gelu_and_slope(
-        mm(
-            jnp.concatenate([pairs[0], pairs[0]], axis=1),
-            jnp.concatenate([blank, first_high, blank, first_low], axis=0),
-        )
-        + bias_one
-    )
+    if pre_one is None:
+        pre_one = first_product(pairs[0], weight_one) + bias_one
+    act, slope = gelu_and_slope(pre_one)
     act_high = act.astype(bf16)
     bias_column = jnp.broadcast_to(bias_two, (MINI, D_HEAD)).T
     made = [] if ready is not None else prepare(0, backward, tokens, gain, shift, columns)
@@ -283,11 +285,12 @@
     delta_ref[...] = jnp.concatenate([ends[0], ends[2], biases], axis=0).astype(bf16)
 
 
-def between_phases(total, dir_ref, qk_ref, v_ref, r_ref, gain_ref, shift_ref, dual_ref, low_ref, act_ref, weighted_ref,
-                   second_ref, bias_ref, tail_ref, plain_ref, mixer_ref, pull_ref, turned_ref, row_ref):
+def between_phases(total, dir_ref, qk_ref, v_ref, r_ref, w1_ref, c1_ref, gain_ref, shift_ref, dual_ref, low_ref, act_ref, weighted_ref,
+                   second_ref, bias_ref, tail_ref, pre_ref, plain_ref, mixer_ref, pull_ref, turned_ref, row_ref):
     gain, shift = gain_ref[...], shift_ref[...]
     backward = 1 - dir_ref[0]
     tokens = tokens_of(0, total, total, backward, qk_ref, v_ref, r_ref)
+    pre_ref[...] = first_product(tokens[1][0], w1_ref[...]) + c1_ref[...]
     columns = columns_of(gain, shift)
     for one in range(0, total, 2):
         for at, made in enumerate(prepare(one, backward, tokens, gain, shift, columns)):
@@ -319,7 +322,7 @@
     start = centre_start(w1_ref, c1_ref, w2t_ref, c2_ref)
     state = tuple(part + delta for part, delta in zip(start, deltas))
     if total <= CHUNK:
-        tail_ref, *ready_refs, out_ref = refs
+        tail_ref, pre_ref, *ready_refs, out_ref = refs
         tokens = tokens_of(0, total, total, backward, qk_ref, None, r_ref)
         done = []
 
@@ -340,10 +343,14 @@
                 folded = jnp.concatenate([summed[at : at + fold], summed[at + fold : at + 2 * fold]], axis=1)
                 out_ref[spot * (MINI // (2 * fold)) + block] = folded
 
+        blank = jnp.zeros((D_HEAD, INNER), bf16)
+        moved = jnp.concatenate([blank, delta_ref[0:D_HEAD, :]], axis=0)
+        pre_one = pre_ref[...] + mm(tokens[1][0], moved) + deltas[1]
+
         def ready(step):
             return tuple(ref[step] for ref in ready_refs)
 
-        run_chunk(backward, tokens, state, gain, shift, emit, ready, ends=True)
+        run_chunk(backward, tokens, state, gain, shift, emit, ready, ends=True, pre_one=pre_one)
     else:
         out_ref, *state_refs = refs
         for ref, part in zip(state_refs, state):
@@ -537,13 +544,14 @@
     if short:
         outs = [
             shape((2 * MINI, D_HEAD), f32),
+            shape((MINI, INNER), f32),
             shape((total, 3 * MINI + 16, 2 * D_HEAD), bf16),
             shape((total, 3 * MINI + 16, D_HEAD), bf16),
             shape((total, MINI, D_HEAD), f32),
             shape((total, MINI, D_HEAD), f32),
             shape((total, 1, MINI), f32),
         ]
-        extra = call_phase(functools.partial(between_phases, total), outs, False, *tokens, *params[4:], *left)
+        extra = call_phase(functools.partial(between_phases, total), outs, False, *tokens, *params[:2], *params[4:], *left)
     (summed,) = call_phase(
         functools.partial(second_phase, total, fold),
         [shape((half_tokens, D_HEAD) if fold is None else (group, fold, 2 * D_HEAD), bf16)],

time: 38.8 us -> 38.7 us (level)
  no operation moved by 1% of the time
where the time goes in v8:
time: 38.7 us; the launch traced here: 38.3 us
  Pallas kernels  10.7 us (28%)
  starting transfers between devices  8.96 us (23%)
  blocking collectives  8.53 us (22%)
  waiting for transfers between devices  7.08 us (18%)
  local copies, waits for them, and re-layouts  2.97 us (8%)
    all_to_all x1, blocking collectives, exchange(): lax.all_to_all(blocks, ('seq', 'head'), 0, 0, axis_index_groups=halves)  8.53 us
    pallas_call x3, Pallas kernels, call_phase(): pl.pallas_call(kernel, out_shape=outs, in_specs=[pl.BlockSpec(memory_spac...  8.29 us
    all_to_all x1, starting transfers between devices, exchange(): lax.all_to_all(blocks, ('seq', 'head'), 0, 0, axis_index_groups=halves)  6.3 us
    all_to_all x1, waiting for transfers between devices, exchange(): lax.all_to_all(blocks, ('seq', 'head'), 0, 0, axis_index_groups=halves)  4.41 us
    ppermute x1, waiting for transfers between devices, local(): delta = lax.ppermute(delta, 'seq', route)  2.67 us
    ppermute x1, starting transfers between devices, local(): delta = lax.ppermute(delta, 'seq', route)  2.66 us
    dynamic_slice x3, local copies, waits for them, and re-layouts, pick(): return lax.dynamic_index_in_dim(array_in, slot, 0, keepdims=False)  2.08 us
    pallas_call x1, Pallas kernels, local(): pl.pallas_call(functools.partial(pack_kernel, head_size, heads_local), ou...  1.7 us
  transfers between devices with their start and end apart: 2, of which 2 were waited for; matrix products, arithmetic and copies ran while one was open for 8% of the time, Pallas kernels for 2%

profile of v8, /device:TPU:0, one launch (start us, length us, event | category | flops | bytes accessed | tf_op | source)
XLA Modules:
  0.0 38.3 jit_solution(62824797162796115)
XLA Ops:
  0.0 0.0 copy-start
  0.0 1.7 %shard_map.109 = bf16[16,56,128]{2,1,0:T(8,128)(2,1)} custom-call(bf16[32,768]{1,0:T(8,128)(2,1)} %query_hbm.1, bf16[32,768]{1,0:T(8,128)(2,1)} %key_hbm.1, bf16[32,768]{1,0:T(8,128)(2,1)} %value_hbm.1, f32[3,128]{1,0:T(4,128)} %bitcast.19), custom_call_target="tpu_custom_call" | custom-call | tf_op jit(solution)/shard_map/pallas_call | solution.py:485
  1.7 6.3 %all-to-all-start = ((bf16[16,56,128]{2,1,0:T(8,128)(2,1)}), bf16[16,56,128]{2,1,0:T(8,128)(2,1)S(1)}, u32[]{:S(2)}, u32[]{:S(2)}) async-start(bf16[16,56,128]{2,1,0:T(8,128)(2,1)} %shard_map.109), calls=%async_computation | async-start | bytes 458752 | tf_op jit(solution)/shard_map/all_to_all | solution.py:480
  8.0 0.7 %constant_dynamic-slice_fusion.3.c1_ref = f32[1,256]{1,0:T(1,128)S(1)} fusion(f32[3,256]{1,0:T(4,128)} %param.17, s32[]{:T(128)S(6)} %select_n.30), kind=kLoop, calls=%fused_computation.8 | loop fusion | bytes 2052 | tf_op jit(solution)/shard_map/jit(dynamic_index_in_dim)/dynamic_slice | solution.py:517
  8.7 0.7 %constant_dynamic-slice_fusion.2.c2_ref = f32[1,64]{1,0:T(1,128)S(1)} fusion(f32[3,64]{1,0:T(4,128)} %param.19, s32[]{:T(128)S(6)} %select_n.30), kind=kLoop, calls=%fused_computation.7 | loop fusion | bytes 516 | tf_op jit(solution)/shard_map/jit(dynamic_index_in_dim)/dynamic_slice | solution.py:517
  9.4 0.7 %constant_dynamic-slice_fusion = (f32[1,64]{1,0:T(1,128)S(1)}, f32[1,64]{1,0:T(1,128)S(1)}) fusion(f32[3,64]{1,0:T(4,128)} %param.21, s32[]{:T(128)S(6)} %select_n.30, f32[3,64]{1,0:T(4,128)} %param.20), kind=kLoop, calls=%fused_computation.5 | loop fusion | bytes 1028 | tf_op jit(solution)/shard_map/jit(dynamic_index_in_dim)/dynamic_slice | solution.py:517
  10.1 0.0 copy-done
  10.1 0.9 %dynamic-slice_bitcast_fusion.w2t_ref = f32[64,256]{1,0:T(8,128)S(1)} fusion(f32[3,256,64]{1,2,0:T(8,128)} %param.18, s32[]{:T(128)S(6)} %select_n.30), kind=kLoop, calls=%fused_computation | loop fusion | bytes 131076 | tf_op jit(solution)/shard_map/transpose | solution.py:522
  11.0 4.4 %all-to-all-done = bf16[16,56,128]{2,1,0:T(8,128)(2,1)S(1)} async-done(((bf16[16,56,128]{2,1,0:T(8,128)(2,1)}), bf16[16,56,128]{2,1,0:T(8,128)(2,1)S(1)}, u32[]{:S(2)}, u32[]{:S(2)}) %all-to-all-start) | async-done | bytes 229408 | tf_op jit(solution)/shard_map/all_to_all | solution.py:480
  15.5 3.6 %shard_map.110 = (f32[512,64]{1,0:T(8,128)S(1)}, bf16[136,256]{1,0:T(8,128)(2,1)S(1)}, bf16[128,256]{1,0:T(8,128)(2,1)S(1)}, bf16[128,256]{1,0:T(8,128)(2,1)S(1)...) custom-call(s32[1]{0:T(128)} %bitcast.dir_ref, ...), custom_call_target="tpu_custom_call" | custom-call | flops 100000000 | bytes 1000000 | tf_op jit(solution)/shard_map/pallas_call | solution.py:426
  19.1 2.7 %collective-permute-start = (bf16[136,256]{1,0:T(8,128)(2,1)S(1)}, bf16[136,256]{1,0:T(8,128)(2,1)S(1)}, u32[]{:S(2)}, u32[]{:S(2)}) collective-permute-start(bf16[136,256]{1,0:T(8,128)(2,1)S(1)} %get-tuple-element.21), channel_id=1, source_target_pairs={{0,4},{1,5},{2,6},{3,7},{4,0},{5,1},{6,2},{7,3},{8,12},{9,13},{10,... | collective-permute-start | bytes 208904 | tf_op jit(solution)/shard_map/ppermute | solution.py:542
  21.7 0.7 %shard_map.111 = (f32[128,64]{1,0:T(8,128)S(1)}, f32[64,256]{1,0:T(8,128)S(1)}, bf16[8,208,128]{2,1,0:T(8,128)(2,1)S(1)}, bf16[8,208,64]{2,1,0:T(8,128)(2,1)S(1)...) custom-call(s32[1]{0:T(128)} %bitcast.dir_ref, bf16[512,128]{1,0:T(8,128)(2,1)S(1)} %bitcast.16, ...), custom_call_target="tpu_custom_call" | custom-call | flops 100000000 | bytes 1000000 | tf_op jit(solution)/shard_map/pallas_call | solution.py:426
  22.4 2.7 %collective-permute-done.delta_ref = bf16[136,256]{1,0:T(8,128)(2,1)S(1)} collective-permute-done((bf16[136,256]{1,0:T(8,128)(2,1)S(1)}, bf16[136,256]{1,0:T(8,128)(2,1)S(1)}, u32[]{:S(2)}, u32[]{:S(2)}) %collective-permute-start) | collective-permute-done | bytes 69664 | tf_op jit(solution)/shard_map/ppermute | solution.py:542
  25.1 4.0 %shard_map.112 = bf16[16,16,128]{2,1,0:T(8,128)(2,1)S(1)} custom-call(s32[1]{0:T(128)} %bitcast.dir_ref, bf16[512,128]{1,0:T(8,128)(2,1)S(1)} %bitcast.17, bf16[16,16,128]{2,1,0:T(8,128)(2,1)S(1)} %slice.25.v_ref, f32[4,1,128]{2,1,0:T(1,128)S(1)} %slice_add_fusion.r_ref, f32[64,256]{1,0:T(8,128)S(1)} %dynamic-slice_bitcast_fusion.1.w1_ref, ...), custom_call_target="tpu_custom_call" | custom-call | flops 100000000 | bytes 1000000 | tf_op jit(solution)/shard_map/pallas_call | solution.py:426
  29.1 0.0 copy-start.1
  29.1 8.5 %all_to_all.10.back_ref = bf16[16,16,128]{2,1,0:T(8,128)(2,1)S(1)} all-to-all(bf16[16,16,128]{2,1,0:T(8,128)(2,1)S(1)} %shard_map.112), channel_id=1, replica_groups={{0,8,16,24,1,9,17,25,2,10,18,26,3,11,19,27},{4,12,20,28,5,13,21,29,6,14..., dimensions={0} | all-to-all | bytes 131072 | tf_op jit(solution)/shard_map/all_to_all | solution.py:480
  37.6 0.0 copy-done.1
  37.6 0.7 %shard_map.113 = bf16[32,768]{1,0:T(8,128)(2,1)} custom-call(bf16[16,16,128]{2,1,0:T(8,128)(2,1)S(1)} %all_to_all.10.back_ref, bf16[32,768]{1,0:T(8,128)(2,1)S(1)} %copy-done.1), custom_call_target="tpu_custom_call" | custom-call | tf_op jit(solution)/shard_map/pallas_call | solution.py:565
  (6 shorter events, 0.0 us)
Async XLA Ops:
  0.0 10.1 %copy-start = (f32[3,64,256]{2,1,0:T(8,128)S(1)}, f32[3,64,256]{2,1,0:T(8,128)}, u32[]{:S(2)}) copy-start(f32[3,64,256]{2,1,0:T(8,128)} %param.16) | copy-start | bytes 589828
  1.7 13.7 %all-to-all-start = ((bf16[16,56,128]{2,1,0:T(8,128)(2,1)}), bf16[16,56,128]{2,1,0:T(8,128)(2,1)S(1)}, u32[]{:S(2)}, u32[]{:S(2)}) async-start(bf16[16,56,128]{2,1,0:T(8,128)(2,1)} %shard_map.109), calls=%async_computation | async-start | bytes 458752 | tf_op jit(solution)/shard_map/all_to_all | solution.py:480
  19.1 6.0 %collective-permute-start = (bf16[136,256]{1,0:T(8,128)(2,1)S(1)}, bf16[136,256]{1,0:T(8,128)(2,1)S(1)}, u32[]{:S(2)}, u32[]{:S(2)}) collective-permute-start(bf16[136,256]{1,0:T(8,128)(2,1)S(1)} %get-tuple-element.21), channel_id=1, source_target_pairs={{0,4},{1,5},{2,6},{3,7},{4,0},{5,1},{6,2},{7,3},{8,12},{9,13},{10,... | collective-permute-start | bytes 208904 | tf_op jit(solution)/shard_map/ppermute | solution.py:542
  29.1 8.5 %copy-start.1 = (bf16[32,768]{1,0:T(8,128)(2,1)S(1)}, bf16[32,768]{1,0:T(8,128)(2,1)}, u32[]{:S(2)}) copy-start(bf16[32,768]{1,0:T(8,128)(2,1)} %gate_ref.1) | copy-start | bytes 147460

commit v9 on v7

--- a/solution.py
+++ b/solution.py
@@ -180,6 +180,8 @@
         back_scaled = jnp.concatenate([back[MINI + at : MINI + at + 16] for at in range(16, 2 * MINI, 32)], axis=0)
         first_high = weight_one.astype(bf16)
         first_low = (weight_one - first_high.astype(f32)).astype(bf16)
+        if ready is None and step % 2 == 0 and step + 2 < steps:
+            made = made + prepare(step + 2, backward, tokens, gain, shift, columns)
         inverse = lax.rsqrt(row_mean(centred * centred) + eps_norm)
         mean_an = inverse * (inverse * row_mean(scaled * centred) + row_mean(pull * centred))
         front = inverse * slope
@@ -210,11 +212,9 @@
         weighted = weighted_turned.T
         bias_column = bias_column - jnp.sum(weighted_turned, axis=1, keepdims=True)
         bias_two = bias_two - jnp.sum(weighted, axis=0, keepdims=True)
-        if len(waiting) == 2:
+        if len(waiting) == (2 if ready is None else 3):
             finish(waiting, second_before, bias_before, backward, gain, shift, emit)
             waiting = []
-        if ready is None and step % 2 == 0 and step + 2 < steps:
-            made = made + prepare(step + 2, backward, tokens, gain, shift, columns)
         dual = gelu(mixed_query + bias_one)
         dual_high = dual.astype(bf16)
         dual_low = (dual - dual_high.astype(f32)).astype(bf16)

time: 38.8 us -> 38.6 us (level)
  no operation moved by 1% of the time
where the time goes in v9:
time: 38.6 us; the launch traced here: 38.2 us
  Pallas kernels  10.6 us (27%)
  starting transfers between devices  8.96 us (23%)
  blocking collectives  8.53 us (22%)
  waiting for transfers between devices  7.05 us (18%)
  local copies, waits for them, and re-layouts  2.97 us (8%)
    all_to_all x1, blocking collectives, exchange(): lax.all_to_all(blocks, ('seq', 'head'), 0, 0, axis_index_groups=halves)  8.53 us
    pallas_call x3, Pallas kernels, call_phase(): pl.pallas_call(kernel, out_shape=outs, in_specs=[pl.BlockSpec(memory_spac...  8.22 us
    all_to_all x1, starting transfers between devices, exchange(): lax.all_to_all(blocks, ('seq', 'head'), 0, 0, axis_index_groups=halves)  6.3 us
    all_to_all x1, waiting for transfers between devices, exchange(): lax.all_to_all(blocks, ('seq', 'head'), 0, 0, axis_index_groups=halves)  4.41 us
    ppermute x1, starting transfers between devices, local(): delta = lax.ppermute(delta, 'seq', route)  2.66 us
    ppermute x1, waiting for transfers between devices, local(): delta = lax.ppermute(delta, 'seq', route)  2.64 us
    dynamic_slice x3, local copies, waits for them, and re-layouts, pick(): return lax.dynamic_index_in_dim(array_in, slot, 0, keepdims=False)  2.08 us
    pallas_call x1, Pallas kernels, local(): pl.pallas_call(functools.partial(pack_kernel, head_size, heads_local), ou...  1.7 us
  transfers between devices with their start and end apart: 2, of which 2 were waited for; matrix products, arithmetic and copies ran while one was open for 8% of the time, Pallas kernels for 2%

profile of v9, /device:TPU:0, one launch (start us, length us, event | category | flops | bytes accessed | tf_op | source)
XLA Modules:
  0.0 38.2 jit_solution(16292992721498364921)
XLA Ops:
  0.0 0.0 copy-start
  0.0 1.7 %shard_map.109 = bf16[16,56,128]{2,1,0:T(8,128)(2,1)} custom-call(bf16[32,768]{1,0:T(8,128)(2,1)} %query_hbm.1, bf16[32,768]{1,0:T(8,128)(2,1)} %key_hbm.1, bf16[32,768]{1,0:T(8,128)(2,1)} %value_hbm.1, f32[3,128]{1,0:T(4,128)} %bitcast.19), custom_call_target="tpu_custom_call" | custom-call | tf_op jit(solution)/shard_map/pallas_call | solution.py:478
  1.7 6.3 %all-to-all-start = ((bf16[16,56,128]{2,1,0:T(8,128)(2,1)}), bf16[16,56,128]{2,1,0:T(8,128)(2,1)S(1)}, u32[]{:S(2)}, u32[]{:S(2)}) async-start(bf16[16,56,128]{2,1,0:T(8,128)(2,1)} %shard_map.109), calls=%async_computation | async-start | bytes 458752 | tf_op jit(solution)/shard_map/all_to_all | solution.py:473
  8.0 0.7 %constant_dynamic-slice_fusion.3.c1_ref = f32[1,256]{1,0:T(1,128)S(1)} fusion(f32[3,256]{1,0:T(4,128)} %param.17, s32[]{:T(128)S(6)} %select_n.30), kind=kLoop, calls=%fused_computation.8 | loop fusion | bytes 2052 | tf_op jit(solution)/shard_map/jit(dynamic_index_in_dim)/dynamic_slice | solution.py:510
  8.7 0.7 %constant_dynamic-slice_fusion.2.c2_ref = f32[1,64]{1,0:T(1,128)S(1)} fusion(f32[3,64]{1,0:T(4,128)} %param.19, s32[]{:T(128)S(6)} %select_n.30), kind=kLoop, calls=%fused_computation.7 | loop fusion | bytes 516 | tf_op jit(solution)/shard_map/jit(dynamic_index_in_dim)/dynamic_slice | solution.py:510
  9.4 0.7 %constant_dynamic-slice_fusion = (f32[1,64]{1,0:T(1,128)S(1)}, f32[1,64]{1,0:T(1,128)S(1)}) fusion(f32[3,64]{1,0:T(4,128)} %param.21, s32[]{:T(128)S(6)} %select_n.30, f32[3,64]{1,0:T(4,128)} %param.20), kind=kLoop, calls=%fused_computation.5 | loop fusion | bytes 1028 | tf_op jit(solution)/shard_map/jit(dynamic_index_in_dim)/dynamic_slice | solution.py:510
  10.1 0.0 copy-done
  10.1 0.9 %dynamic-slice_bitcast_fusion.w2t_ref = f32[64,256]{1,0:T(8,128)S(1)} fusion(f32[3,256,64]{1,2,0:T(8,128)} %param.18, s32[]{:T(128)S(6)} %select_n.30), kind=kLoop, calls=%fused_computation | loop fusion | bytes 131076 | tf_op jit(solution)/shard_map/transpose | solution.py:515
  11.0 4.4 %all-to-all-done = bf16[16,56,128]{2,1,0:T(8,128)(2,1)S(1)} async-done(((bf16[16,56,128]{2,1,0:T(8,128)(2,1)}), bf16[16,56,128]{2,1,0:T(8,128)(2,1)S(1)}, u32[]{:S(2)}, u32[]{:S(2)}) %all-to-all-start) | async-done | bytes 229408 | tf_op jit(solution)/shard_map/all_to_all | solution.py:473
  15.5 3.6 %shard_map.110 = (f32[512,64]{1,0:T(8,128)S(1)}, bf16[136,256]{1,0:T(8,128)(2,1)S(1)}, bf16[128,256]{1,0:T(8,128)(2,1)S(1)}, bf16[128,256]{1,0:T(8,128)(2,1)S(1)...) custom-call(s32[1]{0:T(128)} %bitcast.dir_ref, ...), custom_call_target="tpu_custom_call" | custom-call | flops 100000000 | bytes 1000000 | tf_op jit(solution)/shard_map/pallas_call | solution.py:419
  19.1 2.7 %collective-permute-start = (bf16[136,256]{1,0:T(8,128)(2,1)S(1)}, bf16[136,256]{1,0:T(8,128)(2,1)S(1)}, u32[]{:S(2)}, u32[]{:S(2)}) collective-permute-start(bf16[136,256]{1,0:T(8,128)(2,1)S(1)} %get-tuple-element.20), channel_id=1, source_target_pairs={{0,4},{1,5},{2,6},{3,7},{4,0},{5,1},{6,2},{7,3},{8,12},{9,13},{10,... | collective-permute-start | bytes 208904 | tf_op jit(solution)/shard_map/ppermute | solution.py:535
  21.7 0.7 %shard_map.111 = (f32[128,64]{1,0:T(8,128)S(1)}, bf16[8,208,128]{2,1,0:T(8,128)(2,1)S(1)}, bf16[8,208,64]{2,1,0:T(8,128)(2,1)S(1)}, f32[8,64,64]{2,1,0:T(8,128)S...) custom-call(s32[1]{0:T(128)} %bitcast.dir_ref, bf16[512,128]{1,0:T(8,128)(2,1)S(1)} %bitcast.16, ...), custom_call_target="tpu_custom_call" | custom-call | flops 100000000 | bytes 1000000 | tf_op jit(solution)/shard_map/pallas_call | solution.py:419
  22.5 2.6 %collective-permute-done.delta_ref = bf16[136,256]{1,0:T(8,128)(2,1)S(1)} collective-permute-done((bf16[136,256]{1,0:T(8,128)(2,1)S(1)}, bf16[136,256]{1,0:T(8,128)(2,1)S(1)}, u32[]{:S(2)}, u32[]{:S(2)}) %collective-permute-start) | collective-permute-done | bytes 69664 | tf_op jit(solution)/shard_map/ppermute | solution.py:535
  25.1 3.9 %shard_map.112 = bf16[16,16,128]{2,1,0:T(8,128)(2,1)S(1)} custom-call(s32[1]{0:T(128)} %bitcast.dir_ref, bf16[512,128]{1,0:T(8,128)(2,1)S(1)} %bitcast.17, bf16[16,16,128]{2,1,0:T(8,128)(2,1)S(1)} %slice.25.v_ref, f32[4,1,128]{2,1,0:T(1,128)S(1)} %slice_add_fusion.r_ref, f32[64,256]{1,0:T(8,128)S(1)} %dynamic-slice_bitcast_fusion.1.w1_ref, ...), custom_call_target="tpu_custom_call" | custom-call | flops 100000000 | bytes 1000000 | tf_op jit(solution)/shard_map/pallas_call | solution.py:419
  29.0 0.0 copy-start.1
  29.0 8.5 %all_to_all.10.back_ref = bf16[16,16,128]{2,1,0:T(8,128)(2,1)S(1)} all-to-all(bf16[16,16,128]{2,1,0:T(8,128)(2,1)S(1)} %shard_map.112), channel_id=1, replica_groups={{0,8,16,24,1,9,17,25,2,10,18,26,3,11,19,27},{4,12,20,28,5,13,21,29,6,14..., dimensions={0} | all-to-all | bytes 131072 | tf_op jit(solution)/shard_map/all_to_all | solution.py:473
  37.5 0.0 copy-done.1
  37.5 0.7 %shard_map.113 = bf16[32,768]{1,0:T(8,128)(2,1)} custom-call(bf16[16,16,128]{2,1,0:T(8,128)(2,1)S(1)} %all_to_all.10.back_ref, bf16[32,768]{1,0:T(8,128)(2,1)S(1)} %copy-done.1), custom_call_target="tpu_custom_call" | custom-call | tf_op jit(solution)/shard_map/pallas_call | solution.py:557
  (6 shorter events, 0.0 us)
Async XLA Ops:
  0.0 10.1 %copy-start = (f32[3,64,256]{2,1,0:T(8,128)S(1)}, f32[3,64,256]{2,1,0:T(8,128)}, u32[]{:S(2)}) copy-start(f32[3,64,256]{2,1,0:T(8,128)} %param.16) | copy-start | bytes 589828
  1.7 13.7 %all-to-all-start = ((bf16[16,56,128]{2,1,0:T(8,128)(2,1)}), bf16[16,56,128]{2,1,0:T(8,128)(2,1)S(1)}, u32[]{:S(2)}, u32[]{:S(2)}) async-start(bf16[16,56,128]{2,1,0:T(8,128)(2,1)} %shard_map.109), calls=%async_computation | async-start | bytes 458752 | tf_op jit(solution)/shard_map/all_to_all | solution.py:473
  19.1 6.0 %collective-permute-start = (bf16[136,256]{1,0:T(8,128)(2,1)S(1)}, bf16[136,256]{1,0:T(8,128)(2,1)S(1)}, u32[]{:S(2)}, u32[]{:S(2)}) collective-permute-start(bf16[136,256]{1,0:T(8,128)(2,1)S(1)} %get-tuple-element.20), channel_id=1, source_target_pairs={{0,4},{1,5},{2,6},{3,7},{4,0},{5,1},{6,2},{7,3},{8,12},{9,13},{10,... | collective-permute-start | bytes 208904 | tf_op jit(solution)/shard_map/ppermute | solution.py:535
  29.0 8.5 %copy-start.1 = (bf16[32,768]{1,0:T(8,128)(2,1)S(1)}, bf16[32,768]{1,0:T(8,128)(2,1)}, u32[]{:S(2)}) copy-start(bf16[32,768]{1,0:T(8,128)(2,1)} %gate_ref.1) | copy-start | bytes 147460
